TPU v7x, 128 devices: a whole 4x4x4 slice. The times are simulated.
128 devices in a mesh: gx: 4 (over x), gy: 32 (over z, y, core).
Axes of the slice: x: 4, y: 4, z: 4, core: 2. Of those that a mesh axis runs over, the one named last changes fastest.
Arguments:
- fine_pop: float32 [512, 19, 4096], P(('gx', 'gy')), may hold values from 0 to 1, as said below
- coarse_pop: float32 [256, 19, 4096], P(('gx', 'gy')), may hold values from 0 to 1, as said below
- fine_nbr: int32 [512, 4], P(('gx', 'gy')), may hold values from -1 to 511, as said below
- coarse_nbr: int32 [256, 6], P(('gx', 'gy')), may hold values from -1 to 255, as said below
- parent: int32 [512, 2], P(('gx', 'gy')), may hold values from 0 to 255, as said below
- children: int32 [256, 4], P(('gx', 'gy')), may hold values from -1 to 511, as said below
- solid: int32 [512, 4096], P(('gx', 'gy')), may hold values from 0 to 1, as said below
Outputs:
- fine_out: float32 [512, 19, 4096], P(('gx', 'gy'))
- coarse_out: float32 [256, 19, 4096], P(('gx', 'gy'))
Inputs may be any that keep to these rules, and one draw needn't show every extreme that they name: `fine_pop`: positive populations. `coarse_pop`: positive populations. `fine_nbr`: -1 where the neighbouring position holds no fine block. A neighbour is held by the same device as the block or by the device just before or after it along gx+gy. The fine blocks form one layer along z. `coarse_nbr`: -1 where the neighbouring position holds no coarse block. A neighbour is held by the same device as the block or by the device just before or after it along gx+gy. Column 0 is the parent's coarse block, column 1 the quadrant 2 qy + qx; every child lies in the lower half of its parent along z. A fine block and its parent are held by devices of the same aligned group of four consecutive devices along gx+gy. children[c,q] = f exactly when parent[f] = (c, q), else -1. `solid`: the outermost layer of cells of every block is 0.
All inputs are finite; a program needn't handle non-finite values.
Results may differ from a plain program's by a relative error of at most 0.0001.
Values sent between devices are 32-bit elements; how exact they have to be, the bound alone decides.
No kernel may reach another device: no remote copies, remote signals or barrier semaphores. Data moves between devices by JAX's collectives and lax.ppermute only.
A program may use at most 128 MiB of HBM per device.

v0:
```python
import jax
import jax.numpy as jnp
import numpy as np
from jax import lax
from jax.sharding import PartitionSpec as P

S = 16


VELOCITIES = (
    (0, 0, 0),
    (1, 0, 0),
    (-1, 0, 0),
    (0, 1, 0),
    (0, -1, 0),
    (0, 0, 1),
    (0, 0, -1),
    (1, 1, 0),
    (-1, -1, 0),
    (1, -1, 0),
    (-1, 1, 0),
    (1, 0, 1),
    (-1, 0, -1),
    (1, 0, -1),
    (-1, 0, 1),
    (0, 1, 1),
    (0, -1, -1),
    (0, 1, -1),
    (0, -1, 1),
)
WEIGHTS = (1.0 / 3.0,) + (1.0 / 18.0,) * 6 + (1.0 / 36.0,) * 12
OPPOSITE = (0, 2, 1, 4, 3, 6, 5, 8, 7, 10, 9, 12, 11, 14, 13, 16, 15, 18, 17)
OMEGA_COARSE = 1.6
OMEGA_FINE = 1.0 / (2.0 * (1.0 / 1.6 - 0.5) + 0.5)
OFFSETS = (-3, -2, -1, 1, 2, 3)


def extended(cells, sides, width):
    for axis, dim in sides:
        count = lax.axis_size(axis)
        ends = count - 1
        head = lax.slice_in_dim(cells, 0, width, axis=dim)
        tail = lax.slice_in_dim(cells, cells.shape[dim] - width, cells.shape[dim], axis=dim)
        cells = jnp.concatenate(
            [
                lax.ppermute(tail, axis, [(i, (i + 1) % count) for i in range(ends)]),
                cells,
                lax.ppermute(head, axis, [((i + 1) % count, i) for i in range(ends)]),
            ],
            axis=dim,
        )
    return cells


def passed_along(block, axis, distance):
    devices = range(lax.axis_size(axis))
    route = [(i - distance, i) for i in devices if i - distance in devices]
    return lax.ppermute(block, axis, route)


def collide(populations, relax_rate):
    kind = populations.dtype
    comp_x = jnp.array([v[0] for v in VELOCITIES], kind)[None, :, None]
    comp_y = jnp.array([v[1] for v in VELOCITIES], kind)[None, :, None]
    comp_z = jnp.array([v[2] for v in VELOCITIES], kind)[None, :, None]
    weight = jnp.array(WEIGHTS, kind)[None, :, None]
    density = jnp.sum(populations, axis=1, keepdims=True)
    vel_x = jnp.sum(populations * comp_x, axis=1, keepdims=True) / density
    vel_y = jnp.sum(populations * comp_y, axis=1, keepdims=True) / density
    vel_z = jnp.sum(populations * comp_z, axis=1, keepdims=True) / density
    square = vel_x * vel_x + vel_y * vel_y + vel_z * vel_z
    projection = comp_x * vel_x + comp_y * vel_y + comp_z * vel_z
    equilibrium = (
        weight * density * (1.0 + 3.0 * projection + 4.5 * projection * projection - 1.5 * square)
    )
    return populations - relax_rate * (populations - equilibrium)


def locate(z_pos, y_pos, x_pos, edge):
    z_pos = np.asarray(z_pos)
    y_pos = np.asarray(y_pos)
    x_pos = np.asarray(x_pos)
    wide = edge + 2
    base_x = edge**3
    base_y = base_x + 2 * edge * edge
    base_z = base_y + 2 * edge * wide
    z_out = (z_pos < 0) | (z_pos >= edge)
    y_out = (y_pos < 0) | (y_pos >= edge)
    x_out = (x_pos < 0) | (x_pos >= edge)
    inside = (z_pos * edge + y_pos) * edge + x_pos
    on_x = base_x + (x_pos >= edge) * edge * edge + z_pos * edge + y_pos
    on_y = base_y + (y_pos >= edge) * edge * wide + z_pos * wide + (x_pos + 1)
    on_z = base_z + (z_pos >= edge) * wide * wide + (y_pos + 1) * wide + (x_pos + 1)
    return np.where(z_out, on_z, np.where(y_out, on_y, np.where(x_out, on_x, inside))).astype(
        np.int32
    )


def build_tables(edge):
    half_edge = edge // 2
    wide = edge + 2
    grid = np.arange(edge**3)
    cell_z, cell_y, cell_x = (grid // (edge * edge), grid // edge % edge, grid % edge)
    tables = {}
    tables["stream"] = np.stack(
        [locate(cell_z - v[2], cell_y - v[1], cell_x - v[0], edge) for v in VELOCITIES]
    )
    plane = np.arange(edge * edge)
    plane_a, plane_b = (plane // edge, plane % edge)
    strip = np.arange(edge * wide)
    strip_z, strip_x = (strip // wide, strip % wide - 1)
    square = np.arange(wide * wide)
    square_y, square_x = (square // wide - 1, square % wide - 1)
    for name, layer in (("first", 0), ("last", edge - 1)):
        tables["xface_" + name] = ((plane_a * edge + plane_b) * edge + layer).astype(np.int32)
        tables["yface_" + name] = locate(strip_z, layer, strip_x, edge)
        tables["zface_" + name] = locate(layer, square_y, square_x, edge)
        tables["yclamp_" + name] = (
            (strip_z * edge + layer) * edge + np.clip(strip_x, 0, edge - 1)
        ).astype(np.int32)
        tables["zclamp_" + name] = (
            (layer * edge + np.clip(square_y, 0, edge - 1)) * edge + np.clip(square_x, 0, edge - 1)
        ).astype(np.int32)
    tables["upsample"] = ((cell_z // 2 * half_edge + cell_y // 2) * half_edge + cell_x // 2).astype(
        np.int32
    )
    octant = np.arange(half_edge**3)
    oct_z, oct_y, oct_x = (
        octant // (half_edge * half_edge),
        octant // half_edge % half_edge,
        octant % half_edge,
    )
    tables["octant"] = np.stack(
        [
            (oct_z * edge + q // 2 * half_edge + oct_y) * edge + q % 2 * half_edge + oct_x
            for q in range(4)
        ]
    ).astype(np.int32)
    tables["coarsen"] = np.stack(
        [
            ((2 * oct_z + a) * edge + 2 * oct_y + b) * edge + 2 * oct_x + d
            for a in range(2)
            for b in range(2)
            for d in range(2)
        ]
    ).astype(np.int32)
    quadrant = cell_y // half_edge * 2 + cell_x // half_edge
    inner = (cell_z * half_edge + cell_y % half_edge) * half_edge + cell_x % half_edge
    lower = cell_z < half_edge
    tables["lift"] = np.where(lower, quadrant * half_edge**3 + inner, 0).astype(np.int32)
    tables["quadrant"] = quadrant.astype(np.int32)
    tables["lower"] = lower
    return tables


def face_halo(outgoing, block_count, level_fine):
    if level_fine:
        return extended(outgoing, ((("gx", "gy"), 0),), block_count)
    return extended(outgoing, ((("gx", "gy"), 0),), block_count)


def spread(picked, chosen):
    if len(chosen) == 19:
        return picked
    full_set = jnp.zeros((picked.shape[0], 19) + picked.shape[2:], picked.dtype)
    return full_set.at[:, jnp.array(chosen)].set(picked)


def sides(
    source,
    face_first,
    face_last,
    low_index,
    high_index,
    low_fallback,
    high_fallback,
    component,
    level_fine,
):
    block_count = source.shape[0]
    first_layer = jnp.take(source, jnp.asarray(face_first), axis=2)
    last_layer = jnp.take(source, jnp.asarray(face_last), axis=2)
    if low_fallback is None:
        low_fallback = first_layer
        high_fallback = last_layer
    down_pops = list(range(19))
    upward = list(range(19))
    face_len = first_layer.shape[2]
    outgoing = jnp.stack(
        [
            first_layer[:, jnp.array(down_pops)].reshape((block_count, -1)),
            last_layer[:, jnp.array(upward)].reshape((block_count, -1)),
        ],
        axis=1,
    )
    widened = face_halo(outgoing, block_count, level_fine)
    first_slot = (lax.axis_index(("gx", "gy")) - 1) * block_count
    low_rows = jnp.take(
        widened[:, 1], jnp.clip(low_index - first_slot, 0, 3 * block_count - 1), axis=0
    )
    high_rows = jnp.take(
        widened[:, 0], jnp.clip(high_index - first_slot, 0, 3 * block_count - 1), axis=0
    )
    low_rows = spread(low_rows.reshape((block_count, len(upward), face_len)), upward)
    high_rows = spread(high_rows.reshape((block_count, len(down_pops), face_len)), down_pops)
    low_side = jnp.where((low_index >= 0)[:, None, None], low_rows, low_fallback)
    high_side = jnp.where((high_index >= 0)[:, None, None], high_rows, high_fallback)
    return (low_side, high_side)


def stream(source, tables):
    stream_rows = tables["stream"]
    return jnp.stack(
        [jnp.take(source[:, i], jnp.asarray(stream_rows[i]), axis=1) for i in range(19)], axis=1
    )


def fine_step(populations, explode_flat, fine_nbr, solid_mask, tables):
    collided = jnp.where(solid_mask[:, None, :], populations, collide(populations, OMEGA_FINE))
    x_fallback_low = jnp.take(explode_flat, jnp.asarray(tables["xface_first"]), axis=2)
    x_fallback_high = jnp.take(explode_flat, jnp.asarray(tables["xface_last"]), axis=2)
    x_low, x_high = sides(
        collided,
        tables["xface_first"],
        tables["xface_last"],
        fine_nbr[:, 0],
        fine_nbr[:, 1],
        x_fallback_low,
        x_fallback_high,
        0,
        True,
    )
    source_x = jnp.concatenate([collided, x_low, x_high], axis=2)
    y_fallback_low = jnp.take(explode_flat, jnp.asarray(tables["yclamp_first"]), axis=2)
    y_fallback_high = jnp.take(explode_flat, jnp.asarray(tables["yclamp_last"]), axis=2)
    y_low, y_high = sides(
        source_x,
        tables["yface_first"],
        tables["yface_last"],
        fine_nbr[:, 2],
        fine_nbr[:, 3],
        y_fallback_low,
        y_fallback_high,
        1,
        True,
    )
    z_low = jnp.take(explode_flat, jnp.asarray(tables["zclamp_first"]), axis=2)
    z_high = jnp.take(explode_flat, jnp.asarray(tables["zclamp_last"]), axis=2)
    full_source = jnp.concatenate([source_x, y_low, y_high, z_low, z_high], axis=2)
    passed = stream(full_source, tables)
    extra = full_source.shape[2] - populations.shape[2]
    wall_source = jnp.concatenate(
        [solid_mask, jnp.zeros((solid_mask.shape[0], extra), solid_mask.dtype)], axis=1
    )
    stream_rows = tables["stream"]
    pieces = []
    for i in range(19):
        from_wall = jnp.take(wall_source, jnp.asarray(stream_rows[i]), axis=1)
        pieces.append(jnp.where(from_wall, collided[:, OPPOSITE[i]], passed[:, i]))
    result = jnp.stack(pieces, axis=1)
    return jnp.where(solid_mask[:, None, :], populations, result)


def coarse_step(coarse_pop, coarse_nbr, tables):
    collided = collide(coarse_pop, OMEGA_COARSE)
    x_low, x_high = sides(
        collided,
        tables["xface_first"],
        tables["xface_last"],
        coarse_nbr[:, 0],
        coarse_nbr[:, 1],
        None,
        None,
        0,
        False,
    )
    source_x = jnp.concatenate([collided, x_low, x_high], axis=2)
    y_low, y_high = sides(
        source_x,
        tables["yface_first"],
        tables["yface_last"],
        coarse_nbr[:, 2],
        coarse_nbr[:, 3],
        None,
        None,
        1,
        False,
    )
    source_y = jnp.concatenate([source_x, y_low, y_high], axis=2)
    z_low, z_high = sides(
        source_y,
        tables["zface_first"],
        tables["zface_last"],
        coarse_nbr[:, 4],
        coarse_nbr[:, 5],
        None,
        None,
        2,
        False,
    )
    full_source = jnp.concatenate([source_y, z_low, z_high], axis=2)
    return stream(full_source, tables)


def on_device(fine_pop, coarse_pop, fine_nbr, coarse_nbr, parent, children, solid):
    tables = build_tables(S)
    fine_count = fine_pop.shape[0]
    coarse_count = coarse_pop.shape[0]
    half_edge = S // 2
    position = lax.axis_index(("gx", "gy"))
    octant_rows = tables["octant"]
    octants = jnp.stack(
        [jnp.take(coarse_pop, jnp.asarray(octant_rows[q]), axis=2) for q in range(4)], axis=1
    )
    octants = octants.reshape((coarse_count * 4, -1))
    child_list = children.reshape(-1)
    slot_ids = jnp.arange(fine_count, dtype=jnp.int32)
    quad_ids = jnp.arange(coarse_count * 4, dtype=jnp.int32)
    arrived = jnp.zeros((fine_count, octants.shape[1]), octants.dtype)
    for shift_by in (0,) + OFFSETS:
        pack_local_rows = child_list - (position + shift_by) * fine_count
        matches = (child_list >= 0)[None, :] & (pack_local_rows[None, :] == slot_ids[:, None])
        source = jnp.sum(jnp.where(matches, quad_ids[None, :], 0), axis=1)
        packed = jnp.where(
            jnp.any(matches, axis=1)[:, None], jnp.take(octants, source, axis=0), 0.0
        )
        if shift_by != 0:
            packed = passed_along(packed, ("gx", "gy"), shift_by)
        arrived = arrived + packed
    explode_flat = jnp.take(
        arrived.reshape((fine_count, 19, half_edge**3)), jnp.asarray(tables["upsample"]), axis=2
    )
    solid_mask = solid > 0
    populations = fine_pop
    for substep in range(2):
        populations = fine_step(populations, explode_flat, fine_nbr, solid_mask, tables)
    passed = coarse_step(coarse_pop, coarse_nbr, tables)
    coarsen_rows = tables["coarsen"]
    child_means = jnp.take(populations, jnp.asarray(coarsen_rows[0]), axis=2)
    for corner in range(1, 8):
        child_means = child_means + jnp.take(populations, jnp.asarray(coarsen_rows[corner]), axis=2)
    child_means = (child_means * 0.125).reshape((fine_count, -1))
    gathered = jnp.zeros((coarse_count * 4, child_means.shape[1]), child_means.dtype)
    for shift_by in (0,) + OFFSETS:
        if shift_by == 0:
            incoming = child_means
        else:
            incoming = passed_along(child_means, ("gx", "gy"), shift_by)
        local_rows = child_list - (position - shift_by) * fine_count
        present = (child_list >= 0) & (local_rows >= 0) & (local_rows < fine_count)
        picked = jnp.take(incoming, jnp.clip(local_rows, 0, fine_count - 1), axis=0)
        gathered = gathered + jnp.where(present[:, None], picked, 0.0)
    gathered = gathered.reshape((coarse_count, 4, 19, half_edge**3))
    gathered = jnp.transpose(gathered, (0, 2, 1, 3)).reshape((coarse_count, 19, 4 * half_edge**3))
    lifted = jnp.take(gathered, jnp.asarray(tables["lift"]), axis=2)
    child_ok = children >= 0
    cell_mask = (
        jnp.take(child_ok, jnp.asarray(tables["quadrant"]), axis=1)
        & jnp.asarray(tables["lower"])[None, :]
    )
    coarse_new = jnp.where(cell_mask[:, None, :], lifted, passed)
    return (populations, coarse_new)


def solution(mesh):
    return jax.shard_map(
        on_device,
        mesh=mesh,
        in_specs=(
            P(("gx", "gy"), None, None),
            P(("gx", "gy"), None, None),
            P(("gx", "gy"), None),
            P(("gx", "gy"), None),
            P(("gx", "gy"), None),
            P(("gx", "gy"), None),
            P(("gx", "gy"), None),
        ),
        out_specs=(P(("gx", "gy"), None, None), P(("gx", "gy"), None, None)),
        check_vma=False,
    )
```

profile of v0, /device:TPU:1, one launch (start us, length us, event | category | flops | bytes accessed | tf_op | source)
XLA Modules:
  0.0 2216.9 jit_solution(10207218747153589513)
XLA Ops:
  570.2 31.5 %gather_fusion.2 = f32[4096,4,19]{2,1,0:T(4,128)} fusion(f32[4,19,512]{1,0,2:T(4,128)} %copy.1485, s32[4096]{0:T(1024)} %get-tuple-element.212), kind=kCustom, calls=%fused_computation.138 | custom fusion | bytes 2506752 | tf_op jit(solution)/shard_map/jit(_take)/gather | solution.py:330
  753.5 16.1 gather_fusion.134
  780.8 16.1 gather_fusion.135
  802.6 16.1 gather_fusion.136
  824.4 16.1 gather_fusion.137
  846.2 16.1 gather_fusion.138
  867.9 16.1 gather_fusion.139
  889.7 16.1 gather_fusion.140
  911.5 16.1 gather_fusion.141
  932.6 16.1 gather_fusion.142
  953.0 16.1 gather_fusion.143
  973.5 16.1 gather_fusion.144
  994.5 16.1 gather_fusion.145
  1015.5 16.1 gather_fusion.146
  1036.6 16.1 gather_fusion.147
  1057.7 16.2 gather_fusion.148
  1083.0 16.1 gather_fusion.149
  1120.2 16.1 gather_fusion.43
  1142.1 16.1 gather_fusion.45
  1163.9 16.1 gather_fusion.47
  1185.8 16.1 gather_fusion.49
  1207.6 16.1 gather_fusion.51
  1229.5 16.1 gather_fusion.53
  1251.4 16.1 gather_fusion.55
  1273.2 16.1 gather_fusion.57
  1295.1 16.1 gather_fusion.59
  1316.9 16.1 gather_fusion.61
  1382.5 16.4 gather_fusion.67
  1509.5 16.2 gather_fusion.79
  1640.4 16.1 gather_fusion.88
  2016.3 16.2 gather_fusion.106
  2167.6 28.3 %gather_fusion.10 = f32[4096,2,19]{2,1,0:T(2,128)} fusion(f32[2,19,2048]{1,0,2:T(2,128)S(1)} %bitcast.927, s32[4096]{0:T(1024)S(1)} %copy-done.187), kind=kCustom, calls=%fused_computation.146 | custom fusion | bytes 1261568 | tf_op jit(solution)/shard_map/jit(_take)/gather | solution.py:355
  (1201 shorter events, 1669.8 us)
Async XLA Ops:
  0.7 112.4 %copy-start.197 = (pred[256]{0:T(512)(128)(4,1)}, pred[256]{0:T(512)(128)(4,1)S(1)}, u32[]{:S(2)}) copy-start(pred[256]{0:T(512)(128)(4,1)S(1)} %compare_and_fusion.24) | copy-start | bytes 772
  13.4 105.0 %copy-start.190 = (s32[1024]{0:T(1024)}, s32[1024]{0:T(1024)S(1)}, u32[]{:S(2)}) copy-start(s32[1024]{0:T(1024)S(1)} %get-tuple-element.274) | copy-start | bytes 12292
  18.7 492.3 %collective-permute-start.20 = (f32[2,2,4864]{2,0,1:T(2,128)}, f32[2,2,4864]{2,0,1:T(2,128)}, u32[]{:S(2)}, u32[]{:S(2)}) collective-permute-start(f32[2,2,4864]{2,0,1:T(2,128)} %pad_maximum_fusion.13), channel_id=1, source_target_pairs={{0,1},{1,2},{2,3},{3,4},{4,5},{5,6},{6,7},{7,8},{8,9},{9,10},{10,1... | collective-permute-start | bytes 233480 | tf_op jit(solution)/shard_map/ppermute | solution.py:46
  23.2 492.0 %collective-permute-start.21 = (f32[2,2,4864]{2,0,1:T(2,128)}, f32[2,2,4864]{2,0,1:T(2,128)}, u32[]{:S(2)}, u32[]{:S(2)}) collective-permute-start(f32[2,2,4864]{2,0,1:T(2,128)} %pad_maximum_fusion.13), channel_id=1, source_target_pairs={{1,0},{2,1},{3,2},{4,3},{5,4},{6,5},{7,6},{8,7},{9,8},{10,9},{11,1... | collective-permute-start | bytes 233480 | tf_op jit(solution)/shard_map/ppermute | solution.py:48
  56.9 495.1 %collective-permute-start.3 = (f32[4,9728]{1,0:T(4,128)}, f32[4,9728]{1,0:T(4,128)}, u32[]{:S(2)}, u32[]{:S(2)}) collective-permute-start(f32[4,9728]{1,0:T(4,128)} %select_select_fusion.11), channel_id=1, source_target_pairs={{2,0},{3,1},{4,2},{5,3},{6,4},{7,5},{8,6},{9,7},{10,8},{11,9},{12,... | collective-permute-start | bytes 466952 | tf_op jit(solution)/shard_map/ppermute | solution.py:58
  59.6 494.3 %collective-permute-start.4 = (f32[4,9728]{1,0:T(4,128)}, f32[4,9728]{1,0:T(4,128)}, u32[]{:S(2)}, u32[]{:S(2)}) collective-permute-start(f32[4,9728]{1,0:T(4,128)} %select_select_fusion.10), channel_id=1, source_target_pairs={{1,0},{2,1},{3,2},{4,3},{5,4},{6,5},{7,6},{8,7},{9,8},{10,9},{11,1... | collective-permute-start | bytes 466952 | tf_op jit(solution)/shard_map/ppermute | solution.py:58
  63.6 494.5 %collective-permute-start.5 = (f32[4,9728]{1,0:T(4,128)}, f32[4,9728]{1,0:T(4,128)}, u32[]{:S(2)}, u32[]{:S(2)}) collective-permute-start(f32[4,9728]{1,0:T(4,128)} %select_select_fusion.9), channel_id=1, source_target_pairs={{0,1},{1,2},{2,3},{3,4},{4,5},{5,6},{6,7},{7,8},{8,9},{9,10},{10,1... | collective-permute-start | bytes 466952 | tf_op jit(solution)/shard_map/ppermute | solution.py:58
  119.0 362.4 %copy-start.12 = (f32[19,4,256]{2,1,0:T(4,128)}, f32[19,4,256]{2,1,0:T(4,128)S(1)}, u32[]{:S(2)}) copy-start(f32[19,4,256]{2,1,0:T(4,128)S(1)} %gather_fusion.1) | copy-start | bytes 233476
  176.5 107.5 %copy-start.80 = (s32[4096]{0:T(1024)}, s32[4096]{0:T(1024)S(1)}, u32[]{:S(2)}) copy-start(s32[4096]{0:T(1024)S(1)} %get-tuple-element.227) | copy-start | bytes 49156
  284.0 107.8 %copy-start.84 = (s32[4096]{0:T(1024)}, s32[4096]{0:T(1024)S(1)}, u32[]{:S(2)}) copy-start(s32[4096]{0:T(1024)S(1)} %get-tuple-element.222) | copy-start | bytes 49156
  389.5 111.8 %copy-start.260 = (pred[4096]{0:T(1024)(128)(4,1)S(1)}, pred[4096]{0:T(1024)(128)(4,1)}, u32[]{:S(2)}) copy-start(pred[4096]{0:T(1024)(128)(4,1)} %constant.449.clone) | copy-start | bytes 12292
  511.0 49.1 %collective-permute-start.6 = (f32[4,9728]{1,0:T(4,128)}, f32[4,9728]{1,0:T(4,128)}, u32[]{:S(2)}, u32[]{:S(2)}) collective-permute-start(f32[4,9728]{1,0:T(4,128)} %select_select_fusion.8), channel_id=1, source_target_pairs={{0,2},{1,3},{2,4},{3,5},{4,6},{5,7},{6,8},{7,9},{8,10},{9,11},{10,... | collective-permute-start | bytes 466952 | tf_op jit(solution)/shard_map/ppermute | solution.py:58
  515.3 48.5 %collective-permute-start.7 = (f32[4,9728]{1,0:T(4,128)}, f32[4,9728]{1,0:T(4,128)}, u32[]{:S(2)}, u32[]{:S(2)}) collective-permute-start(f32[4,9728]{1,0:T(4,128)} %select_select_fusion.7), channel_id=1, source_target_pairs={{0,3},{1,4},{2,5},{3,6},{4,7},{5,8},{6,9},{7,10},{8,11},{9,12},{10... | collective-permute-start | bytes 466952 | tf_op jit(solution)/shard_map/ppermute | solution.py:58
  552.0 13.7 collective-permute-start.2
  553.9 60.2 %collective-permute-start = (f32[4,2,4864]{2,0,1:T(4,128)}, f32[4,2,4864]{2,0,1:T(4,128)}, u32[]{:S(2)}, u32[]{:S(2)}) collective-permute-start(f32[4,2,4864]{2,0,1:T(4,128)} %pad_maximum_fusion.11), channel_id=1, source_target_pairs={{0,1},{1,2},{2,3},{3,4},{4,5},{5,6},{6,7},{7,8},{8,9},{9,10},{10,1... | collective-permute-start | bytes 466952 | tf_op jit(solution)/shard_map/ppermute | solution.py:46
  558.1 56.0 %collective-permute-start.1 = (f32[4,2,4864]{2,0,1:T(4,128)}, f32[4,2,4864]{2,0,1:T(4,128)}, u32[]{:S(2)}, u32[]{:S(2)}) collective-permute-start(f32[4,2,4864]{2,0,1:T(4,128)} %pad_maximum_fusion.11), channel_id=1, source_target_pairs={{1,0},{2,1},{3,2},{4,3},{5,4},{6,5},{7,6},{8,7},{9,8},{10,9},{11,1... | collective-permute-start | bytes 466952 | tf_op jit(solution)/shard_map/ppermute | solution.py:48
  560.1 94.1 %collective-permute-start.22 = (f32[2,2,5472]{2,0,1:T(2,128)}, f32[2,2,5472]{2,0,1:T(2,128)}, u32[]{:S(2)}, u32[]{:S(2)}) collective-permute-start(f32[2,2,5472]{2,0,1:T(2,128)} %constant_dynamic-update-slice_fusion.42), channel_id=1, source_target_pairs={{0,1},{1,2},{2,3},{3,4},{4,5},{5,6},{6,7},{7,8},{8,9},{9,10},{10,1... | collective-permute-start | bytes 262664 | tf_op jit(solution)/shard_map/ppermute | solution.py:46
  563.7 90.5 %collective-permute-start.23 = (f32[2,2,5472]{2,0,1:T(2,128)}, f32[2,2,5472]{2,0,1:T(2,128)}, u32[]{:S(2)}, u32[]{:S(2)}) collective-permute-start(f32[2,2,5472]{2,0,1:T(2,128)} %constant_dynamic-update-slice_fusion.42), channel_id=1, source_target_pairs={{1,0},{2,1},{3,2},{4,3},{5,4},{6,5},{7,6},{8,7},{9,8},{10,9},{11,1... | collective-permute-start | bytes 262664 | tf_op jit(solution)/shard_map/ppermute | solution.py:48
  688.6 42.2 %collective-permute-start.24 = (f32[2,2,6156]{2,0,1:T(2,128)}, f32[2,2,6156]{2,0,1:T(2,128)}, u32[]{:S(2)}, u32[]{:S(2)}) collective-permute-start(f32[2,2,6156]{2,0,1:T(2,128)} %constant_dynamic-update-slice_fusion.44), channel_id=1, source_target_pairs={{0,1},{1,2},{2,3},{3,4},{4,5},{5,6},{6,7},{7,8},{8,9},{9,10},{10,1... | collective-permute-start | bytes 295496 | tf_op jit(solution)/shard_map/ppermute | solution.py:46
  692.2 38.6 %collective-permute-start.25 = (f32[2,2,6156]{2,0,1:T(2,128)}, f32[2,2,6156]{2,0,1:T(2,128)}, u32[]{:S(2)}, u32[]{:S(2)}) collective-permute-start(f32[2,2,6156]{2,0,1:T(2,128)} %constant_dynamic-update-slice_fusion.44), channel_id=1, source_target_pairs={{1,0},{2,1},{3,2},{4,3},{5,4},{6,5},{7,6},{8,7},{9,8},{10,9},{11,1... | collective-permute-start | bytes 295496 | tf_op jit(solution)/shard_map/ppermute | solution.py:48
  695.7 406.2 %collective-permute-start.8 = (f32[4,2,5472]{2,0,1:T(4,128)}, f32[4,2,5472]{2,0,1:T(4,128)}, u32[]{:S(2)}, u32[]{:S(2)}) collective-permute-start(f32[4,2,5472]{2,0,1:T(4,128)} %constant_dynamic-update-slice_fusion), channel_id=1, source_target_pairs={{0,1},{1,2},{2,3},{3,4},{4,5},{5,6},{6,7},{7,8},{8,9},{9,10},{10,1... | collective-permute-start | bytes 525320 | tf_op jit(solution)/shard_map/ppermute | solution.py:46
  699.3 402.6 %collective-permute-start.9 = (f32[4,2,5472]{2,0,1:T(4,128)}, f32[4,2,5472]{2,0,1:T(4,128)}, u32[]{:S(2)}, u32[]{:S(2)}) collective-permute-start(f32[4,2,5472]{2,0,1:T(4,128)} %constant_dynamic-update-slice_fusion), channel_id=1, source_target_pairs={{1,0},{2,1},{3,2},{4,3},{5,4},{6,5},{7,6},{8,7},{9,8},{10,9},{11,1... | collective-permute-start | bytes 525320 | tf_op jit(solution)/shard_map/ppermute | solution.py:48
  1553.3 27.3 %collective-permute-start.10 = (f32[4,2,4864]{2,0,1:T(4,128)S(1)}, f32[4,2,4864]{2,0,1:T(4,128)S(1)}, u32[]{:S(2)}, u32[]{:S(2)}) collective-permute-start(f32[4,2,4864]{2,0,1:T(4,128)S(1)} %pad_maximum_fusion.12), channel_id=1, source_target_pairs={{0,1},{1,2},{2,3},{3,4},{4,5},{5,6},{6,7},{7,8},{8,9},{9,10},{10,1... | collective-permute-start | bytes 466952 | tf_op jit(solution)/shard_map/ppermute | solution.py:46
  1557.0 23.6 %collective-permute-start.11 = (f32[4,2,4864]{2,0,1:T(4,128)S(1)}, f32[4,2,4864]{2,0,1:T(4,128)S(1)}, u32[]{:S(2)}, u32[]{:S(2)}) collective-permute-start(f32[4,2,4864]{2,0,1:T(4,128)S(1)} %pad_maximum_fusion.12), channel_id=1, source_target_pairs={{1,0},{2,1},{3,2},{4,3},{5,4},{6,5},{7,6},{8,7},{9,8},{10,9},{11,1... | collective-permute-start | bytes 466952 | tf_op jit(solution)/shard_map/ppermute | solution.py:48
  1603.6 27.4 %collective-permute-start.12 = (f32[4,2,5472]{2,0,1:T(4,128)S(1)}, f32[4,2,5472]{2,0,1:T(4,128)S(1)}, u32[]{:S(2)}, u32[]{:S(2)}) collective-permute-start(f32[4,2,5472]{2,0,1:T(4,128)S(1)} %constant_dynamic-update-slice_fusion.21), channel_id=1, source_target_pairs={{0,1},{1,2},{2,3},{3,4},{4,5},{5,6},{6,7},{7,8},{8,9},{9,10},{10,1... | collective-permute-start | bytes 525320 | tf_op jit(solution)/shard_map/ppermute | solution.py:46
  1607.2 23.8 %collective-permute-start.13 = (f32[4,2,5472]{2,0,1:T(4,128)S(1)}, f32[4,2,5472]{2,0,1:T(4,128)S(1)}, u32[]{:S(2)}, u32[]{:S(2)}) collective-permute-start(f32[4,2,5472]{2,0,1:T(4,128)S(1)} %constant_dynamic-update-slice_fusion.21), channel_id=1, source_target_pairs={{1,0},{2,1},{3,2},{4,3},{5,4},{6,5},{7,6},{8,7},{9,8},{10,9},{11,1... | collective-permute-start | bytes 525320 | tf_op jit(solution)/shard_map/ppermute | solution.py:48
  2105.5 36.4 %collective-permute-start.14 = (f32[4,9728]{1,0:T(4,128)S(1)}, f32[4,9728]{1,0:T(4,128)S(1)}, u32[]{:S(2)}, u32[]{:S(2)}) collective-permute-start(f32[4,9728]{1,0:T(4,128)S(1)} %bitcast.920), channel_id=1, source_target_pairs={{3,0},{4,1},{5,2},{6,3},{7,4},{8,5},{9,6},{10,7},{11,8},{12,9},{13... | collective-permute-start | bytes 466952 | tf_op jit(solution)/shard_map/ppermute | solution.py:58
  2127.9 34.0 %collective-permute-start.15 = (f32[4,9728]{1,0:T(4,128)S(1)}, f32[4,9728]{1,0:T(4,128)S(1)}, u32[]{:S(2)}, u32[]{:S(2)}) collective-permute-start(f32[4,9728]{1,0:T(4,128)S(1)} %bitcast.921), channel_id=1, source_target_pairs={{2,0},{3,1},{4,2},{5,3},{6,4},{7,5},{8,6},{9,7},{10,8},{11,9},{12,... | collective-permute-start | bytes 466952 | tf_op jit(solution)/shard_map/ppermute | solution.py:58
  2129.2 33.5 %collective-permute-start.16 = (f32[4,9728]{1,0:T(4,128)S(1)}, f32[4,9728]{1,0:T(4,128)S(1)}, u32[]{:S(2)}, u32[]{:S(2)}) collective-permute-start(f32[4,9728]{1,0:T(4,128)S(1)} %bitcast.922), channel_id=1, source_target_pairs={{1,0},{2,1},{3,2},{4,3},{5,4},{6,5},{7,6},{8,7},{9,8},{10,9},{11,1... | collective-permute-start | bytes 466952 | tf_op jit(solution)/shard_map/ppermute | solution.py:58
  2131.1 32.4 %collective-permute-start.17 = (f32[4,9728]{1,0:T(4,128)S(1)}, f32[4,9728]{1,0:T(4,128)S(1)}, u32[]{:S(2)}, u32[]{:S(2)}) collective-permute-start(f32[4,9728]{1,0:T(4,128)S(1)} %bitcast.923), channel_id=1, source_target_pairs={{0,1},{1,2},{2,3},{3,4},{4,5},{5,6},{6,7},{7,8},{8,9},{9,10},{10,1... | collective-permute-start | bytes 466952 | tf_op jit(solution)/shard_map/ppermute | solution.py:58
  2135.4 28.9 %collective-permute-start.18 = (f32[4,9728]{1,0:T(4,128)S(1)}, f32[4,9728]{1,0:T(4,128)S(1)}, u32[]{:S(2)}, u32[]{:S(2)}) collective-permute-start(f32[4,9728]{1,0:T(4,128)S(1)} %bitcast.924), channel_id=1, source_target_pairs={{0,2},{1,3},{2,4},{3,5},{4,6},{5,7},{6,8},{7,9},{8,10},{9,11},{10,... | collective-permute-start | bytes 466952 | tf_op jit(solution)/shard_map/ppermute | solution.py:58
  2141.9 23.3 %collective-permute-start.19 = (f32[4,9728]{1,0:T(4,128)S(1)}, f32[4,9728]{1,0:T(4,128)S(1)}, u32[]{:S(2)}, u32[]{:S(2)}) collective-permute-start(f32[4,9728]{1,0:T(4,128)S(1)} %bitcast.925), channel_id=1, source_target_pairs={{0,3},{1,4},{2,5},{3,6},{4,7},{5,8},{6,9},{7,10},{8,11},{9,12},{10... | collective-permute-start | bytes 466952 | tf_op jit(solution)/shard_map/ppermute | solution.py:58
  (289 other events, 5129.2 us)
where the time goes:
time: 2260 us; the launch traced here: 2220 us
  local copies, waits for them, and re-layouts  1980 us (88%)
  other arithmetic  147 us (7%)
  starting transfers between devices  87.1 us (4%)
    gather x113, local copies, waits for them, and re-layouts, stream(): jnp.take(source[:, i], jnp.asarray(stream_rows[i]), axis=1)  1070 us
    gather x38, local copies, waits for them, and re-layouts, fine_step(): from_wall = jnp.take(wall_source, jnp.asarray(stream_rows[i]), axis=1)  340 us
    squeeze x60, local copies, waits for them, and re-layouts, stream(): source[:, i]  146 us
    ppermute x12, starting transfers between devices, passed_along(): return lax.ppermute(block, axis, route)  46.7 us
  transfers between devices with their start and end apart: 26, of which 0 were waited for; matrix products, arithmetic and copies ran while one was open for 48% of the time, Pallas kernels for 0%

commit v1 on v0

v1 whole, which is shorter than its diff:
```python
import functools

import jax
import jax.numpy as jnp
from jax import lax
from jax.experimental import pallas as pl
from jax.experimental.pallas import tpu as pltpu
from jax.sharding import PartitionSpec as P

AXES = ("gx", "gy")
VELOCITIES = (
    (0, 0, 0),
    (1, 0, 0),
    (-1, 0, 0),
    (0, 1, 0),
    (0, -1, 0),
    (0, 0, 1),
    (0, 0, -1),
    (1, 1, 0),
    (-1, -1, 0),
    (1, -1, 0),
    (-1, 1, 0),
    (1, 0, 1),
    (-1, 0, -1),
    (1, 0, -1),
    (-1, 0, 1),
    (0, 1, 1),
    (0, -1, -1),
    (0, 1, -1),
    (0, -1, 1),
)
WEIGHTS = (1.0 / 3.0,) + (1.0 / 18.0,) * 6 + (1.0 / 36.0,) * 12
OPPOSITE = (0, 2, 1, 4, 3, 6, 5, 8, 7, 10, 9, 12, 11, 14, 13, 16, 15, 18, 17)
OMEGA_COARSE = 1.6
OMEGA_FINE = 1.0 / (2.0 * (1.0 / 1.6 - 0.5) + 0.5)

XP = (1, 7, 9, 11, 13)
XM = (2, 8, 10, 12, 14)
YP = (3, 7, 10, 15, 17)
YM = (4, 8, 9, 16, 18)
ZP = (5, 11, 14, 15, 18)
ZM = (6, 12, 13, 16, 17)
YP1, YM1 = (3, 15, 17), (4, 16, 18)
YP2, YM2 = (7, 10), (8, 9)
ZP2, ZM2 = (11, 14, 15, 18), (12, 13, 16, 17)

R = 32
BLOCK = 19 * R
FB, CB = 4, 2
EDGES = FB * 64
META = EDGES + R
F_ROWS = META + 8
E_BLOCK = 96
EC_AT = CB * E_BLOCK
E_ROWS = EC_AT + 8
C1_BLOCK = 72
C1_ROWS = CB * C1_BLOCK
C2_BLOCK = 64
C2_ROWS = CB * C2_BLOCK
K_ROWS = 2 * 19 * 8
EZ_BLOCK = 80
HALO = 3 * (META) + FB * 64


def iotas(rows=R):
    row = lax.broadcasted_iota(jnp.int32, (rows, 128), 0)
    lane = lax.broadcasted_iota(jnp.int32, (rows, 128), 1)
    return row, lane


def roll(a, shift, axis):
    if isinstance(shift, int):
        shift = shift % a.shape[axis]
        if shift == 0:
            return a
    return pltpu.roll(a, shift, axis)


def at(ref, start, size=R):
    if not isinstance(start, int):
        start = pl.multiple_of(start, 8)
    return ref[pl.ds(start, size), :]


def put(ref, start, value):
    if not isinstance(start, int):
        start = pl.multiple_of(start, 8)
    ref[pl.ds(start, value.shape[0]), :] = value


def rows_in(src, dst, blocks):
    def body(b, carry):
        for t, n in ((0, 8), (1, 8), (2, 3)):
            for r in range(R):
                dst[pl.ds(b * BLOCK + t * 8 * R + r, n, stride=R), :] = src[
                    b, 8 * t : 8 * t + n, 128 * r : 128 * r + 128
                ]
        return carry

    lax.fori_loop(0, blocks, body, 0)


def rows_out(src, dst, blocks):
    def body(b, carry):
        for t, n in ((0, 8), (1, 8), (2, 3)):
            for r in range(R):
                dst[b, 8 * t : 8 * t + n, 128 * r : 128 * r + 128] = src[
                    pl.ds(b * BLOCK + t * 8 * R + r, n, stride=R), :
                ]
        return carry

    lax.fori_loop(0, blocks, body, 0)


def collide(f, rate):
    rho = functools.reduce(lambda a, b: a + b, f)
    mom = []
    for axis in range(3):
        plus = [f[i] for i in range(19) if VELOCITIES[i][axis] == 1]
        minus = [f[i] for i in range(19) if VELOCITIES[i][axis] == -1]
        mom.append(sum(plus[1:], plus[0]) - sum(minus[1:], minus[0]))
    inv = 1.0 / rho
    u = [m * inv for m in mom]
    base = 1.0 - 1.5 * (u[0] * u[0] + u[1] * u[1] + u[2] * u[2])
    scaled = {w: (rate * w) * rho for w in sorted(set(WEIGHTS))}
    keep = 1.0 - rate
    out = [None] * 19
    out[0] = keep * f[0] + scaled[WEIGHTS[0]] * base
    for i in range(1, 19, 2):
        proj = None
        for axis in range(3):
            c = VELOCITIES[i][axis]
            if c:
                term = u[axis]
                if proj is None:
                    proj = term if c > 0 else -term
                else:
                    proj = proj + term if c > 0 else proj - term
        even = base + 4.5 * (proj * proj)
        odd = 3.0 * proj
        w = scaled[WEIGHTS[i]]
        out[i] = keep * f[i] + w * (even + odd)
        out[i + 1] = keep * f[i + 1] + w * (even - odd)
    return out


def collide_rows(src, src_base, dst, dst_base, rate, mask, mask_base):
    def body(v, carry):
        f = [at(src, src_base + i * R + v * 8, 8) for i in range(19)]
        post = collide(f, rate)
        if mask is not None:
            solid = (at(mask, mask_base + v * 8, 8) & 1) > 0
            post = [jnp.where(solid, f[i], post[i]) for i in range(19)]
        for i in range(19):
            put(dst, dst_base + i * R + v * 8, post[i])
        return carry

    lax.fori_loop(0, 4, body, 0)


def pack_x(get):
    _, lane = iotas()
    x = lane & 15
    packed = jnp.zeros((R, 128), jnp.float32)
    for j in range(5):
        packed = jnp.where(x == j, roll(get(XP[j]), j - 15, 1), packed)
        packed = jnp.where(x == 5 + j, roll(get(XM[j]), 5 + j, 1), packed)
    return packed


def swap_rows(a):
    row, _ = iotas()
    return jnp.where((row & 1) == 0, roll(a, -1, 0), roll(a, 1, 0))


def pack_y(get, plus, minus):
    row, lane = iotas()
    upper = (row & 1) == 1
    packed = jnp.zeros((R, 128), jnp.float32)
    for p in range(len(plus)):
        one = jnp.where(upper, roll(get(plus[p]), 16 * p - 112, 1), roll(get(minus[p]), 16 * p, 1))
        packed = jnp.where((lane >> 4) == p, one, packed)
    return swap_rows(packed)


def pack_edges(get):
    row, lane = iotas()
    upper = (row & 1) == 1
    first = jnp.where(upper, roll(get(7), -127, 1), get(8))
    second = jnp.where(upper, roll(get(10), 1 - 112, 1), roll(get(9), 1 - 15, 1))
    return swap_rows(jnp.where(lane == 0, first, second))


def move_x(a, cx, halo):
    _, lane = iotas()
    x = lane & 15
    if cx == 1:
        return jnp.where(x == 0, halo, roll(a, 1, 1))
    return jnp.where(x == 15, halo, roll(a, -1, 1))


def move_y(a, cy, halo):
    row, lane = iotas()
    upper = (row & 1) == 1
    if cy == 1:
        near = roll(a, 16, 1)
        return jnp.where(lane < 16, jnp.where(upper, roll(near, 1, 0), halo), near)
    near = roll(a, -16, 1)
    return jnp.where(lane >= 112, jnp.where(upper, halo, roll(near, -1, 0)), near)


def move_z(a, cz, halo8):
    row, _ = iotas(8)
    if cz == 1:
        near = roll(a, 2, 0)
        return jnp.concatenate([jnp.where(row < 2, halo8, near[:8]), near[8:]], axis=0)
    near = roll(a, -2, 0)
    return jnp.concatenate([near[:24], jnp.where(row >= 6, halo8, near[24:])], axis=0)


def send_faces(get, out, b):
    put(out, b * 64, pack_x(get))
    put(out, b * 64 + R, pack_y(get, YP, YM))
    _, lane = iotas()
    edges = roll(pack_edges(get), 2 * b, 1)
    put(out, EDGES, jnp.where((lane >> 1) == b, edges, at(out, EDGES)))


def place():
    device = lax.axis_index("gx") * lax.axis_size("gy") + lax.axis_index("gy")
    sign = 1 - 2 * (device & 1)
    return device, sign


def coarse_first_kernel(pop, post, e_out, c_out, raw):
    rows_in(pop, raw, CB)
    _, lane = iotas(16)
    _, lane8 = iotas(8)
    x16 = lane & 15
    corner = jnp.zeros((8, 128), jnp.float32)
    for c in range(CB):
        base = c * BLOCK
        half = lambda i: at(raw, base + i * R, 16)
        for qx in range(2):
            packed = jnp.zeros((16, 128), jnp.float32)
            for j in range(5):
                packed = jnp.where(x16 == j, roll(half(XP[j]), j - 8 * qx, 1), packed)
                packed = jnp.where(x16 == 5 + j, roll(half(XM[j]), 5 + j - 8 * qx - 7, 1), packed)
            put(e_out, c * E_BLOCK + qx * 16, packed)
        low = jnp.zeros((16, 128), jnp.float32)
        high = jnp.zeros((16, 128), jnp.float32)
        for p in range(5):
            low = jnp.where((lane >> 4) == p, roll(half(YP[p]), 16 * p, 1), low)
            high = jnp.where((lane >> 4) == p, roll(half(YM[p]), 16 * p - 112, 1), high)
        put(e_out, c * E_BLOCK + 32, low)
        put(e_out, c * E_BLOCK + 48, high)
        put(e_out, c * E_BLOCK + 64, jnp.zeros((R, 128), jnp.float32))
        for k in range(5):
            e_out[pl.ds(c * E_BLOCK + 64 + 2 * k, 2), :] = raw[pl.ds(base + ZP[k] * R, 2), :]
            e_out[pl.ds(c * E_BLOCK + 74 + 2 * k, 2), :] = raw[pl.ds(base + ZM[k] * R + 14, 2), :]
        for q in range(4):
            for e, (i, yq, xq) in enumerate(((7, 7, 0), (10, 7, 7), (9, 0, 0), (8, 0, 7))):
                to = (c * 4 + q) * 4 + e
                rows = raw[pl.ds(base + i * R + q // 2, 8, stride=2), :]
                rows = roll(rows, to - (yq * 16 + 8 * (q % 2) + xq), 1)
                corner = jnp.where(lane8 == to, rows, corner)
    put(e_out, EC_AT, corner)
    row8, _ = iotas(8)
    for c in range(CB):
        base = c * BLOCK
        collide_rows(raw, base, post, base, OMEGA_COARSE, None, 0)
        get = lambda i: at(post, base + i * R)
        put(c_out, c * C1_BLOCK, pack_x(get))
        put(c_out, c * C1_BLOCK + R, pack_y(get, YP1, YM1))
        top = roll(at(post, base + 5 * R + 24, 8), 2, 0)
        bottom = roll(at(post, base + 6 * R, 8), 6, 0)
        put(c_out, c * C1_BLOCK + 2 * R, jnp.where(row8 < 2, top, bottom))


def fine_first_kernel(nbr, parent, pop, solid, post, mask, f_out, raw, sol):
    rows_in(pop, raw, FB)
    for r in range(R):
        sol[pl.ds(r, FB, stride=R), :] = solid[:, 128 * r : 128 * r + 128]
    put(f_out, EDGES, jnp.zeros((R, 128), jnp.float32))

    def body(b, carry):
        s = jnp.where(at(sol, b * R) > 0, 1, 0)
        bits = s
        for i in range(1, 19):
            cx, cy, cz = VELOCITIES[i]
            m = s
            if cx:
                m = roll(m, cx, 1)
            if cy:
                m = move_y(m, cy, jnp.zeros_like(m))
            if cz:
                m = roll(m, 2 * cz, 0)
            bits = bits | (m << i)
        put(mask, b * R, bits)
        base = b * BLOCK
        collide_rows(raw, base, post, base, OMEGA_FINE, mask, b * R)
        send_faces(lambda i: at(post, base + i * R), f_out, b)
        return carry

    lax.fori_loop(0, FB, body, 0)
    row, lane = iotas(8)
    meta = jnp.zeros((8, 128), jnp.float32)
    for b in range(FB):
        for k in range(4):
            meta = jnp.where((row == b) & (lane == k), nbr[b, k].astype(jnp.float32), meta)
        for k in range(2):
            meta = jnp.where((row == b) & (lane == 4 + k), parent[b, k].astype(jnp.float32), meta)
    put(f_out, META, meta)


def onehot(rows, cols, source):
    row = lax.broadcasted_iota(jnp.int32, (rows, cols), 0)
    col = lax.broadcasted_iota(jnp.int32, (rows, cols), 1)
    return jnp.where(row == source(col), 1.0, 0.0).astype(jnp.float32)


def exact_dot(a, b):
    return jnp.dot(a, b, preferred_element_type=jnp.float32, precision=lax.Precision.HIGHEST)


def expand(parent, device, gathered, halo, ez):
    _, lane = iotas(16)
    row, _ = iotas(16)
    x = lane & 15
    spread_x = onehot(
        128, 256, lambda m: ((m >> 7) * 4 + ((m & 127) >> 5)) * 16 + (m & 15)
    )

    def body(b, carry):
        p, q = parent[b, 0], parent[b, 1]
        qy, qx = q >> 1, q & 1
        base = ((p >> 1) ^ device) * E_ROWS + (p & 1) * E_BLOCK
        home = 3 * META + b * 64
        ex = exact_dot(gathered[pl.ds(base + qx * 16 + qy, 8, stride=2), :], spread_x)
        spread_y = onehot(128, 128, lambda m: (m >> 4) * 16 + 8 * qx + ((m & 15) >> 1))
        ey0 = exact_dot(gathered[pl.ds(base + 32 + qy, 8, stride=2), :], spread_y)
        ey1 = exact_dot(gathered[pl.ds(base + 48 + qy, 8, stride=2), :], spread_y)
        for k in range(2):
            halo[pl.ds(home + 2 * k, 8, stride=4), :] = ex[:, :128]
            halo[pl.ds(home + 2 * k + 1, 8, stride=4), :] = ex[:, 128:]
            halo[pl.ds(home + R + 2 * k, 8, stride=4), :] = ey0
            halo[pl.ds(home + R + 2 * k + 1, 8, stride=4), :] = ey1
        spread_z = onehot(
            128,
            256,
            lambda m: ((m >> 7) * 4 + ((m & 127) >> 5)) * 16 + 8 * qx + ((m & 15) >> 1),
        )
        ezs = exact_dot(gathered[pl.ds(base + 64 + qy, 16, stride=2), :], spread_z)
        a0, a1 = ezs[:, :128], ezs[:, 128:]
        moves = {}
        moves[0, 0] = (a0, a1)
        moves[1, 0] = tuple(jnp.where(x == 0, a, roll(a, 1, 1)) for a in (a0, a1))
        moves[-1, 0] = tuple(jnp.where(x == 15, a, roll(a, -1, 1)) for a in (a0, a1))
        moves[0, 1] = (
            jnp.where(lane < 16, a0, roll(a0, 16, 1)),
            jnp.where(lane < 16, roll(a0, 16, 1), roll(a1, 16, 1)),
        )
        moves[0, -1] = (
            jnp.where(lane >= 112, roll(a1, -16, 1), roll(a0, -16, 1)),
            jnp.where(lane >= 112, a1, roll(a1, -16, 1)),
        )
        out = [a0, a1]
        for k, i in enumerate(ZP + ZM):
            moved = moves[VELOCITIES[i][:2]]
            out = [jnp.where(row == k, moved[h], out[h]) for h in range(2)]
        for h in range(2):
            for k in range(5):
                ez[pl.ds(b * EZ_BLOCK + 8 * k + h, 1), :] = out[h][k : k + 1]
                ez[pl.ds(b * EZ_BLOCK + 40 + 8 * k + 6 + h, 1), :] = out[h][5 + k : 6 + k]
        return carry

    lax.fori_loop(0, FB, body, 0)


def gather_halo(own, x_in, n_in, x_late, relayed, halo, edges):
    for k, ref in enumerate((n_in, own, x_in)):
        put(halo, k * META, ref[0:META, :])
        put(edges, (k + 1) * R, ref[EDGES : EDGES + R, :])
    put(edges, 0, n_in[pl.ds(relayed, R), :])
    put(edges, 4 * R, x_late[...])


def corners(nbr, meta_n, meta_own, meta_x, device, sign, halo, edges, fixed, b):
    row, lane = iotas()
    upper = (row & 1) == 1
    result = jnp.zeros((R, 128), jnp.float32)
    for side in range(2):
        n = nbr[b, 2 + side]
        safe = jnp.maximum(n, 0)
        which = ((safe >> 2) - device) * sign + 1
        which = jnp.clip(which, 0, 2)
        row_n = safe & 3
        for end in range(2):
            i = ((7, 10), (9, 8))[side][end]
            p = (YP, YM)[side].index(i)
            edge_col = ((0, 1), (1, 0))[side][end]
            to = 112 * side + 15 * end
            m = jnp.where(
                which == 0,
                meta_n[row_n, end],
                jnp.where(which == 1, meta_own[row_n, end], meta_x[row_n, end]),
            ).astype(jnp.int32)
            m_safe = jnp.maximum(m, 0)
            slot = jnp.clip(((m_safe >> 2) - device) * sign + 2, 0, 4)
            shift = (to - (2 * (m_safe & 3) + edge_col)) & 127
            sent = roll(at(edges, slot * R), shift, 1)
            own = roll(at(halo, 3 * META + b * 64 + R), to - (16 * p + 15 * end), 1)
            value = jnp.where(n < 0, own, jnp.where(m >= 0, sent, at(fixed, b * R)))
            here = (lane == to) & (upper if side else jnp.logical_not(upper))
            result = jnp.where(here, value, result)
    return result


def fixed_corners(nbr, meta_n, meta_own, meta_x, device, sign, group, from_n, fixed, spare):
    _, lane = iotas()
    npart = device - sign

    def body(b, carry):
        result = jnp.zeros((R, 128), jnp.float32)
        for side in range(2):
            safe = jnp.maximum(nbr[b, 2 + side], 0)
            which = jnp.clip(((safe >> 2) - device) * sign + 1, 0, 2)
            row_n = safe & 3
            pq = [
                jnp.where(
                    which == 0,
                    meta_n[row_n, 4 + k],
                    jnp.where(which == 1, meta_own[row_n, 4 + k], meta_x[row_n, 4 + k]),
                ).astype(jnp.int32)
                for k in range(2)
            ]
            p, q = pq
            near = ((p >> 1) ^ device) & 3
            far = ((p >> 1) ^ npart) & 3
            quad = jnp.where(
                which == 0, at(from_n, far * 8, 8), at(group, near * E_ROWS + EC_AT, 8)
            )
            for k in range(4):
                spare[pl.ds(k, 8, stride=4), :] = quad
            rows = spare[...]
            for end in range(2):
                to = 112 * side + 15 * end
                source = ((p & 1) * 4 + q) * 4 + 2 * side + end
                result = jnp.where(lane == to, roll(rows, (to - source) & 127, 1), result)
        put(fixed, b * R, result)
        return carry

    lax.fori_loop(0, FB, body, 0)


def stream_fine(nbr, device, sign, post, mask, halo, ez, corner, dst, dst_base, b):
    base = b * BLOCK
    bits = at(mask, b * R)
    faces = []
    for k in range(4):
        n = nbr[b, k]
        safe = jnp.maximum(n, 0)
        which = jnp.clip(((safe >> 2) - device) * sign + 1, 0, 2)
        start = jnp.where(n >= 0, which * META + (safe & 3) * 64, 3 * META + b * 64)
        faces.append(at(halo, start + (R if k >= 2 else 0)))
    row, lane = iotas()
    solid = (bits & 1) > 0
    for i in range(19):
        cx, cy, cz = VELOCITIES[i]
        a = at(post, base + i * R)
        if i == 0:
            put(dst, dst_base, a)
            continue
        g = a
        if cx == 1:
            g = move_x(g, 1, roll(faces[0], -XP.index(i), 1))
        elif cx == -1:
            g = move_x(g, -1, roll(faces[1], 10 - XM.index(i), 1))
        if cy:
            first = 112 * (cy == -1)
            p = (YP if cy == 1 else YM).index(i)
            side = roll(faces[2 if cy == 1 else 3], first - 16 * p + cx, 1)
            if cx:
                side = jnp.where(lane == first + (0 if cx == 1 else 15), corner, side)
            g = move_y(g, cy, side)
        if cz:
            k = ZP.index(i) if cz == 1 else 5 + ZM.index(i)
            g = move_z(g, cz, at(ez, b * EZ_BLOCK + 8 * k, 8))
        from_wall = (bits & (1 << i)) > 0
        g = jnp.where(from_wall, at(post, base + OPPOSITE[i] * R), g)
        put(dst, dst_base + i * R, jnp.where(solid, a, g))


def fetch_meta(pairs, sem):
    copies = [
        pltpu.make_async_copy(ref.at[pl.ds(META, 8)], dst, sem.at[k])
        for k, (ref, dst) in enumerate(pairs)
    ]
    for c in copies:
        c.start()
    return copies


X_E = F_ROWS
X_E2 = X_E + E_ROWS
X_C = X_E2 + E_ROWS
X_ROWS = X_C + C1_ROWS
N_EDGE = F_ROWS
N_EC = N_EDGE + R
N_C = N_EC + 4 * 8
N_ROWS = N_C + C1_ROWS


def coarse_source(index, device, sign):
    safe = jnp.maximum(index, 0)
    which = jnp.clip(((safe >> 1) - device) * sign + 1, 0, 2)
    return which, safe & 1


def middle_kernel(
    nbr,
    parent,
    cnbr,
    post,
    mask,
    f_own,
    e_own,
    e_two,
    x_in,
    n_in,
    x_late,
    cpost,
    c_own,
    post2,
    f_out,
    e_halo,
    ez,
    fixed,
    cmid,
    c_out,
    gathered,
    halo,
    edges,
    spare,
    new,
    chalo,
    meta_n,
    meta_own,
    meta_x,
    sem,
):
    device, sign = place()
    copies = fetch_meta(((n_in, meta_n), (f_own, meta_own), (x_in, meta_x)), sem)
    put(gathered, 0, e_own[...])
    put(gathered, E_ROWS, x_in[X_E : X_E + E_ROWS, :])
    put(gathered, 2 * E_ROWS, e_two[...])
    put(gathered, 3 * E_ROWS, x_in[X_E2 : X_E2 + E_ROWS, :])
    expand(parent, device, gathered, halo, ez)
    put(e_halo, 0, halo[3 * META : HALO, :])
    gather_halo(f_own, x_in, n_in, x_late, N_EDGE, halo, edges)
    for c in copies:
        c.wait()
    fixed_corners(
        nbr,
        meta_n,
        meta_own,
        meta_x,
        device,
        sign,
        gathered,
        n_in.at[pl.ds(N_EC, 32)],
        fixed,
        spare,
    )
    put(f_out, EDGES, jnp.zeros((R, 128), jnp.float32))
    put(f_out, META, jnp.zeros((8, 128), jnp.float32))

    def body(b, carry):
        corner = corners(nbr, meta_n, meta_own, meta_x, device, sign, halo, edges, fixed, b)
        stream_fine(nbr, device, sign, post, mask, halo, ez, corner, new, 0, b)
        base = b * BLOCK
        collide_rows(new, 0, post2, base, OMEGA_FINE, mask, b * R)
        send_faces(lambda i: at(post2, base + i * R), f_out, b)
        return carry

    lax.fori_loop(0, FB, body, 0)

    put(chalo, 0, n_in[N_C : N_C + C1_ROWS, :])
    put(chalo, C1_ROWS, c_own[...])
    put(chalo, 2 * C1_ROWS, x_in[X_C : X_C + C1_ROWS, :])
    row8, _ = iotas(8)

    def coarse_body(c, carry):
        base = c * BLOCK
        has, sources = [], []
        for k in range(6):
            which, slot = coarse_source(cnbr[c, k], device, sign)
            has.append(cnbr[c, k] >= 0)
            sources.append(which * C1_ROWS + slot * C1_BLOCK)
        faces = [at(chalo, sources[k] + (0 if k < 2 else R)) for k in range(4)]
        zs = [at(chalo, sources[k] + 2 * R, 8) for k in (4, 5)]
        put(cmid, base, at(cpost, base))
        for i in range(1, 19):
            cx, cy, cz = VELOCITIES[i]
            a = at(cpost, base + i * R)
            if cx == 1:
                g = move_x(a, 1, jnp.where(has[0], roll(faces[0], -XP.index(i), 1), a))
            elif cx == -1:
                g = move_x(a, -1, jnp.where(has[1], roll(faces[1], 10 - XM.index(i), 1), a))
            elif cy == 1:
                side = roll(faces[2], -16 * YP1.index(i), 1)
                g = move_y(a, 1, jnp.where(has[2], side, a))
            elif cy == -1:
                side = roll(faces[3], 112 - 16 * YM1.index(i), 1)
                g = move_y(a, -1, jnp.where(has[3], side, a))
            elif cz == 1:
                g = move_z(a, 1, jnp.where(has[4], zs[0], a[:8]))
            else:
                g = move_z(a, -1, jnp.where(has[5], zs[1], a[24:]))
            put(cmid, base + i * R, g)
        get = lambda i: at(cmid, base + i * R)
        put(c_out, c * C2_BLOCK, pack_y(get, YP2, YM2))
        for k in range(4):
            top = roll(at(cmid, base + ZP2[k] * R + 24, 8), 2, 0)
            bottom = roll(at(cmid, base + ZM2[k] * R, 8), 6, 0)
            put(c_out, c * C2_BLOCK + R + 8 * k, jnp.where(row8 < 2, top, bottom))
        return carry

    lax.fori_loop(0, CB, coarse_body, 0)


X2_C = F_ROWS
N2_EDGE = F_ROWS
N2_C = N2_EDGE + R


def fine_last_kernel(
    nbr,
    cnbr,
    post,
    mask,
    f_own,
    x_in,
    n_in,
    x_late,
    e_halo,
    ez,
    fixed,
    f_first,
    x_first,
    n_first,
    cmid,
    c_own,
    fine_out,
    means,
    cpassed,
    halo,
    edges,
    new,
    summed,
    chalo,
    meta_n,
    meta_own,
    meta_x,
    sem,
):
    device, sign = place()
    copies = fetch_meta(((n_first, meta_n), (f_first, meta_own), (x_first, meta_x)), sem)
    gather_halo(f_own, x_in, n_in, x_late, N2_EDGE, halo, edges)
    put(halo, 3 * META, e_halo[...])
    for c in copies:
        c.wait()

    def body(b, carry):
        corner = corners(nbr, meta_n, meta_own, meta_x, device, sign, halo, edges, fixed, b)
        stream_fine(nbr, device, sign, post, mask, halo, ez, corner, new, b * BLOCK, b)
        return carry

    lax.fori_loop(0, FB, body, 0)
    rows_out(new, fine_out, FB)

    row = lax.broadcasted_iota(jnp.int32, (128, 128), 0)
    col = lax.broadcasted_iota(jnp.int32, (128, 128), 1)
    target = lambda yh, h: (yh * 4 + (row >> 5)) * 16 + ((row & 15) >> 1) + 8 * h
    mats = [
        [jnp.where(col == target(yh, h), 0.125, 0.0).astype(jnp.float32) for yh in range(2)]
        for h in range(2)
    ]
    rows = 19 * 8
    for pair in range(2):
        total = None
        for h in range(2):
            b = 2 * pair + h
            for yh in range(2):
                z0 = new[pl.ds(b * BLOCK + yh, rows, stride=4), :]
                z1 = new[pl.ds(b * BLOCK + 2 + yh, rows, stride=4), :]
                part = exact_dot(z0 + z1, mats[h][yh])
                total = part if total is None else total + part
        put(means, pair * rows, total)

    put(chalo, 0, n_in[N2_C : N2_C + C2_ROWS, :])
    put(chalo, C2_ROWS, c_own[...])
    put(chalo, 2 * C2_ROWS, x_in[X2_C : X2_C + C2_ROWS, :])

    def coarse_body(c, carry):
        base = c * BLOCK
        has, sources = [], []
        for k in range(6):
            which, slot = coarse_source(cnbr[c, k], device, sign)
            has.append(cnbr[c, k] >= 0)
            sources.append(which * C2_ROWS + slot * C2_BLOCK)
        faces = [at(chalo, sources[k]) for k in (2, 3)]
        for i in range(19):
            a = at(cmid, base + i * R)
            g = a
            if i in YP2:
                g = move_y(a, 1, jnp.where(has[2], roll(faces[0], -16 * YP2.index(i), 1), a))
            elif i in YM2:
                side = roll(faces[1], 112 - 16 * YM2.index(i), 1)
                g = move_y(a, -1, jnp.where(has[3], side, a))
            elif i in ZP2:
                side = at(chalo, sources[4] + R + 8 * ZP2.index(i), 8)
                g = move_z(a, 1, jnp.where(has[4], side, a[:8]))
            elif i in ZM2:
                side = at(chalo, sources[5] + R + 8 * ZM2.index(i), 8)
                g = move_z(a, -1, jnp.where(has[5], side, a[24:]))
            put(cpassed, base + i * R, g)
        return carry

    lax.fori_loop(0, CB, coarse_body, 0)


def coarse_last_kernel(children, cpassed, own, two, x_in, coarse_out, merged, gathered):
    device, _ = place()
    put(gathered, 0, own[...])
    put(gathered, K_ROWS, x_in[0:K_ROWS, :])
    put(gathered, 2 * K_ROWS, two[...])
    put(gathered, 3 * K_ROWS, x_in[K_ROWS : 2 * K_ROWS, :])
    merged[...] = cpassed[...]
    _, lane = iotas(8)
    x_half = (lane >> 3) & 1

    def body(step, carry):
        c, q = step >> 2, step & 3
        qy, qx = q >> 1, q & 1
        child = children[c, q]

        @pl.when(child >= 0)
        def _():
            slot = ((child >> 2) ^ device) & 3
            start = slot * K_ROWS + ((child & 3) >> 1) * (19 * 8)
            shift = (8 * (qx - (child & 1))) & 127
            mine = x_half == qx
            for i in range(19):
                value = roll(at(gathered, start + 8 * i, 8), shift, 1)
                rows = pl.ds(c * BLOCK + i * R + qy, 8, stride=2)
                merged[rows, :] = jnp.where(mine, value, merged[rows, :])

        return carry

    lax.fori_loop(0, CB * 4, body, 0)
    rows_out(merged, coarse_out, CB)


VMEM = pl.BlockSpec(memory_space=pltpu.VMEM)
SMEM = pl.BlockSpec(memory_space=pltpu.SMEM)


def rows_of(n, dtype=jnp.float32):
    return jax.ShapeDtypeStruct((n, 128), dtype)


def scratch(n, dtype=jnp.float32):
    return pltpu.VMEM((n, 128), dtype)


def call(kernel, name, specs, outs, scratches):
    return pl.pallas_call(
        kernel,
        name=name,
        in_specs=specs,
        out_specs=[VMEM] * len(outs),
        out_shape=outs,
        scratch_shapes=scratches,
        compiler_params=pltpu.CompilerParams(vmem_limit_bytes=32 * 1024 * 1024),
    )


def meta_scratch():
    return [pltpu.SMEM((8, 128), jnp.float32)] * 3 + [pltpu.SemaphoreType.DMA((3,))]


def exchange(rows, devices, partner):
    return lax.ppermute(rows, AXES, [(i, partner(i)) for i in range(devices)])


def on_device(fine_pop, coarse_pop, fine_nbr, coarse_nbr, parent, children, solid):
    devices = lax.axis_size(AXES)
    by_one = lambda a: exchange(a, devices, lambda i: i ^ 1)
    by_two = lambda a: exchange(a, devices, lambda i: i ^ 2)
    odd_even = lambda a: exchange(a, devices, lambda i: (((i + 1) ^ 1) - 1) % devices)

    cpost, e_own, c_own = call(
        coarse_first_kernel,
        "coarse_first",
        [VMEM],
        [rows_of(CB * BLOCK), rows_of(E_ROWS), rows_of(C1_ROWS)],
        [scratch(CB * BLOCK)],
    )(coarse_pop)
    e_two = by_two(e_own)
    post, mask, f_own = call(
        fine_first_kernel,
        "fine_first",
        [SMEM, SMEM, VMEM, VMEM],
        [rows_of(FB * BLOCK), rows_of(FB * R, jnp.int32), rows_of(F_ROWS)],
        [scratch(FB * BLOCK), scratch(FB * R, jnp.int32)],
    )(fine_nbr, parent, fine_pop, solid)

    x_in = by_one(jnp.concatenate([f_own, e_own, e_two, c_own]))
    n_in = odd_even(
        jnp.concatenate(
            [
                f_own,
                x_in[EDGES:META],
                e_own[EC_AT:],
                x_in[X_E + EC_AT : X_E2],
                e_two[EC_AT:],
                x_in[X_E2 + EC_AT : X_C],
                c_own,
            ]
        )
    )
    x_late = by_one(n_in[EDGES:META])
    post2, f2_own, e_halo, ez, fixed, cmid, c2_own = call(
        middle_kernel,
        "middle",
        [SMEM] * 3 + [VMEM] * 10,
        [
            rows_of(FB * BLOCK),
            rows_of(F_ROWS),
            rows_of(FB * 64),
            rows_of(FB * EZ_BLOCK),
            rows_of(FB * R),
            rows_of(CB * BLOCK),
            rows_of(C2_ROWS),
        ],
        [
            scratch(4 * E_ROWS),
            scratch(HALO),
            scratch(5 * R),
            scratch(R),
            scratch(BLOCK),
            scratch(3 * C1_ROWS),
        ]
        + meta_scratch(),
    )(
        fine_nbr,
        parent,
        coarse_nbr,
        post,
        mask,
        f_own,
        e_own,
        e_two,
        x_in,
        n_in,
        x_late,
        cpost,
        c_own,
    )

    x2_in = by_one(jnp.concatenate([f2_own, c2_own]))
    n2_in = odd_even(jnp.concatenate([f2_own, x2_in[EDGES:META], c2_own]))
    x2_late = by_one(n2_in[EDGES:META])
    fine_out, means, cpassed = call(
        fine_last_kernel,
        "fine_last",
        [SMEM] * 2 + [VMEM] * 14,
        [
            jax.ShapeDtypeStruct(fine_pop.shape, jnp.float32),
            rows_of(K_ROWS),
            rows_of(CB * BLOCK),
        ],
        [
            scratch(HALO),
            scratch(5 * R),
            scratch(FB * BLOCK),
            scratch(8),
            scratch(3 * C2_ROWS),
        ]
        + meta_scratch(),
    )(
        fine_nbr,
        coarse_nbr,
        post2,
        mask,
        f2_own,
        x2_in,
        n2_in,
        x2_late,
        e_halo,
        ez,
        fixed,
        f_own,
        x_in,
        n_in,
        cmid,
        c2_own,
    )

    k_two = by_two(means)
    k_one = by_one(jnp.concatenate([means, k_two]))
    (coarse_out,) = call(
        coarse_last_kernel,
        "coarse_last",
        [SMEM] + [VMEM] * 4,
        [jax.ShapeDtypeStruct(coarse_pop.shape, jnp.float32)],
        [scratch(CB * BLOCK), scratch(4 * K_ROWS)],
    )(children, cpassed, means, k_two, k_one)
    return fine_out, coarse_out


def solution(mesh):
    rows = P(AXES, None)
    blocks = P(AXES, None, None)
    return jax.shard_map(
        on_device,
        mesh=mesh,
        in_specs=(blocks, blocks, rows, rows, rows, rows, rows),
        out_specs=(blocks, blocks),
        check_vma=False,
    )
```

time: 2260 us -> 62.8 us (0.03); the launches traced: 2220 us -> 62.7 us
  local copies, waits for them, and re-layouts: 1980 us -> 5.67 us
  other arithmetic: 147 us -> 0.09 us
  starting transfers between devices: 87.1 us -> 17.5 us
    gather x254 -> x0, local copies, waits for them, and re-layouts: 1710 us -> none  [the longest x113 1070 us: stream(): jnp.take(source[:, i], jnp.asarray(stream_rows[i]), axis=1)]
    squeeze x67 -> x0, local copies, waits for them, and re-layouts: 147 us -> none  [the longest x60 146 us: stream(): source[:, i]]
    ppermute x26 -> x9, starting transfers between devices: 87.1 us -> 17.5 us  [exchange(): return lax.ppermute(rows, AXES, [(i, partner(i)) for i in range(devices)])]
    select_n x60 -> x0, other arithmetic: 60.8 us -> none  [the longest x1 14.6 us: on_device(): coarse_new = jnp.where(cell_mask[:, None, :], lifted, passed)]
    concatenate x9 -> x1, local copies, waits for them, and re-layouts: 43.9 us -> 0.01 us  [on_device(): jnp.concatenate([f_own, x_in[EDGES:META], e_own[EC_AT:], x_in[X_E + EC_AT...]
    gather x36 -> x0, other arithmetic: 26.3 us -> none
    select_n x8 -> x0, local copies, waits for them, and re-layouts: 24.7 us -> none  [the longest x2 11.7 us: fine_step(): jnp.where(solid_mask[:, None, :], populations, collide(populations, OMEGA...]
  transfers between devices with their start and end apart: 26 -> 9, of which waited for: 0 -> 7; matrix products, arithmetic and copies ran while one was open for 48% -> 4% of each run, Pallas kernels for 0% -> 6%
where the time goes in v1:
time: 62.8 us; the launch traced here: 62.7 us
  waiting for transfers between devices  20.3 us (32%)
  Pallas kernels  18.4 us (29%)
  starting transfers between devices  17.5 us (28%)
  local copies, waits for them, and re-layouts  5.67 us (9%)
  between operations  0.77 us (1%)
    ppermute x9, waiting for transfers between devices, exchange(): return lax.ppermute(rows, AXES, [(i, partner(i)) for i in range(devices)])  20.3 us
    ppermute x9, starting transfers between devices, exchange(): return lax.ppermute(rows, AXES, [(i, partner(i)) for i in range(devices)])  17.5 us
    pallas_call x1, Pallas kernels, on_device(): call(middle_kernel, 'middle', [SMEM] * 3 + [VMEM] * 10, [rows_of(FB * BLO...  6.64 us
    unnamed x23, local copies, waits for them, and re-layouts  5.65 us
    pallas_call x1, Pallas kernels, on_device(): call(fine_last_kernel, 'fine_last', [SMEM] * 2 + [VMEM] * 14, [jax.ShapeD...  5.27 us
    pallas_call x1, Pallas kernels, on_device(): call(fine_first_kernel, 'fine_first', [SMEM, SMEM, VMEM, VMEM], [rows_of(...  3.59 us
    pallas_call x1, Pallas kernels, on_device(): call(coarse_last_kernel, 'coarse_last', [SMEM] + [VMEM] * 4, [jax.ShapeDt...  1.63 us
  transfers between devices with their start and end apart: 9, of which 7 were waited for; matrix products, arithmetic and copies ran while one was open for 4% of the time, Pallas kernels for 6%

profile of v1, /device:TPU:1, one launch (start us, length us, event | category | flops | bytes accessed | tf_op | source)
XLA Modules:
  0.0 62.7 jit_solution(8552276396702515495)
XLA Ops:
  0.6 0.0 copy-start.5
  0.6 0.0 copy-start.4
  0.6 1.5 %copy.11.pop = f32[2,19,4096]{2,1,0:T(8,128)S(1)} copy(f32[2,19,4096]{2,0,1:T(2,128)} %param.8) | data formatting | bytes 1245184 | tf_op args[1]
  2.2 1.2 %coarse_first.1 = (f32[1216,128]{1,0:T(8,128)S(1)}, f32[200,128]{1,0:T(8,128)S(1)}, f32[144,128]{1,0:T(8,128)S(1)}) custom-call(f32[2,19,4096]{2,1,0:T(8,128)S(1)} %copy.11.pop), custom_call_target="tpu_custom_call" | custom-call | tf_op jit(solution)/shard_map/coarse_first/pallas_call | solution.py:803
  3.4 2.2 %collective-permute-start = (f32[200,128]{1,0:T(8,128)S(1)}, f32[200,128]{1,0:T(8,128)S(1)}, u32[]{:S(2)}, u32[]{:S(2)}) collective-permute-start(f32[200,128]{1,0:T(8,128)S(1)} %get-tuple-element.21.e_own), channel_id=1, source_target_pairs={{0,2},{1,3},{2,0},{3,1},{4,6},{5,7},{6,4},{7,5},{8,10},{9,11},{10,... | collective-permute-start | bytes 307208 | tf_op jit(solution)/shard_map/ppermute | solution.py:794
  5.6 0.0 copy-done.5
  5.6 0.1 copy.12.parent
  5.7 0.7 %copy.10.pop = f32[4,19,4096]{2,1,0:T(8,128)S(1)} copy(f32[4,19,4096]{2,0,1:T(4,128)S(1)} %copy-done.4) | data formatting | bytes 2490368 | tf_op args[0]
  6.5 0.1 copy-done
  6.6 3.6 %fine_first.1 = (f32[2432,128]{1,0:T(8,128)S(1)}, s32[128,128]{1,0:T(8,128)S(1)}, f32[296,128]{1,0:T(8,128)S(1)}) custom-call(s32[4,4]{1,0:T(4,128)S(1)} %copy-done.1, s32[4,2]{1,0:T(4,128)S(1)} %copy.12.parent, f32[4,19,4096]{2,1,0:T(8,128)S(1)} %copy.10.pop, s32[4,4096]{1,0:T(4,128)S(1)} %copy-done), custom_call_target="tpu_custom_call" | custom-call | tf_op jit(solution)/shard_map/fine_first/pallas_call | solution.py:811
  10.2 0.0 collective-permute-done.e_two
  10.2 1.0 %collective-permute-start.1 = (f32[840,128]{1,0:T(8,128)S(1)}, f32[840,128]{1,0:T(8,128)S(1)}, u32[]{:S(2)}, u32[]{:S(2)}) collective-permute-start(f32[840,128]{1,0:T(8,128)S(1)} %pad_maximum_fusion), channel_id=1, source_target_pairs={{0,1},{1,0},{2,3},{3,2},{4,5},{5,4},{6,7},{7,6},{8,9},{9,8},{10,11... | collective-permute-start | bytes 1290248 | tf_op jit(solution)/shard_map/ppermute | solution.py:794
  11.3 1.4 %collective-permute-done.1.x_in.x_first = f32[840,128]{1,0:T(8,128)S(1)} collective-permute-done((f32[840,128]{1,0:T(8,128)S(1)}, f32[840,128]{1,0:T(8,128)S(1)}, u32[]{:S(2)}, u32[]{:S(2)}) %collective-permute-start.1) | collective-permute-done | bytes 430112 | tf_op jit(solution)/shard_map/ppermute | solution.py:794
  12.7 0.4 collective-permute-start.2
  13.1 5.4 %collective-permute-done.2.n_in.n_first = f32[504,128]{1,0:T(8,128)S(1)} collective-permute-done((f32[504,128]{1,0:T(8,128)S(1)}, f32[504,128]{1,0:T(8,128)S(1)}, u32[]{:S(2)}, u32[]{:S(2)}) %collective-permute-start.2) | collective-permute-done | bytes 258080 | tf_op jit(solution)/shard_map/ppermute | solution.py:794
  18.5 6.2 %collective-permute-start.3 = (f32[32,128]{1,0:T(8,128)S(1)}, f32[32,128]{1,0:T(8,128)S(1)}, u32[]{:S(2)}, u32[]{:S(2)}) collective-permute-start(f32[32,128]{1,0:T(8,128)S(1)} %slice.36), channel_id=1, source_target_pairs={{0,1},{1,0},{2,3},{3,2},{4,5},{5,4},{6,7},{7,6},{8,9},{9,8},{10,11... | collective-permute-start | bytes 49160 | tf_op jit(solution)/shard_map/ppermute | solution.py:794
  24.8 0.8 %collective-permute-done.3.x_late = f32[32,128]{1,0:T(8,128)S(1)} collective-permute-done((f32[32,128]{1,0:T(8,128)S(1)}, f32[32,128]{1,0:T(8,128)S(1)}, u32[]{:S(2)}, u32[]{:S(2)}) %collective-permute-start.3) | collective-permute-done | bytes 16416 | tf_op jit(solution)/shard_map/ppermute | solution.py:794
  25.6 6.6 %middle.1 = (f32[2432,128]{1,0:T(8,128)S(1)}, f32[296,128]{1,0:T(8,128)S(1)}, f32[256,128]{1,0:T(8,128)S(1)}, f32[320,128]{1,0:T(8,128)S(1)}, f32[128,128]{1,0:T...) custom-call(s32[4,4]{1,0:T(4,128)S(1)} %copy-done.1, s32[4,2]{1,0:T(4,128)S(1)} %copy.12.parent, ...), custom_call_target="tpu_custom_call" | custom-call | tf_op jit(solution)/shard_map/middle/pallas_call | solution.py:834
  32.3 0.4 collective-permute-start.4
  32.7 1.1 %collective-permute-done.4.x_in = f32[424,128]{1,0:T(8,128)S(1)} collective-permute-done((f32[424,128]{1,0:T(8,128)S(1)}, f32[424,128]{1,0:T(8,128)S(1)}, u32[]{:S(2)}, u32[]{:S(2)}) %collective-permute-start.4) | collective-permute-done | bytes 217120 | tf_op jit(solution)/shard_map/ppermute | solution.py:794
  33.8 0.1 collective-permute-start.5
  33.9 5.5 %collective-permute-done.5.n_in = f32[456,128]{1,0:T(8,128)S(1)} collective-permute-done((f32[456,128]{1,0:T(8,128)S(1)}, f32[456,128]{1,0:T(8,128)S(1)}, u32[]{:S(2)}, u32[]{:S(2)}) %collective-permute-start.5) | collective-permute-done | bytes 233504 | tf_op jit(solution)/shard_map/ppermute | solution.py:794
  39.4 5.8 %collective-permute-start.6 = (f32[32,128]{1,0:T(8,128)S(1)}, f32[32,128]{1,0:T(8,128)S(1)}, u32[]{:S(2)}, u32[]{:S(2)}) collective-permute-start(f32[32,128]{1,0:T(8,128)S(1)} %slice.38), channel_id=1, source_target_pairs={{0,1},{1,0},{2,3},{3,2},{4,5},{5,4},{6,7},{7,6},{8,9},{9,8},{10,11... | collective-permute-start | bytes 49160 | tf_op jit(solution)/shard_map/ppermute | solution.py:794
  45.2 0.8 %collective-permute-done.6.x_late = f32[32,128]{1,0:T(8,128)S(1)} collective-permute-done((f32[32,128]{1,0:T(8,128)S(1)}, f32[32,128]{1,0:T(8,128)S(1)}, u32[]{:S(2)}, u32[]{:S(2)}) %collective-permute-start.6) | collective-permute-done | bytes 16416 | tf_op jit(solution)/shard_map/ppermute | solution.py:794
  46.0 5.3 %fine_last.1 = (f32[4,19,4096]{2,1,0:T(8,128)S(1)}, f32[304,128]{1,0:T(8,128)S(1)}, f32[1216,128]{1,0:T(8,128)S(1)}) custom-call(s32[4,4]{1,0:T(4,128)S(1)} %copy-done.1, s32[2,6]{1,0:T(2,128)S(1)} %copy-done.2, f32[2432,128]{1,0:T(8,128)S(1)} %get-tuple-element.24.post, s32[128,128]{1,0:T(8,128)S(1)} %get-tuple-element.19.mask, ...), custom_call_target="tpu_custom_call" | custom-call | tf_op jit(solution)/shard_map/fine_last/pallas_call | solution.py:875
  51.3 0.1 collective-permute-start.7
  51.4 5.3 %collective-permute-done.7.two = f32[304,128]{1,0:T(8,128)S(1)} collective-permute-done((f32[304,128]{1,0:T(8,128)S(1)}, f32[304,128]{1,0:T(8,128)S(1)}, u32[]{:S(2)}, u32[]{:S(2)}) %collective-permute-start.7) | collective-permute-done | bytes 155680 | tf_op jit(solution)/shard_map/ppermute | solution.py:794
  56.7 1.3 %collective-permute-start.8 = (f32[608,128]{1,0:T(8,128)S(1)}, f32[608,128]{1,0:T(8,128)S(1)}, u32[]{:S(2)}, u32[]{:S(2)}) collective-permute-start(f32[608,128]{1,0:T(8,128)S(1)} %pad_maximum_fusion.1), channel_id=1, source_target_pairs={{0,1},{1,0},{2,3},{3,2},{4,5},{5,4},{6,7},{7,6},{8,9},{9,8},{10,11... | collective-permute-start | bytes 933896 | tf_op jit(solution)/shard_map/ppermute | solution.py:794
  57.9 1.8 %copy.13 = f32[4,19,4096]{2,0,1:T(4,128)} copy(f32[4,19,4096]{2,1,0:T(8,128)S(1)} %get-tuple-element.34) | data formatting | bytes 2490368
  59.8 0.0 collective-permute-done.8.x_in
  59.8 1.6 %coarse_last.1 = f32[2,19,4096]{2,1,0:T(8,128)S(1)} custom-call(s32[2,4]{1,0:T(2,128)S(1)} %copy-done.3, f32[1216,128]{1,0:T(8,128)S(1)} %get-tuple-element.32.cpassed, f32[304,128]{1,0:T(8,128)S(1)} %get-tuple-element.33.own, f32[304,128]{1,0:T(8,128)S(1)} %collective-permute-done.7.two, f32[608,128]{1,0:T(8,128)S(1)} %collective-permute-done.8.x_in), custom_call_target="tpu_custom_call" | custom-call | tf_op jit(solution)/shard_map/coarse_last/pallas_call | solution.py:913
  61.4 1.3 %copy.14 = f32[2,19,4096]{2,0,1:T(2,128)} copy(f32[2,19,4096]{2,1,0:T(8,128)S(1)} %coarse_last.1) | data formatting | bytes 1245184
  (22 shorter events, 0.1 us)
Async XLA Ops:
  0.6 5.0 %copy-start.5 = (s32[4,2]{0,1:T(2,128)S(1)}, s32[4,2]{0,1:T(2,128)}, u32[]{:S(2)}) copy-start(s32[4,2]{0,1:T(2,128)} %param.11) | copy-start | bytes 100
  0.6 5.1 %copy-start.4 = (f32[4,19,4096]{2,0,1:T(4,128)S(1)}, f32[4,19,4096]{2,0,1:T(4,128)}, u32[]{:S(2)}) copy-start(f32[4,19,4096]{2,0,1:T(4,128)} %param.7) | copy-start | bytes 3735556
  3.4 6.7 %collective-permute-start = (f32[200,128]{1,0:T(8,128)S(1)}, f32[200,128]{1,0:T(8,128)S(1)}, u32[]{:S(2)}, u32[]{:S(2)}) collective-permute-start(f32[200,128]{1,0:T(8,128)S(1)} %get-tuple-element.21.e_own), channel_id=1, source_target_pairs={{0,2},{1,3},{2,0},{3,1},{4,6},{5,7},{6,4},{7,5},{8,10},{9,11},{10,... | collective-permute-start | bytes 307208 | tf_op jit(solution)/shard_map/ppermute | solution.py:794
  5.7 0.8 %copy-start = (s32[4,4096]{1,0:T(4,128)S(1)}, s32[4,4096]{1,0:T(4,128)}, u32[]{:S(2)}) copy-start(s32[4,4096]{1,0:T(4,128)} %solid.1) | copy-start | bytes 196612
  5.7 0.8 %copy-start.1 = (s32[4,4]{1,0:T(4,128)S(1)}, s32[4,4]{1,0:T(4,128)}, u32[]{:S(2)}) copy-start(s32[4,4]{1,0:T(4,128)} %nbr.5) | copy-start | bytes 196
  6.6 19.0 %copy-start.2 = (s32[2,6]{1,0:T(2,128)S(1)}, s32[2,6]{1,0:T(2,128)}, u32[]{:S(2)}) copy-start(s32[2,6]{1,0:T(2,128)} %cnbr.3) | copy-start | bytes 148
  10.2 2.4 %collective-permute-start.1 = (f32[840,128]{1,0:T(8,128)S(1)}, f32[840,128]{1,0:T(8,128)S(1)}, u32[]{:S(2)}, u32[]{:S(2)}) collective-permute-start(f32[840,128]{1,0:T(8,128)S(1)} %pad_maximum_fusion), channel_id=1, source_target_pairs={{0,1},{1,0},{2,3},{3,2},{4,5},{5,4},{6,7},{7,6},{8,9},{9,8},{10,11... | collective-permute-start | bytes 1290248 | tf_op jit(solution)/shard_map/ppermute | solution.py:794
  12.7 5.8 %collective-permute-start.2 = (f32[504,128]{1,0:T(8,128)S(1)}, f32[504,128]{1,0:T(8,128)S(1)}, u32[]{:S(2)}, u32[]{:S(2)}) collective-permute-start(f32[504,128]{1,0:T(8,128)S(1)} %constant_dynamic-update-slice_fusion), channel_id=1, source_target_pairs={{0,127},{1,2},{2,1},{3,4},{4,3},{5,6},{6,5},{7,8},{8,7},{9,10},{10... | collective-permute-start | bytes 774152 | tf_op jit(solution)/shard_map/ppermute | solution.py:794
  18.5 7.1 %collective-permute-start.3 = (f32[32,128]{1,0:T(8,128)S(1)}, f32[32,128]{1,0:T(8,128)S(1)}, u32[]{:S(2)}, u32[]{:S(2)}) collective-permute-start(f32[32,128]{1,0:T(8,128)S(1)} %slice.36), channel_id=1, source_target_pairs={{0,1},{1,0},{2,3},{3,2},{4,5},{5,4},{6,7},{7,6},{8,9},{9,8},{10,11... | collective-permute-start | bytes 49160 | tf_op jit(solution)/shard_map/ppermute | solution.py:794
  32.3 1.6 %collective-permute-start.4 = (f32[424,128]{1,0:T(8,128)S(1)}, f32[424,128]{1,0:T(8,128)S(1)}, u32[]{:S(2)}, u32[]{:S(2)}) collective-permute-start(f32[424,128]{1,0:T(8,128)S(1)} %pad_maximum_fusion.3), channel_id=1, source_target_pairs={{0,1},{1,0},{2,3},{3,2},{4,5},{5,4},{6,7},{7,6},{8,9},{9,8},{10,11... | collective-permute-start | bytes 651272 | tf_op jit(solution)/shard_map/ppermute | solution.py:794
  33.8 5.6 %collective-permute-start.5 = (f32[456,128]{1,0:T(8,128)S(1)}, f32[456,128]{1,0:T(8,128)S(1)}, u32[]{:S(2)}, u32[]{:S(2)}) collective-permute-start(f32[456,128]{1,0:T(8,128)S(1)} %pad_maximum_fusion.2), channel_id=1, source_target_pairs={{0,127},{1,2},{2,1},{3,4},{4,3},{5,6},{6,5},{7,8},{8,7},{9,10},{10... | collective-permute-start | bytes 700424 | tf_op jit(solution)/shard_map/ppermute | solution.py:794
  39.4 6.6 %collective-permute-start.6 = (f32[32,128]{1,0:T(8,128)S(1)}, f32[32,128]{1,0:T(8,128)S(1)}, u32[]{:S(2)}, u32[]{:S(2)}) collective-permute-start(f32[32,128]{1,0:T(8,128)S(1)} %slice.38), channel_id=1, source_target_pairs={{0,1},{1,0},{2,3},{3,2},{4,5},{5,4},{6,7},{7,6},{8,9},{9,8},{10,11... | collective-permute-start | bytes 49160 | tf_op jit(solution)/shard_map/ppermute | solution.py:794
  51.3 5.3 %collective-permute-start.7 = (f32[304,128]{1,0:T(8,128)S(1)}, f32[304,128]{1,0:T(8,128)S(1)}, u32[]{:S(2)}, u32[]{:S(2)}) collective-permute-start(f32[304,128]{1,0:T(8,128)S(1)} %get-tuple-element.33.own), channel_id=1, source_target_pairs={{0,2},{1,3},{2,0},{3,1},{4,6},{5,7},{6,4},{7,5},{8,10},{9,11},{10,... | collective-permute-start | bytes 466952 | tf_op jit(solution)/shard_map/ppermute | solution.py:794
  56.7 3.1 %collective-permute-start.8 = (f32[608,128]{1,0:T(8,128)S(1)}, f32[608,128]{1,0:T(8,128)S(1)}, u32[]{:S(2)}, u32[]{:S(2)}) collective-permute-start(f32[608,128]{1,0:T(8,128)S(1)} %pad_maximum_fusion.1), channel_id=1, source_target_pairs={{0,1},{1,0},{2,3},{3,2},{4,5},{5,4},{6,7},{7,6},{8,9},{9,8},{10,11... | collective-permute-start | bytes 933896 | tf_op jit(solution)/shard_map/ppermute | solution.py:794
  57.9 1.8 %copy-start.3 = (s32[2,4]{1,0:T(2,128)S(1)}, s32[2,4]{1,0:T(2,128)}, u32[]{:S(2)}) copy-start(s32[2,4]{1,0:T(2,128)} %children.1) | copy-start | bytes 100

commit v2 on v1

v2 whole, which is shorter than its diff:
```python
import jax
import jax.numpy as jnp
from jax import lax
from jax.experimental import pallas as pl
from jax.experimental.pallas import tpu as pltpu
from jax.sharding import PartitionSpec as P

AXES = ("gx", "gy")
VELOCITIES = (
    (0, 0, 0),
    (1, 0, 0),
    (-1, 0, 0),
    (0, 1, 0),
    (0, -1, 0),
    (0, 0, 1),
    (0, 0, -1),
    (1, 1, 0),
    (-1, -1, 0),
    (1, -1, 0),
    (-1, 1, 0),
    (1, 0, 1),
    (-1, 0, -1),
    (1, 0, -1),
    (-1, 0, 1),
    (0, 1, 1),
    (0, -1, -1),
    (0, 1, -1),
    (0, -1, 1),
)
WEIGHTS = (1.0 / 3.0,) + (1.0 / 18.0,) * 6 + (1.0 / 36.0,) * 12
OPPOSITE = (0, 2, 1, 4, 3, 6, 5, 8, 7, 10, 9, 12, 11, 14, 13, 16, 15, 18, 17)
OMEGA_COARSE = 1.6
OMEGA_FINE = 1.0 / (2.0 * (1.0 / 1.6 - 0.5) + 0.5)

XP = (1, 7, 9, 11, 13)
XM = (2, 8, 10, 12, 14)
YP = (3, 7, 10, 15, 17)
YM = (4, 8, 9, 16, 18)
ZP = (5, 11, 14, 15, 18)
ZM = (6, 12, 13, 16, 17)
YP1, YM1 = (3, 15, 17), (4, 16, 18)
YP2, YM2 = (7, 10), (8, 9)
ZP2, ZM2 = (11, 14, 15, 18), (12, 13, 16, 17)

R = 32
BLOCK = 19 * R
FB, CB = 4, 2
ZS = FB * 64
EDGES = ZS + R
META = EDGES + R
F_ROWS = META + 8
F2_ROWS = META
E_BLOCK = 96
EC_AT = CB * E_BLOCK
E_ROWS = EC_AT + 8
C_ROWS = FB * 64 + 16
K_ROWS = 2 * 19 * 8
EZ_BLOCK = 80
HALO = 3 * EDGES + FB * 64
X_E = F_ROWS
X_E2 = X_E + E_ROWS
N_EDGE = F_ROWS
N_EC = N_EDGE + R
M_PARENT, M_CNBR, M_CHILD = 4, 8, 16


def iotas(rows=R):
    row = lax.broadcasted_iota(jnp.int32, (rows, 128), 0)
    lane = lax.broadcasted_iota(jnp.int32, (rows, 128), 1)
    return row, lane


def roll(a, shift, axis):
    if isinstance(shift, int):
        shift = shift % a.shape[axis]
        if shift == 0:
            return a
    return pltpu.roll(a, shift, axis)


def at(ref, start, size=R):
    if not isinstance(start, int):
        start = pl.multiple_of(start, 8)
    return ref[pl.ds(start, size), :]


def put(ref, start, value):
    if not isinstance(start, int):
        start = pl.multiple_of(start, 8)
    ref[pl.ds(start, value.shape[0]), :] = value


def rows_in(src, dst, blocks):
    def body(i, carry):
        for r in range(R):
            dst[pl.ds(i * R + r, blocks, stride=BLOCK), :] = src[i, :, 128 * r : 128 * r + 128]
        return carry

    lax.fori_loop(0, 19, body, 0)


def rows_out(src, dst, blocks):
    def body(i, carry):
        for r in range(R):
            dst[i, :, 128 * r : 128 * r + 128] = src[pl.ds(i * R + r, blocks, stride=BLOCK), :]
        return carry

    lax.fori_loop(0, 19, body, 0)


def total(terms):
    while len(terms) > 1:
        pairs = [terms[k] + terms[k + 1] for k in range(0, len(terms) - 1, 2)]
        terms = pairs + terms[len(terms) - len(terms) % 2 :]
    return terms[0]


def collide(f, rate):
    rho = total(f)
    mom = []
    for axis in range(3):
        plus = [f[i] for i in range(19) if VELOCITIES[i][axis] == 1]
        minus = [f[i] for i in range(19) if VELOCITIES[i][axis] == -1]
        mom.append(total(plus) - total(minus))
    inv = 1.0 / rho
    u = [m * inv for m in mom]
    base = 1.0 - 1.5 * (u[0] * u[0] + u[1] * u[1] + u[2] * u[2])
    scaled = {w: (rate * w) * rho for w in sorted(set(WEIGHTS))}
    keep = 1.0 - rate
    out = [None] * 19
    out[0] = keep * f[0] + scaled[WEIGHTS[0]] * base
    for i in range(1, 19, 2):
        proj = None
        for axis in range(3):
            c = VELOCITIES[i][axis]
            if c:
                term = u[axis]
                if proj is None:
                    proj = term if c > 0 else -term
                else:
                    proj = proj + term if c > 0 else proj - term
        even = base + 4.5 * (proj * proj)
        odd = 3.0 * proj
        w = scaled[WEIGHTS[i]]
        out[i] = keep * f[i] + w * (even + odd)
        out[i + 1] = keep * f[i + 1] + w * (even - odd)
    return out


def collide_rows(src, src_base, dst, dst_base, rate, mask, mask_base, corner=None):
    def body(v, carry):
        f = [at(src, src_base + i * R + v * 16, 16) for i in range(19)]
        if corner is not None:
            edge = at(corner, v * 16, 16)
            f = [with_corners(f[i], i, edge) for i in range(19)]
        post = collide(f, rate)
        if mask is not None:
            solid = (at(mask, mask_base + v * 16, 16) & 1) > 0
            post = [jnp.where(solid, f[i], post[i]) for i in range(19)]
        for i in range(19):
            put(dst, dst_base + i * R + v * 16, post[i])
        return carry

    lax.fori_loop(0, 2, body, 0)


def pack_x(get, packed):
    _, lane = iotas()
    x = lane & 15
    for j in range(5):
        packed = jnp.where(x == j, roll(get(XP[j]), j - 15, 1), packed)
        packed = jnp.where(x == 5 + j, roll(get(XM[j]), 5 + j, 1), packed)
    return packed


def swap_rows(a):
    row, _ = iotas()
    return jnp.where((row & 1) == 0, roll(a, -1, 0), roll(a, 1, 0))


def pack_y(get, plus, minus, first, rest):
    row, lane = iotas()
    upper = (row & 1) == 1
    packed = jnp.zeros((R, 128), jnp.float32)
    for k in range(len(plus)):
        p = first + k
        one = jnp.where(upper, roll(get(plus[k]), 16 * p - 112, 1), roll(get(minus[k]), 16 * p, 1))
        packed = jnp.where((lane >> 4) == p, one, packed)
    packed = swap_rows(packed)
    if rest is None:
        return packed
    group = lane >> 4
    return jnp.where((group >= first) & (group < first + len(plus)), packed, rest)


def pack_edges(get):
    row, lane = iotas()
    upper = (row & 1) == 1
    first = jnp.where(upper, roll(get(7), -127, 1), get(8))
    second = jnp.where(upper, roll(get(10), 1 - 112, 1), roll(get(9), 1 - 15, 1))
    return swap_rows(jnp.where(lane == 0, first, second))


def move_x(a, cx, halo):
    _, lane = iotas()
    x = lane & 15
    if cx == 1:
        return jnp.where(x == 0, halo, roll(a, 1, 1))
    return jnp.where(x == 15, halo, roll(a, -1, 1))


def move_y(a, cy, halo):
    row, lane = iotas()
    upper = (row & 1) == 1
    if cy == 1:
        near = roll(a, 16, 1)
        return jnp.where(lane < 16, jnp.where(upper, roll(near, 1, 0), halo), near)
    near = roll(a, -16, 1)
    return jnp.where(lane >= 112, jnp.where(upper, halo, roll(near, -1, 0)), near)


def move_z(a, cz, halo8):
    row, _ = iotas(8)
    if cz == 1:
        near = roll(a, 2, 0)
        return jnp.concatenate([jnp.where(row < 2, halo8, near[:8]), near[8:]], axis=0)
    near = roll(a, -2, 0)
    return jnp.concatenate([near[:24], jnp.where(row >= 6, halo8, near[24:])], axis=0)


def send_faces(get, out, coarse, b):
    put(out, b * 64, pack_x(get, at(coarse, b * 64)))
    put(out, b * 64 + R, pack_y(get, YP, YM, 0, at(coarse, b * 64 + R)))
    _, lane = iotas()
    edges = roll(pack_edges(get), 2 * b, 1)
    put(out, EDGES, jnp.where((lane >> 1) == b, edges, at(out, EDGES)))


def place():
    device = lax.axis_index("gx") * lax.axis_size("gy") + lax.axis_index("gy")
    sign = 1 - 2 * (device & 1)
    return device, sign


def coarse_first_kernel(
    pop_hbm,
    fine_hbm,
    solid_hbm,
    nbr_hbm,
    parent_hbm,
    cnbr_hbm,
    children_hbm,
    post,
    e_out,
    c_out,
    fine_out,
    solid_out,
    meta_out,
    pop,
    nbr,
    parent,
    cnbr,
    children,
    raw,
    sem,
):
    copies = [
        pltpu.make_async_copy(src, dst, sem.at[k])
        for k, (src, dst) in enumerate(
            (
                (pop_hbm, pop),
                (nbr_hbm, nbr),
                (parent_hbm, parent),
                (cnbr_hbm, cnbr),
                (children_hbm, children),
                (fine_hbm, fine_out),
                (solid_hbm, solid_out),
            )
        )
    ]
    for c in copies:
        c.start()
    copies[0].wait()
    rows_in(pop, raw, CB)
    _, lane = iotas(16)
    _, lane8 = iotas(8)
    x16 = lane & 15
    corner = jnp.zeros((8, 128), jnp.float32)
    for c in range(CB):
        base = c * BLOCK
        half = lambda i: at(raw, base + i * R, 16)
        for qx in range(2):
            packed = jnp.zeros((16, 128), jnp.float32)
            for j in range(5):
                packed = jnp.where(x16 == j, roll(half(XP[j]), j - 8 * qx, 1), packed)
                packed = jnp.where(x16 == 5 + j, roll(half(XM[j]), 5 + j - 8 * qx - 7, 1), packed)
            put(e_out, c * E_BLOCK + qx * 16, packed)
        low = jnp.zeros((16, 128), jnp.float32)
        high = jnp.zeros((16, 128), jnp.float32)
        for p in range(5):
            low = jnp.where((lane >> 4) == p, roll(half(YP[p]), 16 * p, 1), low)
            high = jnp.where((lane >> 4) == p, roll(half(YM[p]), 16 * p - 112, 1), high)
        put(e_out, c * E_BLOCK + 32, low)
        put(e_out, c * E_BLOCK + 48, high)
        put(e_out, c * E_BLOCK + 64, jnp.zeros((R, 128), jnp.float32))
        for k in range(5):
            e_out[pl.ds(c * E_BLOCK + 64 + 2 * k, 2), :] = raw[pl.ds(base + ZP[k] * R, 2), :]
            e_out[pl.ds(c * E_BLOCK + 74 + 2 * k, 2), :] = raw[pl.ds(base + ZM[k] * R + 14, 2), :]
        for q in range(4):
            for e, (i, yq, xq) in enumerate(((7, 7, 0), (10, 7, 7), (9, 0, 0), (8, 0, 7))):
                to = (c * 4 + q) * 4 + e
                rows = raw[pl.ds(base + i * R + q // 2, 8, stride=2), :]
                rows = roll(rows, to - (yq * 16 + 8 * (q % 2) + xq), 1)
                corner = jnp.where(lane8 == to, rows, corner)
    put(e_out, EC_AT, corner)
    row8, _ = iotas(8)
    for c in range(CB):
        base = c * BLOCK
        collide_rows(raw, base, post, base, OMEGA_COARSE, None, 0)
        get = lambda i: at(post, base + i * R)
        x_wide = lax.broadcasted_iota(jnp.int32, (R, 128), 1) & 15
        ahead = jnp.zeros((R, 128), jnp.float32)
        back = jnp.zeros((R, 128), jnp.float32)
        for j in range(5):
            ahead = jnp.where(x_wide == 10 + j, roll(get(XP[j]), 10 + j - 15, 1), ahead)
            back = jnp.where(x_wide == 10 + j, roll(get(XM[j]), 10 + j, 1), back)
        put(c_out, c * 128, ahead)
        put(c_out, c * 128 + 64, back)
        put(c_out, c * 64 + R, pack_y(get, YP1, YM1, 5, None))
        put(c_out, (c + 2) * 64 + R, jnp.zeros((R, 128), jnp.float32))
        top = roll(at(post, base + 5 * R + 24, 8), 2, 0)
        bottom = roll(at(post, base + 6 * R, 8), 6, 0)
        put(c_out, FB * 64 + 8 * c, jnp.where(row8 < 2, top, bottom))
    for c in copies[1:]:
        c.wait()
    meta = jnp.zeros((8, 128), jnp.float32)
    entries = []
    for b in range(FB):
        entries += [(b, k, nbr[b, k]) for k in range(4)]
        entries += [(b, 4 + k, parent[k, b]) for k in range(2)]
    for c in range(CB):
        entries += [(c, M_CNBR + k, cnbr[c, k]) for k in range(6)]
        entries += [(c, M_CHILD + k, children[c, k]) for k in range(4)]
    for b, k, value in entries:
        meta = jnp.where((row8 == b) & (lane8 == k), value.astype(jnp.float32), meta)
    put(meta_out, 0, meta)


def fine_first_kernel(meta, pop, solid, coarse, post, mask, f_out, raw, sol):
    rows_in(pop, raw, FB)
    for r in range(R):
        sol[pl.ds(r, FB, stride=R), :] = solid[:, 128 * r : 128 * r + 128]
    put(f_out, EDGES, jnp.zeros((R, 128), jnp.float32))
    put(f_out, ZS, coarse[pl.ds(FB * 64, 16), :])
    put(f_out, ZS + 16, jnp.zeros((16, 128), jnp.float32))

    def body(b, carry):
        s = jnp.where(at(sol, b * R) > 0, 1, 0)
        bits = s
        for i in range(1, 19):
            cx, cy, cz = VELOCITIES[i]
            m = s
            if cx:
                m = roll(m, cx, 1)
            if cy:
                m = move_y(m, cy, jnp.zeros_like(m))
            if cz:
                m = roll(m, 2 * cz, 0)
            bits = bits | (m << i)
        put(mask, b * R, bits)
        base = b * BLOCK
        collide_rows(raw, base, post, base, OMEGA_FINE, mask, b * R)
        send_faces(lambda i: at(post, base + i * R), f_out, coarse, b)
        return carry

    lax.fori_loop(0, FB, body, 0)
    put(f_out, META, meta[...])


def number(meta, row, column):
    return meta[row, column].astype(jnp.int32)


def onehot(rows, cols, source):
    row = lax.broadcasted_iota(jnp.int32, (rows, cols), 0)
    col = lax.broadcasted_iota(jnp.int32, (rows, cols), 1)
    return jnp.where(row == source(col), 1.0, 0.0).astype(jnp.float32)


def exact_dot(a, b):
    return jnp.dot(a, b, preferred_element_type=jnp.float32, precision=lax.Precision.HIGHEST)


def expand(meta, device, gathered, halo, ez):
    _, lane = iotas(16)
    row, _ = iotas(16)
    x = lane & 15
    spread_x = onehot(
        128, 256, lambda m: ((m >> 7) * 4 + ((m & 127) >> 5)) * 16 + (m & 15)
    )

    def body(b, carry):
        p, q = number(meta, b, M_PARENT), number(meta, b, M_PARENT + 1)
        qy, qx = q >> 1, q & 1
        base = ((p >> 1) ^ device) * E_ROWS + (p & 1) * E_BLOCK
        home = b * 64
        ex = exact_dot(gathered[pl.ds(base + qx * 16 + qy, 8, stride=2), :], spread_x)
        spread_y = onehot(128, 128, lambda m: (m >> 4) * 16 + 8 * qx + ((m & 15) >> 1))
        ey0 = exact_dot(gathered[pl.ds(base + 32 + qy, 8, stride=2), :], spread_y)
        ey1 = exact_dot(gathered[pl.ds(base + 48 + qy, 8, stride=2), :], spread_y)
        for k in range(2):
            halo[pl.ds(home + 2 * k, 8, stride=4), :] = ex[:, :128]
            halo[pl.ds(home + 2 * k + 1, 8, stride=4), :] = ex[:, 128:]
            halo[pl.ds(home + R + 2 * k, 8, stride=4), :] = ey0
            halo[pl.ds(home + R + 2 * k + 1, 8, stride=4), :] = ey1
        spread_z = onehot(
            128,
            256,
            lambda m: ((m >> 7) * 4 + ((m & 127) >> 5)) * 16 + 8 * qx + ((m & 15) >> 1),
        )
        ezs = exact_dot(gathered[pl.ds(base + 64 + qy, 16, stride=2), :], spread_z)
        a0, a1 = ezs[:, :128], ezs[:, 128:]
        moves = {}
        moves[0, 0] = (a0, a1)
        moves[1, 0] = tuple(jnp.where(x == 0, a, roll(a, 1, 1)) for a in (a0, a1))
        moves[-1, 0] = tuple(jnp.where(x == 15, a, roll(a, -1, 1)) for a in (a0, a1))
        moves[0, 1] = (
            jnp.where(lane < 16, a0, roll(a0, 16, 1)),
            jnp.where(lane < 16, roll(a0, 16, 1), roll(a1, 16, 1)),
        )
        moves[0, -1] = (
            jnp.where(lane >= 112, roll(a1, -16, 1), roll(a0, -16, 1)),
            jnp.where(lane >= 112, a1, roll(a1, -16, 1)),
        )
        out = [a0, a1]
        for k, i in enumerate(ZP + ZM):
            moved = moves[VELOCITIES[i][:2]]
            out = [jnp.where(row == k, moved[h], out[h]) for h in range(2)]
        for h in range(2):
            for k in range(5):
                ez[pl.ds(b * EZ_BLOCK + 8 * k + h, 1), :] = out[h][k : k + 1]
                ez[pl.ds(b * EZ_BLOCK + 40 + 8 * k + 6 + h, 1), :] = out[h][5 + k : 6 + k]
        return carry

    lax.fori_loop(0, FB, body, 0)


def gather_halo(own, x_in, n_in, e_halo, halo):
    put(halo, 3 * EDGES, e_halo[...])
    for k, ref in enumerate((n_in, own, x_in)):
        put(halo, k * EDGES, ref[0:EDGES, :])


def gather_edges(own, x_in, n_in, x_late, relayed, edges):
    for k, ref in enumerate((n_in, own, x_in)):
        put(edges, (k + 1) * R, ref[EDGES : EDGES + R, :])
    put(edges, 0, n_in[pl.ds(relayed, R), :])
    put(edges, 4 * R, x_late[...])


def corners(meta_n, meta_own, meta_x, device, sign, e_halo, edges, fixed, b):
    row, lane = iotas()
    upper = (row & 1) == 1
    result = jnp.zeros((R, 128), jnp.float32)
    for side in range(2):
        n = number(meta_own, b, 2 + side)
        safe = jnp.maximum(n, 0)
        which = ((safe >> 2) - device) * sign + 1
        which = jnp.clip(which, 0, 2)
        row_n = safe & 3
        for end in range(2):
            i = ((7, 10), (9, 8))[side][end]
            p = (YP, YM)[side].index(i)
            edge_col = ((0, 1), (1, 0))[side][end]
            to = 112 * side + 15 * end
            m = jnp.where(
                which == 0,
                meta_n[row_n, end],
                jnp.where(which == 1, meta_own[row_n, end], meta_x[row_n, end]),
            ).astype(jnp.int32)
            m_safe = jnp.maximum(m, 0)
            slot = jnp.clip(((m_safe >> 2) - device) * sign + 2, 0, 4)
            shift = (to - (2 * (m_safe & 3) + edge_col)) & 127
            sent = roll(at(edges, slot * R), shift, 1)
            own = roll(at(e_halo, b * 64 + R), to - (16 * p + 15 * end), 1)
            value = jnp.where(n < 0, own, jnp.where(m >= 0, sent, at(fixed, b * R)))
            here = (lane == to) & (upper if side else jnp.logical_not(upper))
            result = jnp.where(here, value, result)
    return result


def fixed_corners(meta_n, meta_own, meta_x, device, sign, group, from_n, fixed, spare):
    _, lane = iotas()
    npart = device - sign

    def body(b, carry):
        result = jnp.zeros((R, 128), jnp.float32)
        for side in range(2):
            safe = jnp.maximum(number(meta_own, b, 2 + side), 0)
            which = jnp.clip(((safe >> 2) - device) * sign + 1, 0, 2)
            row_n = safe & 3
            pq = [
                jnp.where(
                    which == 0,
                    meta_n[row_n, 4 + k],
                    jnp.where(which == 1, meta_own[row_n, 4 + k], meta_x[row_n, 4 + k]),
                ).astype(jnp.int32)
                for k in range(2)
            ]
            p, q = pq
            near = ((p >> 1) ^ device) & 3
            far = ((p >> 1) ^ npart) & 3
            quad = jnp.where(
                which == 0, at(from_n, far * 8, 8), at(group, near * 8, 8)
            )
            for k in range(4):
                spare[pl.ds(k, 8, stride=4), :] = quad
            rows = spare[...]
            for end in range(2):
                to = 112 * side + 15 * end
                source = ((p & 1) * 4 + q) * 4 + 2 * side + end
                result = jnp.where(lane == to, roll(rows, (to - source) & 127, 1), result)
        put(fixed, b * R, result)
        return carry

    lax.fori_loop(0, FB, body, 0)


def stream_fine(meta, device, sign, post, mask, halo, ez, dst, dst_base, b):
    base = b * BLOCK
    bits = at(mask, b * R)
    faces = []
    for k in range(4):
        n = number(meta, b, k)
        safe = jnp.maximum(n, 0)
        which = jnp.clip(((safe >> 2) - device) * sign + 1, 0, 2)
        start = jnp.where(n >= 0, which * EDGES + (safe & 3) * 64, 3 * EDGES + b * 64)
        faces.append(at(halo, start + (R if k >= 2 else 0)))
    solid = (bits & 1) > 0
    for i in range(19):
        cx, cy, cz = VELOCITIES[i]
        a = at(post, base + i * R)
        if i == 0:
            put(dst, dst_base, a)
            continue
        g = a
        if cx == 1:
            g = move_x(g, 1, roll(faces[0], -XP.index(i), 1))
        elif cx == -1:
            g = move_x(g, -1, roll(faces[1], 10 - XM.index(i), 1))
        if cy:
            first = 112 * (cy == -1)
            p = (YP if cy == 1 else YM).index(i)
            side = roll(faces[2 if cy == 1 else 3], first - 16 * p + cx, 1)
            g = move_y(g, cy, side)
        if cz:
            k = ZP.index(i) if cz == 1 else 5 + ZM.index(i)
            g = move_z(g, cz, at(ez, b * EZ_BLOCK + 8 * k, 8))
        from_wall = (bits & (1 << i)) > 0
        g = jnp.where(from_wall, at(post, base + OPPOSITE[i] * R), g)
        put(dst, dst_base + i * R, jnp.where(solid, a, g))


def with_corners(cells, i, corner):
    if i not in (7, 8, 9, 10):
        return cells
    row, lane = iotas(cells.shape[0])
    column, upper = {7: (0, 0), 10: (15, 0), 9: (112, 1), 8: (127, 1)}[i]
    return jnp.where((lane == column) & ((row & 1) == upper), corner, cells)


def fetch_meta(pairs, sem):
    copies = [
        pltpu.make_async_copy(ref.at[pl.ds(META, 8)], dst, sem.at[k])
        for k, (ref, dst) in enumerate(pairs)
    ]
    for c in copies:
        c.start()
    return copies


def expand_kernel(f_own, e_own, e_two, x_in, e_halo, ez, gathered, meta, sem):
    device, _ = place()
    (fetch,) = fetch_meta(((f_own, meta),), sem)
    put(gathered, 0, e_own[...])
    put(gathered, E_ROWS, x_in[X_E : X_E + E_ROWS, :])
    put(gathered, 2 * E_ROWS, e_two[...])
    put(gathered, 3 * E_ROWS, x_in[X_E2 : X_E2 + E_ROWS, :])
    fetch.wait()
    expand(meta, device, gathered, e_halo, ez)


def coarse_source(index, device, sign):
    safe = jnp.maximum(index, 0)
    which = jnp.clip(((safe >> 1) - device) * sign + 1, 0, 2)
    return which, safe & 1


def first_stream_kernel(
    post,
    mask,
    f_own,
    e_own,
    e_two,
    x_in,
    n_in,
    cpost,
    e_halo,
    ez,
    new,
    fixed,
    cmid,
    c_out,
    group,
    halo,
    spare,
    meta_n,
    meta_own,
    meta_x,
    sem,
):
    device, sign = place()
    copies = fetch_meta(((n_in, meta_n), (f_own, meta_own), (x_in, meta_x)), sem)
    put(group, 0, e_own[EC_AT:E_ROWS, :])
    put(group, 8, x_in[X_E + EC_AT : X_E + E_ROWS, :])
    put(group, 16, e_two[EC_AT:E_ROWS, :])
    put(group, 24, x_in[X_E2 + EC_AT : X_E2 + E_ROWS, :])
    gather_halo(f_own, x_in, n_in, e_halo, halo)
    for k in range(FB):
        put(c_out, k * 64, jnp.zeros((64, 128), jnp.float32))
    for c in copies:
        c.wait()

    row8, _ = iotas(8)

    def coarse_body(c, carry):
        base = c * BLOCK
        has, which, slot = [], [], []
        for k in range(6):
            neighbour = number(meta_own, c, M_CNBR + k)
            w, s = coarse_source(neighbour, device, sign)
            has.append(neighbour >= 0)
            which.append(w * EDGES)
            slot.append(s)
        faces = [at(halo, which[k] + slot[k] * 128 + 64 * k) for k in range(2)]
        faces += [at(halo, which[k] + slot[k] * 64 + R) for k in (2, 3)]
        zs = [at(halo, which[k] + ZS + slot[k] * 8, 8) for k in (4, 5)]
        put(cmid, base, at(cpost, base))
        for i in range(1, 19):
            cx, cy, cz = VELOCITIES[i]
            a = at(cpost, base + i * R)
            if cx == 1:
                g = move_x(a, 1, jnp.where(has[0], roll(faces[0], -10 - XP.index(i), 1), a))
            elif cx == -1:
                g = move_x(a, -1, jnp.where(has[1], roll(faces[1], 5 - XM.index(i), 1), a))
            elif cy == 1:
                side = roll(faces[2], -16 * (5 + YP1.index(i)), 1)
                g = move_y(a, 1, jnp.where(has[2], side, a))
            elif cy == -1:
                side = roll(faces[3], 112 - 16 * (5 + YM1.index(i)), 1)
                g = move_y(a, -1, jnp.where(has[3], side, a))
            elif cz == 1:
                g = move_z(a, 1, jnp.where(has[4], zs[0], a[:8]))
            else:
                g = move_z(a, -1, jnp.where(has[5], zs[1], a[24:]))
            put(cmid, base + i * R, g)
        get = lambda i: at(cmid, base + i * R)
        put(c_out, c * 64 + R, pack_y(get, YP2, YM2, 5, None))
        for k in (0, 2):
            layers = None
            for h in range(2):
                top = roll(at(cmid, base + ZP2[k + h] * R + 24, 8), 2 + 2 * h, 0)
                bottom = roll(at(cmid, base + ZM2[k + h] * R, 8), 6 - 2 * h, 0)
                both = jnp.where(row8 < 4, top, bottom)
                layers = both if h == 0 else jnp.where((row8 < 2) | (row8 >= 6), layers, both)
            put(c_out, FB * 64 + c * 16 + 4 * k, layers)
        return carry

    lax.fori_loop(0, CB, coarse_body, 0)
    fixed_corners(
        meta_n,
        meta_own,
        meta_x,
        device,
        sign,
        group,
        n_in.at[pl.ds(N_EC, 32)],
        fixed,
        spare,
    )

    def body(b, carry):
        stream_fine(meta_own, device, sign, post, mask, halo, ez, new, b * BLOCK, b)
        return carry

    lax.fori_loop(0, FB, body, 0)


def second_collision_kernel(
    new,
    mask,
    f_own,
    x_in,
    n_in,
    x_late,
    e_halo,
    fixed,
    coarse,
    post,
    f_out,
    spot,
    edges,
    meta_n,
    meta_own,
    meta_x,
    sem,
):
    device, sign = place()
    copies = fetch_meta(((n_in, meta_n), (f_own, meta_own), (x_in, meta_x)), sem)
    gather_edges(f_own, x_in, n_in, x_late, N_EDGE, edges)
    put(f_out, EDGES, jnp.zeros((R, 128), jnp.float32))
    put(f_out, ZS, coarse[pl.ds(FB * 64, R), :])
    for c in copies:
        c.wait()

    def body(b, carry):
        base = b * BLOCK
        spot[...] = corners(meta_n, meta_own, meta_x, device, sign, e_halo, edges, fixed, b)
        collide_rows(new, base, post, base, OMEGA_FINE, mask, b * R, spot)
        send_faces(lambda i: at(post, base + i * R), f_out, coarse, b)
        return carry

    lax.fori_loop(0, FB, body, 0)


def second_stream_kernel(
    post, mask, f_own, x_in, n_in, e_halo, ez, f_first, new, halo, meta, sem
):
    device, sign = place()
    (fetch,) = fetch_meta(((f_first, meta),), sem)
    gather_halo(f_own, x_in, n_in, e_halo, halo)
    fetch.wait()

    def body(b, carry):
        stream_fine(meta, device, sign, post, mask, halo, ez, new, b * BLOCK, b)
        return carry

    lax.fori_loop(0, FB, body, 0)


def coarsen_kernel(
    new_in,
    f_own,
    x_in,
    n_in,
    x_late,
    e_halo,
    fixed,
    f_first,
    x_first,
    n_first,
    new,
    means,
    edges,
    meta_n,
    meta_own,
    meta_x,
    sem,
):
    device, sign = place()
    copies = fetch_meta(((n_first, meta_n), (f_first, meta_own), (x_first, meta_x)), sem)
    gather_edges(f_own, x_in, n_in, x_late, F2_ROWS, edges)
    for c in copies:
        c.wait()

    def body(b, carry):
        corner = corners(meta_n, meta_own, meta_x, device, sign, e_halo, edges, fixed, b)
        for i in range(19):
            start = b * BLOCK + i * R
            put(new, start, with_corners(at(new_in, start), i, corner))
        return carry

    lax.fori_loop(0, FB, body, 0)

    row = lax.broadcasted_iota(jnp.int32, (128, 128), 0)
    col = lax.broadcasted_iota(jnp.int32, (128, 128), 1)
    target = lambda yh, h: (yh * 4 + (row >> 5)) * 16 + ((row & 15) >> 1) + 8 * h
    mats = [
        [jnp.where(col == target(yh, h), 0.125, 0.0).astype(jnp.float32) for yh in range(2)]
        for h in range(2)
    ]
    rows = 19 * 8
    for pair in range(2):
        total = None
        for h in range(2):
            b = 2 * pair + h
            for yh in range(2):
                z0 = new[pl.ds(b * BLOCK + yh, rows, stride=4), :]
                z1 = new[pl.ds(b * BLOCK + 2 + yh, rows, stride=4), :]
                part = exact_dot(z0 + z1, mats[h][yh])
                total = part if total is None else total + part
        put(means, pair * rows, total)


def tail_kernel(
    f_first, new, f_own, x_in, n_in, cmid, fine_out, cpassed, halo, meta_own, sem
):
    device, sign = place()
    (fetch,) = fetch_meta(((f_first, meta_own),), sem)
    rows_out(new, fine_out, FB)
    for k, ref in enumerate((n_in, f_own, x_in)):
        put(halo, k * EDGES, ref[0:EDGES, :])
    fetch.wait()

    def coarse_body(c, carry):
        base = c * BLOCK
        has, which, slot = [], [], []
        for k in range(6):
            neighbour = number(meta_own, c, M_CNBR + k)
            w, s = coarse_source(neighbour, device, sign)
            has.append(neighbour >= 0)
            which.append(w * EDGES)
            slot.append(s)
        faces = [at(halo, which[k] + slot[k] * 64 + R) for k in (2, 3)]

        def layer(k, n, back):
            side = at(halo, which[k] + ZS + slot[k] * 16 + 8 * (n // 2), 8)
            return roll(side, (2 if back else -2) * (n & 1), 0)

        for i in range(19):
            a = at(cmid, base + i * R)
            g = a
            if i in YP2:
                side = roll(faces[0], -16 * (5 + YP2.index(i)), 1)
                g = move_y(a, 1, jnp.where(has[2], side, a))
            elif i in YM2:
                side = roll(faces[1], 112 - 16 * (5 + YM2.index(i)), 1)
                g = move_y(a, -1, jnp.where(has[3], side, a))
            elif i in ZP2:
                g = move_z(a, 1, jnp.where(has[4], layer(4, ZP2.index(i), False), a[:8]))
            elif i in ZM2:
                g = move_z(a, -1, jnp.where(has[5], layer(5, ZM2.index(i), True), a[24:]))
            put(cpassed, base + i * R, g)
        return carry

    lax.fori_loop(0, CB, coarse_body, 0)


def coarse_last_kernel(
    f_first, cpassed, own, two, x_in, coarse_out, merged, gathered, meta, sem
):
    device, _ = place()
    (fetch,) = fetch_meta(((f_first, meta),), sem)
    put(gathered, 0, own[...])
    put(gathered, K_ROWS, x_in[0:K_ROWS, :])
    put(gathered, 2 * K_ROWS, two[...])
    put(gathered, 3 * K_ROWS, x_in[K_ROWS : 2 * K_ROWS, :])
    merged[...] = cpassed[...]
    fetch.wait()
    _, lane = iotas(8)
    x_half = (lane >> 3) & 1

    def body(step, carry):
        c, q = step >> 2, step & 3
        qy, qx = q >> 1, q & 1
        child = number(meta, c, M_CHILD + q)

        @pl.when(child >= 0)
        def _():
            slot = ((child >> 2) ^ device) & 3
            start = slot * K_ROWS + ((child & 3) >> 1) * (19 * 8)
            shift = (8 * (qx - (child & 1))) & 127
            mine = x_half == qx
            for i in range(19):
                value = roll(at(gathered, start + 8 * i, 8), shift, 1)
                rows = pl.ds(c * BLOCK + i * R + qy, 8, stride=2)
                merged[rows, :] = jnp.where(mine, value, merged[rows, :])

        return carry

    lax.fori_loop(0, CB * 4, body, 0)
    rows_out(merged, coarse_out, CB)


VMEM = pl.BlockSpec(memory_space=pltpu.VMEM)
HBM = pl.BlockSpec(memory_space=pltpu.HBM)


def rows_of(n, dtype=jnp.float32):
    return jax.ShapeDtypeStruct((n, 128), dtype)


def scratch(n, dtype=jnp.float32):
    return pltpu.VMEM((n, 128), dtype)


def call(kernel, name, specs, outs, scratches, flops=1 << 20):
    return pl.pallas_call(
        kernel,
        name=name,
        in_specs=specs,
        out_specs=[VMEM] * len(outs),
        out_shape=outs,
        scratch_shapes=scratches,
        cost_estimate=pl.CostEstimate(flops=flops, bytes_accessed=4 << 20, transcendentals=0),
        compiler_params=pltpu.CompilerParams(vmem_limit_bytes=32 * 1024 * 1024),
    )


def meta_scratch(n=3):
    return [pltpu.SMEM((8, 128), jnp.float32)] * n + [pltpu.SemaphoreType.DMA((n,))]


def exchange(rows, devices, partner):
    return lax.ppermute(rows, AXES, [(i, partner(i)) for i in range(devices)])


def on_device(fine_pop, coarse_pop, fine_nbr, coarse_nbr, parent, children, solid):
    devices = lax.axis_size(AXES)
    by_one = lambda a: exchange(a, devices, lambda i: i ^ 1)
    by_two = lambda a: exchange(a, devices, lambda i: i ^ 2)
    odd_even = lambda a: exchange(a, devices, lambda i: (((i + 1) ^ 1) - 1) % devices)
    by_direction = lambda a: jnp.transpose(a, (1, 0, 2))
    parent = parent.T
    fine_cells, coarse_cells = by_direction(fine_pop), by_direction(coarse_pop)
    small = lambda a: pltpu.SMEM(a.shape, jnp.int32)

    cpost, e_own, c_own, fine_raw, solid_raw, meta = call(
        coarse_first_kernel,
        "coarse_first",
        [HBM] * 7,
        [
            rows_of(CB * BLOCK),
            rows_of(E_ROWS),
            rows_of(C_ROWS),
            jax.ShapeDtypeStruct(fine_cells.shape, jnp.float32),
            jax.ShapeDtypeStruct(solid.shape, jnp.int32),
            rows_of(8),
        ],
        [
            pltpu.VMEM(coarse_cells.shape, jnp.float32),
            small(fine_nbr),
            small(parent),
            small(coarse_nbr),
            small(children),
            scratch(CB * BLOCK),
            pltpu.SemaphoreType.DMA((7,)),
        ],
    )(
        *(
            pltpu.with_memory_space_constraint(a, pltpu.HBM)
            for a in (coarse_cells, fine_cells, solid, fine_nbr, parent, coarse_nbr, children)
        )
    )
    e_two = by_two(e_own)
    post, mask, f_own = call(
        fine_first_kernel,
        "fine_first",
        [VMEM] * 4,
        [rows_of(FB * BLOCK), rows_of(FB * R, jnp.int32), rows_of(F_ROWS)],
        [scratch(FB * BLOCK), scratch(FB * R, jnp.int32)],
    )(meta, fine_raw, solid_raw, c_own)

    x_in = by_one(jnp.concatenate([f_own, e_own, e_two]))
    n_in = odd_even(
        jnp.concatenate(
            [
                f_own,
                x_in[EDGES:META],
                e_own[EC_AT:],
                x_in[X_E + EC_AT : X_E2],
                e_two[EC_AT:],
                x_in[X_E2 + EC_AT :],
            ]
        )
    )
    e_halo, ez = call(
        expand_kernel,
        "expand",
        [VMEM] * 4,
        [rows_of(FB * 64), rows_of(FB * EZ_BLOCK)],
        [scratch(4 * E_ROWS)] + meta_scratch(1),
    )(f_own, e_own, e_two, x_in)
    far_edges, ez = lax.optimization_barrier((n_in[EDGES:META], ez))
    x_late = by_one(far_edges)
    new, fixed, cmid, c2_own = call(
        first_stream_kernel,
        "first_stream",
        [VMEM] * 10,
        [
            rows_of(FB * BLOCK),
            rows_of(FB * R),
            rows_of(CB * BLOCK),
            rows_of(FB * 64 + R),
        ],
        [scratch(32), scratch(HALO), scratch(R)] + meta_scratch(),
    )(post, mask, f_own, e_own, e_two, x_in, n_in, cpost, e_halo, ez)
    post2, f2_own = call(
        second_collision_kernel,
        "second_collision",
        [VMEM] * 9,
        [rows_of(FB * BLOCK), rows_of(F2_ROWS)],
        [scratch(R), scratch(5 * R)] + meta_scratch(),
    )(new, mask, f_own, x_in, n_in, x_late, e_halo, fixed, c2_own)

    x2_in = by_one(f2_own)
    n2_in = odd_even(jnp.concatenate([f2_own, x2_in[EDGES:META]]))
    x2_late = by_one(n2_in[EDGES:META])
    (new2,) = call(
        second_stream_kernel,
        "second_stream",
        [VMEM] * 8,
        [rows_of(FB * BLOCK)],
        [scratch(HALO)] + meta_scratch(1),
    )(post2, mask, f2_own, x2_in, n2_in, e_halo, ez, f_own)
    new2, means = call(
        coarsen_kernel,
        "coarsen",
        [VMEM] * 10,
        [rows_of(FB * BLOCK), rows_of(K_ROWS)],
        [scratch(5 * R)] + meta_scratch(),
    )(new2, f2_own, x2_in, n2_in, x2_late, e_halo, fixed, f_own, x_in, n_in)

    k_two = by_two(means)
    fine_out, cpassed = call(
        tail_kernel,
        "tail",
        [VMEM] * 6,
        [
            jax.ShapeDtypeStruct(fine_cells.shape, jnp.float32),
            rows_of(CB * BLOCK),
        ],
        [scratch(3 * EDGES)] + meta_scratch(1),
    )(f_own, new2, f2_own, x2_in, n2_in, cmid)
    k_two, cpassed = lax.optimization_barrier((k_two, cpassed))
    k_one = by_one(jnp.concatenate([means, k_two]))
    (coarse_out,) = call(
        coarse_last_kernel,
        "coarse_last",
        [VMEM] * 5,
        [jax.ShapeDtypeStruct(coarse_cells.shape, jnp.float32)],
        [scratch(CB * BLOCK), scratch(4 * K_ROWS)] + meta_scratch(1),
    )(f_own, cpassed, means, k_two, k_one)
    return by_direction(fine_out), by_direction(coarse_out)


def solution(mesh):
    rows = P(AXES, None)
    blocks = P(AXES, None, None)
    return jax.shard_map(
        on_device,
        mesh=mesh,
        in_specs=(blocks, blocks, rows, rows, rows, rows, rows),
        out_specs=(blocks, blocks),
        check_vma=False,
    )
```

time: 62.8 us -> 55.1 us (0.88)
  waiting for transfers between devices: 20.3 us -> 13.5 us
  local copies, waits for them, and re-layouts: 5.67 us -> 0.03 us
  Pallas kernels: 18.4 us -> 21.5 us
  starting transfers between devices: 17.5 us -> 19 us
    ppermute x9, waiting for transfers between devices: 20.3 us -> 13.5 us  [exchange(): return lax.ppermute(rows, AXES, [(i, partner(i)) for i in range(devices)])]
    unnamed x23 -> x5, local copies, waits for them, and re-layouts: 5.65 us -> 0.02 us
    pallas_call x5 -> x9, Pallas kernels: 18.4 us -> 21.5 us  [the longest x1 2.79 us: on_device(): call(first_stream_kernel, 'first_stream', [VMEM] * 10, [rows_of(FB * BLOC...]
    ppermute x9, starting transfers between devices: 17.5 us -> 19 us  [exchange(): return lax.ppermute(rows, AXES, [(i, partner(i)) for i in range(devices)])]
  transfers between devices with their start and end apart: 9 -> 9, of which waited for: 7 -> 6; matrix products, arithmetic and copies ran while one was open for 4% -> 0% of each run, Pallas kernels for 6% -> 21%
where the time goes in v2:
time: 55.1 us; the launch traced here: 55 us
  Pallas kernels  21.5 us (39%)
  starting transfers between devices  19 us (34%)
  waiting for transfers between devices  13.5 us (25%)
  between operations  0.77 us (1%)
    ppermute x9, starting transfers between devices, exchange(): return lax.ppermute(rows, AXES, [(i, partner(i)) for i in range(devices)])  19 us
    ppermute x9, waiting for transfers between devices, exchange(): return lax.ppermute(rows, AXES, [(i, partner(i)) for i in range(devices)])  13.5 us
    pallas_call x1, Pallas kernels, on_device(): call(first_stream_kernel, 'first_stream', [VMEM] * 10, [rows_of(FB * BLOC...  2.79 us
    pallas_call x1, Pallas kernels, on_device(): call(fine_first_kernel, 'fine_first', [VMEM] * 4, [rows_of(FB * BLOCK), r...  2.76 us
    pallas_call x1, Pallas kernels, on_device(): call(second_collision_kernel, 'second_collision', [VMEM] * 9, [rows_of(FB...  2.5 us
    pallas_call x1, Pallas kernels, on_device(): call(coarse_first_kernel, 'coarse_first', [HBM] * 7, [rows_of(CB * BLOCK)...  2.48 us
    pallas_call x1, Pallas kernels, on_device(): call(coarse_last_kernel, 'coarse_last', [VMEM] * 5, [jax.ShapeDtypeStruct...  2.45 us
    pallas_call x1, Pallas kernels, on_device(): call(coarsen_kernel, 'coarsen', [VMEM] * 10, [rows_of(FB * BLOCK), rows_o...  2.37 us
  transfers between devices with their start and end apart: 9, of which 6 were waited for; matrix products, arithmetic and copies ran while one was open for 0% of the time, Pallas kernels for 21%

profile of v2, /device:TPU:1, one launch (start us, length us, event | category | flops | bytes accessed | tf_op | source)
XLA Modules:
  0.0 55.0 jit_solution(4955611787250884781)
XLA Ops:
  0.6 2.5 %coarse_first.1 = (f32[1216,128]{1,0:T(8,128)S(1)}, f32[200,128]{1,0:T(8,128)S(1)}, f32[272,128]{1,0:T(8,128)S(1)}, f32[19,4,4096]{2,1,0:T(4,128)S(1)}, s32[4,4096]{1,0:T(4,128)S(1)}, /*index=5*/f32[8,128]{1,0:T(8,128)S(1)}) custom-call(f32[19,2,4096]{2,1,0:T(2,128)} %bitcast.6, f32[19,4,4096]{2,1,0:T(4,128)} %bitcast.5, s32[4,4096]{1,0:T(4,128)} %solid_hbm.1, ...), custom_call_target="tpu_custom_call" | custom-call | flops 1048576 | bytes 4194304 | tf_op jit(solution)/shard_map/coarse_first/pallas_call | solution.py:928
  3.1 2.2 %collective-permute-start = (f32[200,128]{1,0:T(8,128)S(1)}, f32[200,128]{1,0:T(8,128)S(1)}, u32[]{:S(2)}, u32[]{:S(2)}) collective-permute-start(f32[200,128]{1,0:T(8,128)S(1)} %get-tuple-element.34.e_own), channel_id=1, source_target_pairs={{0,2},{1,3},{2,0},{3,1},{4,6},{5,7},{6,4},{7,5},{8,10},{9,11},{10,... | collective-permute-start | bytes 307208 | tf_op jit(solution)/shard_map/ppermute | solution.py:915
  5.3 2.8 %fine_first.1 = (f32[2432,128]{1,0:T(8,128)S(1)}, s32[128,128]{1,0:T(8,128)S(1)}, f32[328,128]{1,0:T(8,128)S(1)}) custom-call(f32[8,128]{1,0:T(8,128)S(1)} %get-tuple-element.27.meta, f32[19,4,4096]{2,1,0:T(4,128)S(1)} %get-tuple-element.28.pop, s32[4,4096]{1,0:T(4,128)S(1)} %get-tuple-element.29.solid, f32[272,128]{1,0:T(8,128)S(1)} %get-tuple-element.30.coarse), custom_call_target="tpu_custom_call" | custom-call | flops 1048576 | bytes 4194304 | tf_op jit(solution)/shard_map/fine_first/pallas_call | solution.py:956
  8.1 0.0 collective-permute-done.e_two
  8.1 1.3 %collective-permute-start.1 = (f32[728,128]{1,0:T(8,128)S(1)}, f32[728,128]{1,0:T(8,128)S(1)}, u32[]{:S(2)}, u32[]{:S(2)}) collective-permute-start(f32[728,128]{1,0:T(8,128)S(1)} %pad_maximum_fusion), channel_id=1, source_target_pairs={{0,1},{1,0},{2,3},{3,2},{4,5},{5,4},{6,7},{7,6},{8,9},{9,8},{10,11... | collective-permute-start | bytes 1118216 | tf_op jit(solution)/shard_map/ppermute | solution.py:915
  9.4 1.3 %collective-permute-done.1.x_in.x_first = f32[728,128]{1,0:T(8,128)S(1)} collective-permute-done((f32[728,128]{1,0:T(8,128)S(1)}, f32[728,128]{1,0:T(8,128)S(1)}, u32[]{:S(2)}, u32[]{:S(2)}) %collective-permute-start.1) | collective-permute-done | bytes 372768 | tf_op jit(solution)/shard_map/ppermute | solution.py:915
  10.7 1.7 %collective-permute-start.2 = (f32[392,128]{1,0:T(8,128)S(1)}, f32[392,128]{1,0:T(8,128)S(1)}, u32[]{:S(2)}, u32[]{:S(2)}) collective-permute-start(f32[392,128]{1,0:T(8,128)S(1)} %constant_dynamic-update-slice_fusion), channel_id=1, source_target_pairs={{0,127},{1,2},{2,1},{3,4},{4,3},{5,6},{6,5},{7,8},{8,7},{9,10},{10... | collective-permute-start | bytes 602120 | tf_op jit(solution)/shard_map/ppermute | solution.py:915
  12.5 2.3 %expand.1 = (f32[256,128]{1,0:T(8,128)S(1)}, f32[320,128]{1,0:T(8,128)S(1)}) custom-call(f32[328,128]{1,0:T(8,128)S(1)} %get-tuple-element.31.f_own.f_first, f32[200,128]{1,0:T(8,128)S(1)} %get-tuple-element.34.e_own, f32[200,128]{1,0:T(8,128)S(1)} %collective-permute-done.e_two, f32[728,128]{1,0:T(8,128)S(1)} %collective-permute-done.1.x_in.x_first), custom_call_target="tpu_custom_call" | custom-call | flops 1048576 | bytes 4194304 | tf_op jit(solution)/shard_map/expand/pallas_call | solution.py:977
  14.8 1.2 %collective-permute-done.2.n_in.n_first = f32[392,128]{1,0:T(8,128)S(1)} collective-permute-done((f32[392,128]{1,0:T(8,128)S(1)}, f32[392,128]{1,0:T(8,128)S(1)}, u32[]{:S(2)}, u32[]{:S(2)}) %collective-permute-start.2) | collective-permute-done | bytes 200736 | tf_op jit(solution)/shard_map/ppermute | solution.py:915
  16.0 7.1 %collective-permute-start.3 = (f32[32,128]{1,0:T(8,128)S(1)}, f32[32,128]{1,0:T(8,128)S(1)}, u32[]{:S(2)}, u32[]{:S(2)}) collective-permute-start(f32[32,128]{1,0:T(8,128)S(1)} %slice.36), channel_id=1, source_target_pairs={{0,1},{1,0},{2,3},{3,2},{4,5},{5,4},{6,7},{7,6},{8,9},{9,8},{10,11... | collective-permute-start | bytes 49160 | tf_op jit(solution)/shard_map/ppermute | solution.py:915
  23.1 2.8 %first_stream.1 = (f32[2432,128]{1,0:T(8,128)S(1)}, f32[128,128]{1,0:T(8,128)S(1)}, f32[1216,128]{1,0:T(8,128)S(1)}, f32[288,128]{1,0:T(8,128)S(1)}) custom-call(f32[2432,128]{1,0:T(8,128)S(1)} %get-tuple-element.32.post, s32[128,128]{1,0:T(8,128)S(1)} %get-tuple-element.33.mask, f32[328,128]{1,0:T(8,128)S(1)} %get-tuple-element.31.f_own.f_first, ...), custom_call_target="tpu_custom_call" | custom-call | flops 1048576 | bytes 4194304 | tf_op jit(solution)/shard_map/first_stream/pallas_call | solution.py:986
  25.9 0.0 collective-permute-done.3.x_late
  25.9 2.5 %second_collision.1 = (f32[2432,128]{1,0:T(8,128)S(1)}, f32[320,128]{1,0:T(8,128)S(1)}) custom-call(f32[2432,128]{1,0:T(8,128)S(1)} %get-tuple-element.39.new, s32[128,128]{1,0:T(8,128)S(1)} %get-tuple-element.33.mask, f32[328,128]{1,0:T(8,128)S(1)} %get-tuple-element.31.f_own.f_first, f32[728,128]{1,0:T(8,128)S(1)} %collective-permute-done.1.x_in.x_first, ...), custom_call_target="tpu_custom_call" | custom-call | flops 1048576 | bytes 4194304 | tf_op jit(solution)/shard_map/second_collision/pallas_call | solution.py:998
  28.4 0.1 collective-permute-start.4
  28.5 1.4 %collective-permute-done.4.x_in = f32[320,128]{1,0:T(8,128)S(1)} collective-permute-done((f32[320,128]{1,0:T(8,128)S(1)}, f32[320,128]{1,0:T(8,128)S(1)}, u32[]{:S(2)}, u32[]{:S(2)}) %collective-permute-start.4) | collective-permute-done | bytes 163872 | tf_op jit(solution)/shard_map/ppermute | solution.py:915
  29.9 0.1 collective-permute-start.5
  30.0 4.9 %collective-permute-done.5.n_in = f32[352,128]{1,0:T(8,128)S(1)} collective-permute-done((f32[352,128]{1,0:T(8,128)S(1)}, f32[352,128]{1,0:T(8,128)S(1)}, u32[]{:S(2)}, u32[]{:S(2)}) %collective-permute-start.5) | collective-permute-done | bytes 180256 | tf_op jit(solution)/shard_map/ppermute | solution.py:915
  34.9 5.6 %collective-permute-start.6 = (f32[32,128]{1,0:T(8,128)S(1)}, f32[32,128]{1,0:T(8,128)S(1)}, u32[]{:S(2)}, u32[]{:S(2)}) collective-permute-start(f32[32,128]{1,0:T(8,128)S(1)} %slice.38), channel_id=1, source_target_pairs={{0,1},{1,0},{2,3},{3,2},{4,5},{5,4},{6,7},{7,6},{8,9},{9,8},{10,11... | collective-permute-start | bytes 49160 | tf_op jit(solution)/shard_map/ppermute | solution.py:915
  40.5 1.8 %second_stream.1.new_in = f32[2432,128]{1,0:T(8,128)S(1)} custom-call(f32[2432,128]{1,0:T(8,128)S(1)} %get-tuple-element.43.post, s32[128,128]{1,0:T(8,128)S(1)} %get-tuple-element.33.mask, f32[320,128]{1,0:T(8,128)S(1)} %get-tuple-element.44.f_own, f32[320,128]{1,0:T(8,128)S(1)} %collective-permute-done.4.x_in, f32[352,128]{1,0:T(8,128)S(1)} %collective-permute-done.5.n_in, ...), custom_call_target="tpu_custom_call" | custom-call | flops 1048576 | bytes 4194304 | tf_op jit(solution)/shard_map/second_stream/pallas_call | solution.py:1009
  42.3 0.0 collective-permute-done.6.x_late
  42.3 2.4 %coarsen.1 = (f32[2432,128]{1,0:T(8,128)S(1)}, f32[304,128]{1,0:T(8,128)S(1)}) custom-call(f32[2432,128]{1,0:T(8,128)S(1)} %second_stream.1.new_in, f32[320,128]{1,0:T(8,128)S(1)} %get-tuple-element.44.f_own, f32[320,128]{1,0:T(8,128)S(1)} %collective-permute-done.4.x_in, f32[352,128]{1,0:T(8,128)S(1)} %collective-permute-done.5.n_in, ...), custom_call_target="tpu_custom_call" | custom-call | flops 1048576 | bytes 4194304 | tf_op jit(solution)/shard_map/coarsen/pallas_call | solution.py:1016
  44.7 0.1 collective-permute-start.7
  44.8 2.1 %tail.1 = (f32[19,4,4096]{2,1,0:T(4,128)}, f32[1216,128]{1,0:T(8,128)S(1)}) custom-call(f32[328,128]{1,0:T(8,128)S(1)} %get-tuple-element.31.f_own.f_first, f32[2432,128]{1,0:T(8,128)S(1)} %get-tuple-element.45.new, f32[320,128]{1,0:T(8,128)S(1)} %get-tuple-element.44.f_own, f32[320,128]{1,0:T(8,128)S(1)} %collective-permute-done.4.x_in, ...), custom_call_target="tpu_custom_call" | custom-call | flops 1048576 | bytes 4194304 | tf_op jit(solution)/shard_map/tail/pallas_call | solution.py:1025
  46.9 3.5 %collective-permute-done.7.two = f32[304,128]{1,0:T(8,128)S(1)} collective-permute-done((f32[304,128]{1,0:T(8,128)S(1)}, f32[304,128]{1,0:T(8,128)S(1)}, u32[]{:S(2)}, u32[]{:S(2)}) %collective-permute-start.7) | collective-permute-done | bytes 155680 | tf_op jit(solution)/shard_map/ppermute | solution.py:915
  50.4 0.9 %collective-permute-start.8 = (f32[608,128]{1,0:T(8,128)S(1)}, f32[608,128]{1,0:T(8,128)S(1)}, u32[]{:S(2)}, u32[]{:S(2)}) collective-permute-start(f32[608,128]{1,0:T(8,128)S(1)} %pad_maximum_fusion.1), channel_id=1, source_target_pairs={{0,1},{1,0},{2,3},{3,2},{4,5},{5,4},{6,7},{7,6},{8,9},{9,8},{10,11... | collective-permute-start | bytes 933896 | tf_op jit(solution)/shard_map/ppermute | solution.py:915
  51.3 1.2 %collective-permute-done.8.x_in = f32[608,128]{1,0:T(8,128)S(1)} collective-permute-done((f32[608,128]{1,0:T(8,128)S(1)}, f32[608,128]{1,0:T(8,128)S(1)}, u32[]{:S(2)}, u32[]{:S(2)}) %collective-permute-start.8) | collective-permute-done | bytes 311328 | tf_op jit(solution)/shard_map/ppermute | solution.py:915
  52.5 2.4 %coarse_last.1 = f32[19,2,4096]{2,1,0:T(2,128)} custom-call(f32[328,128]{1,0:T(8,128)S(1)} %get-tuple-element.31.f_own.f_first, f32[1216,128]{1,0:T(8,128)S(1)} %get-tuple-element.50.cpassed, f32[304,128]{1,0:T(8,128)S(1)} %get-tuple-element.48.own, f32[304,128]{1,0:T(8,128)S(1)} %collective-permute-done.7.two, f32[608,128]{1,0:T(8,128)S(1)} %collective-permute-done.8.x_in), custom_call_target="tpu_custom_call" | custom-call | flops 1048576 | bytes 4194304 | tf_op jit(solution)/shard_map/coarse_last/pallas_call | solution.py:1037
  (12 shorter events, 0.1 us)
Async XLA Ops:
  3.1 5.0 %collective-permute-start = (f32[200,128]{1,0:T(8,128)S(1)}, f32[200,128]{1,0:T(8,128)S(1)}, u32[]{:S(2)}, u32[]{:S(2)}) collective-permute-start(f32[200,128]{1,0:T(8,128)S(1)} %get-tuple-element.34.e_own), channel_id=1, source_target_pairs={{0,2},{1,3},{2,0},{3,1},{4,6},{5,7},{6,4},{7,5},{8,10},{9,11},{10,... | collective-permute-start | bytes 307208 | tf_op jit(solution)/shard_map/ppermute | solution.py:915
  8.1 2.6 %collective-permute-start.1 = (f32[728,128]{1,0:T(8,128)S(1)}, f32[728,128]{1,0:T(8,128)S(1)}, u32[]{:S(2)}, u32[]{:S(2)}) collective-permute-start(f32[728,128]{1,0:T(8,128)S(1)} %pad_maximum_fusion), channel_id=1, source_target_pairs={{0,1},{1,0},{2,3},{3,2},{4,5},{5,4},{6,7},{7,6},{8,9},{9,8},{10,11... | collective-permute-start | bytes 1118216 | tf_op jit(solution)/shard_map/ppermute | solution.py:915
  10.7 5.2 %collective-permute-start.2 = (f32[392,128]{1,0:T(8,128)S(1)}, f32[392,128]{1,0:T(8,128)S(1)}, u32[]{:S(2)}, u32[]{:S(2)}) collective-permute-start(f32[392,128]{1,0:T(8,128)S(1)} %constant_dynamic-update-slice_fusion), channel_id=1, source_target_pairs={{0,127},{1,2},{2,1},{3,4},{4,3},{5,6},{6,5},{7,8},{8,7},{9,10},{10... | collective-permute-start | bytes 602120 | tf_op jit(solution)/shard_map/ppermute | solution.py:915
  16.0 9.9 %collective-permute-start.3 = (f32[32,128]{1,0:T(8,128)S(1)}, f32[32,128]{1,0:T(8,128)S(1)}, u32[]{:S(2)}, u32[]{:S(2)}) collective-permute-start(f32[32,128]{1,0:T(8,128)S(1)} %slice.36), channel_id=1, source_target_pairs={{0,1},{1,0},{2,3},{3,2},{4,5},{5,4},{6,7},{7,6},{8,9},{9,8},{10,11... | collective-permute-start | bytes 49160 | tf_op jit(solution)/shard_map/ppermute | solution.py:915
  28.4 1.5 %collective-permute-start.4 = (f32[320,128]{1,0:T(8,128)S(1)}, f32[320,128]{1,0:T(8,128)S(1)}, u32[]{:S(2)}, u32[]{:S(2)}) collective-permute-start(f32[320,128]{1,0:T(8,128)S(1)} %get-tuple-element.44.f_own), channel_id=1, source_target_pairs={{0,1},{1,0},{2,3},{3,2},{4,5},{5,4},{6,7},{7,6},{8,9},{9,8},{10,11... | collective-permute-start | bytes 491528 | tf_op jit(solution)/shard_map/ppermute | solution.py:915
  29.9 5.0 %collective-permute-start.5 = (f32[352,128]{1,0:T(8,128)S(1)}, f32[352,128]{1,0:T(8,128)S(1)}, u32[]{:S(2)}, u32[]{:S(2)}) collective-permute-start(f32[352,128]{1,0:T(8,128)S(1)} %pad_maximum_fusion.2), channel_id=1, source_target_pairs={{0,127},{1,2},{2,1},{3,4},{4,3},{5,6},{6,5},{7,8},{8,7},{9,10},{10... | collective-permute-start | bytes 540680 | tf_op jit(solution)/shard_map/ppermute | solution.py:915
  34.9 7.4 %collective-permute-start.6 = (f32[32,128]{1,0:T(8,128)S(1)}, f32[32,128]{1,0:T(8,128)S(1)}, u32[]{:S(2)}, u32[]{:S(2)}) collective-permute-start(f32[32,128]{1,0:T(8,128)S(1)} %slice.38), channel_id=1, source_target_pairs={{0,1},{1,0},{2,3},{3,2},{4,5},{5,4},{6,7},{7,6},{8,9},{9,8},{10,11... | collective-permute-start | bytes 49160 | tf_op jit(solution)/shard_map/ppermute | solution.py:915
  44.7 5.7 %collective-permute-start.7 = (f32[304,128]{1,0:T(8,128)S(1)}, f32[304,128]{1,0:T(8,128)S(1)}, u32[]{:S(2)}, u32[]{:S(2)}) collective-permute-start(f32[304,128]{1,0:T(8,128)S(1)} %get-tuple-element.48.own), channel_id=1, source_target_pairs={{0,2},{1,3},{2,0},{3,1},{4,6},{5,7},{6,4},{7,5},{8,10},{9,11},{10,... | collective-permute-start | bytes 466952 | tf_op jit(solution)/shard_map/ppermute | solution.py:915
  50.4 2.1 %collective-permute-start.8 = (f32[608,128]{1,0:T(8,128)S(1)}, f32[608,128]{1,0:T(8,128)S(1)}, u32[]{:S(2)}, u32[]{:S(2)}) collective-permute-start(f32[608,128]{1,0:T(8,128)S(1)} %pad_maximum_fusion.1), channel_id=1, source_target_pairs={{0,1},{1,0},{2,3},{3,2},{4,5},{5,4},{6,7},{7,6},{8,9},{9,8},{10,11... | collective-permute-start | bytes 933896 | tf_op jit(solution)/shard_map/ppermute | solution.py:915

commit v3 on v2

v3 whole, which is shorter than its diff:
```python
import jax
import jax.numpy as jnp
from jax import lax
from jax.experimental import pallas as pl
from jax.experimental.pallas import tpu as pltpu
from jax.sharding import PartitionSpec as P

AXES = ("gx", "gy")
VELOCITIES = (
    (0, 0, 0),
    (1, 0, 0),
    (-1, 0, 0),
    (0, 1, 0),
    (0, -1, 0),
    (0, 0, 1),
    (0, 0, -1),
    (1, 1, 0),
    (-1, -1, 0),
    (1, -1, 0),
    (-1, 1, 0),
    (1, 0, 1),
    (-1, 0, -1),
    (1, 0, -1),
    (-1, 0, 1),
    (0, 1, 1),
    (0, -1, -1),
    (0, 1, -1),
    (0, -1, 1),
)
WEIGHTS = (1.0 / 3.0,) + (1.0 / 18.0,) * 6 + (1.0 / 36.0,) * 12
OPPOSITE = (0, 2, 1, 4, 3, 6, 5, 8, 7, 10, 9, 12, 11, 14, 13, 16, 15, 18, 17)
OMEGA_COARSE = 1.6
OMEGA_FINE = 1.0 / (2.0 * (1.0 / 1.6 - 0.5) + 0.5)

XP = (1, 7, 9, 11, 13)
XM = (2, 8, 10, 12, 14)
YP = (3, 7, 10, 15, 17)
YM = (4, 8, 9, 16, 18)
ZP = (5, 11, 14, 15, 18)
ZM = (6, 12, 13, 16, 17)
YP1, YM1 = (3, 15, 17), (4, 16, 18)
YP2, YM2 = (7, 10), (8, 9)
ZP2, ZM2 = (11, 14, 15, 18), (12, 13, 16, 17)


R = 32
FB, CB = 4, 2
FR, CR = FB * R, CB * R
F_ALL, C_ALL = 19 * FR, 19 * CR
PY_AT = FR
ZS = 2 * FR
EDGES = ZS + R
META = EDGES + R
F_ROWS = META + 8
F2_ROWS = META
EC_AT = 6 * R
E_ROWS = EC_AT + 8
C_ROWS = 2 * FR + 8
K_ROWS = 2 * 19 * 8
HALO = 3 * EDGES + 2 * FR
X_E = F_ROWS
X_E2 = X_E + E_ROWS
N_EDGE = F_ROWS
N_EC = N_EDGE + R
M_PARENT, M_CNBR, M_CHILD = 4, 8, 16


def iotas(rows=R):
    row = lax.broadcasted_iota(jnp.int32, (rows, 128), 0)
    lane = lax.broadcasted_iota(jnp.int32, (rows, 128), 1)
    return row, lane


def roll(a, shift, axis):
    if isinstance(shift, int):
        shift = shift % a.shape[axis]
        if shift == 0:
            return a
    return pltpu.roll(a, shift, axis)


def at(ref, start, size=R):
    if not isinstance(start, int):
        start = pl.multiple_of(start, 8)
    return ref[pl.ds(start, size), :]


def put(ref, start, value):
    if not isinstance(start, int):
        start = pl.multiple_of(start, 8)
    ref[pl.ds(start, value.shape[0]), :] = value


def zeros(rows):
    return jnp.zeros((rows, 128), jnp.float32)


def total(terms):
    while len(terms) > 1:
        pairs = [terms[k] + terms[k + 1] for k in range(0, len(terms) - 1, 2)]
        terms = pairs + terms[len(terms) - len(terms) % 2 :]
    return terms[0]


def collide(f, rate):
    rho = total(f)
    mom = []
    for axis in range(3):
        plus = [f[i] for i in range(19) if VELOCITIES[i][axis] == 1]
        minus = [f[i] for i in range(19) if VELOCITIES[i][axis] == -1]
        mom.append(total(plus) - total(minus))
    inv = 1.0 / rho
    u = [m * inv for m in mom]
    base = 1.0 - 1.5 * (u[0] * u[0] + u[1] * u[1] + u[2] * u[2])
    scaled = {w: (rate * w) * rho for w in sorted(set(WEIGHTS))}
    keep = 1.0 - rate
    out = [None] * 19
    out[0] = keep * f[0] + scaled[WEIGHTS[0]] * base
    for i in range(1, 19, 2):
        proj = None
        for axis in range(3):
            c = VELOCITIES[i][axis]
            if c:
                term = u[axis]
                if proj is None:
                    proj = term if c > 0 else -term
                else:
                    proj = proj + term if c > 0 else proj - term
        even = base + 4.5 * (proj * proj)
        odd = 3.0 * proj
        w = scaled[WEIGHTS[i]]
        out[i] = keep * f[i] + w * (even + odd)
        out[i + 1] = keep * f[i + 1] + w * (even - odd)
    return out


def collide_rows(src, dst, rows, rate, mask=None, corner=None):
    def body(v, carry):
        f = [at(src, i * rows + v * 16, 16) for i in range(19)]
        if corner is not None:
            edge = at(corner, v * 16, 16)
            f = [with_corners(f[i], i, edge) for i in range(19)]
        post = collide(f, rate)
        if mask is not None:
            solid = (at(mask, v * 16, 16) & 1) > 0
            post = [jnp.where(solid, f[i], post[i]) for i in range(19)]
        for i in range(19):
            put(dst, i * rows + v * 16, post[i])
        return carry

    lax.fori_loop(0, rows // 16, body, 0)


def upper_of(rows, blocks):
    row, _ = iotas(rows)
    return ((row // blocks) & 1) == 1


def swap_halves(a, blocks):
    if blocks == 4:
        rows = a.shape[0]
        return pltpu.roll(a.reshape(rows // 8, 8, 128), 4, 1).reshape(rows, 128)
    return jnp.where(upper_of(a.shape[0], blocks), roll(a, blocks, 0), roll(a, -blocks, 0))


def pack_x(get, packed, first=0):
    _, lane = iotas(packed.shape[0])
    x = lane & 15
    for j in range(5):
        packed = jnp.where(x == first + j, roll(get(XP[j]), first + j - 15, 1), packed)
        packed = jnp.where(x == first + 5 + j, roll(get(XM[j]), first + 5 + j, 1), packed)
    return packed


def pack_y(get, plus, minus, first, rest, blocks):
    rows = rest.shape[0]
    _, lane = iotas(rows)
    upper = upper_of(rows, blocks)
    group = lane >> 4
    packed = zeros(rows)
    for k in range(len(plus)):
        p = first + k
        one = jnp.where(upper, roll(get(plus[k]), 16 * p - 112, 1), roll(get(minus[k]), 16 * p, 1))
        packed = jnp.where(group == p, one, packed)
    packed = swap_halves(packed, blocks)
    return jnp.where((group >= first) & (group < first + len(plus)), packed, rest)


def pack_edges(get, rows):
    _, lane = iotas(rows)
    upper = upper_of(rows, FB)
    first = jnp.where(upper, roll(get(7), -127, 1), get(8))
    second = jnp.where(upper, roll(get(10), 1 - 112, 1), roll(get(9), 1 - 15, 1))
    return swap_halves(jnp.where(lane == 0, first, second), FB)


def move_x(a, cx, halo):
    _, lane = iotas(a.shape[0])
    x = lane & 15
    if cx == 1:
        return jnp.where(x == 0, halo, roll(a, 1, 1))
    return jnp.where(x == 15, halo, roll(a, -1, 1))


def move_y(a, cy, halo, blocks):
    _, lane = iotas(a.shape[0])
    upper = upper_of(a.shape[0], blocks)
    near = roll(a, 16 * cy, 1)
    if cy == 1:
        return jnp.where(lane < 16, jnp.where(upper, swap_halves(near, blocks), halo), near)
    return jnp.where(lane >= 112, jnp.where(upper, halo, swap_halves(near, blocks)), near)


def move_z_coarse(a, cz, halo8):
    row, _ = iotas(8)
    near = roll(a, 4 * cz, 0)
    if cz == 1:
        return jnp.concatenate([jnp.where(row < 4, halo8, near[:8]), near[8:]], axis=0)
    return jnp.concatenate([near[:-8], jnp.where(row >= 4, halo8, near[-8:])], axis=0)


def send_faces(post, out, coarse, spot):
    for h in range(2):
        rows = h * 64
        get = lambda i: at(post, i * FR + rows, 64)
        put(out, rows, pack_x(get, at(coarse, rows, 64)))
        put(out, PY_AT + rows, pack_y(get, YP, YM, 0, at(coarse, PY_AT + rows, 64), FB))
        put(spot, rows, pack_edges(get, 64))
    _, lane = iotas()
    edges = zeros(R)
    for b in range(FB):
        edges = jnp.where((lane >> 1) == b, roll(spot[pl.ds(b, R, stride=FB), :], 2 * b, 1), edges)
    put(out, EDGES, edges)


def place():
    device = lax.axis_index("gx") * lax.axis_size("gy") + lax.axis_index("gy")
    sign = 1 - 2 * (device & 1)
    return device, sign


def number(meta, row, column):
    return meta[row, column].astype(jnp.int32)


def fetch_meta(pairs, sem):
    copies = [
        pltpu.make_async_copy(ref.at[pl.ds(META, 8)], dst, sem.at[k])
        for k, (ref, dst) in enumerate(pairs)
    ]
    for c in copies:
        c.start()
    return copies


def coarse_first_kernel(
    pop_hbm,
    fine_hbm,
    solid_hbm,
    nbr_hbm,
    parent_hbm,
    cnbr_hbm,
    children_hbm,
    post,
    e_out,
    c_out,
    fine_out,
    solid_out,
    meta_out,
    raw,
    spot,
    nbr,
    parent,
    cnbr,
    children,
    sem,
):
    copies = [
        pltpu.make_async_copy(src, dst, sem.at[k])
        for k, (src, dst) in enumerate(
            (
                (pop_hbm, raw),
                (nbr_hbm, nbr),
                (parent_hbm, parent),
                (cnbr_hbm, cnbr),
                (children_hbm, children),
                (fine_hbm, fine_out),
                (solid_hbm, solid_out),
            )
        )
    ]
    for c in copies:
        c.start()
    copies[0].wait()
    _, lane = iotas()
    row8, lane8 = iotas(8)
    x = lane & 15
    half = lambda i: at(raw, i * CR)
    for qx in range(2):
        packed = zeros(R)
        for j in range(5):
            packed = jnp.where(x == j, roll(half(XP[j]), j - 8 * qx, 1), packed)
            packed = jnp.where(x == 5 + j, roll(half(XM[j]), 5 + j - 8 * qx - 7, 1), packed)
        put(e_out, qx * R, packed)
    low, high = zeros(R), zeros(R)
    for p in range(5):
        low = jnp.where((lane >> 4) == p, roll(half(YP[p]), 16 * p, 1), low)
        high = jnp.where((lane >> 4) == p, roll(half(YM[p]), 16 * p - 112, 1), high)
    put(e_out, 2 * R, low)
    put(e_out, 3 * R, high)
    put(e_out, 4 * R, zeros(2 * R))
    for k in range(5):
        e_out[pl.ds(4 * R + 4 * k, 4), :] = raw[pl.ds(ZP[k] * CR, 4), :]
        e_out[pl.ds(4 * R + 20 + 4 * k, 4), :] = raw[pl.ds(ZM[k] * CR + 28, 4), :]
    corner = zeros(8)
    for c in range(CB):
        for q in range(4):
            for e, (i, yq, xq) in enumerate(((7, 7, 0), (10, 7, 7), (9, 0, 0), (8, 0, 7))):
                to = (c * 4 + q) * 4 + e
                rows = raw[pl.ds(i * CR + (q // 2) * 2 + c, 8, stride=4), :]
                rows = roll(rows, to - (yq * 16 + 8 * (q % 2) + xq), 1)
                corner = jnp.where(lane8 == to, rows, corner)
    put(e_out, EC_AT, corner)

    collide_rows(raw, post, CR, OMEGA_COARSE)
    get = lambda i: at(post, i * CR, CR)
    _, wide = iotas(CR)
    ahead, back = zeros(CR), zeros(CR)
    for j in range(5):
        ahead = jnp.where((wide & 15) == 10 + j, roll(get(XP[j]), 10 + j - 15, 1), ahead)
        back = jnp.where((wide & 15) == 10 + j, roll(get(XM[j]), 10 + j, 1), back)
    for k, packed in enumerate((ahead, back)):
        put(spot, 0, packed)
        for c in range(CB):
            c_out[pl.ds(2 * c + k, R, stride=FB), :] = spot[pl.ds(c, R, stride=CB), :]
    put(spot, 0, pack_y(get, YP1, YM1, 5, zeros(CR), CB))
    for c in range(CB):
        c_out[pl.ds(PY_AT + c, R, stride=FB), :] = spot[pl.ds(c, R, stride=CB), :]
        c_out[pl.ds(PY_AT + 2 + c, R, stride=FB), :] = zeros(R)
    top = roll(at(post, 6 * CR - 8, 8), 4, 0)
    bottom = roll(at(post, 6 * CR, 8), 4, 0)
    put(c_out, 2 * FR, jnp.where(row8 < 4, top, bottom))

    for c in copies[1:]:
        c.wait()
    meta = zeros(8)
    entries = []
    for b in range(FB):
        entries += [(b, k, nbr[b, k]) for k in range(4)]
        entries += [(b, M_PARENT + k, parent[k, b]) for k in range(2)]
    for c in range(CB):
        entries += [(c, M_CNBR + k, cnbr[c, k]) for k in range(6)]
        entries += [(c, M_CHILD + k, children[c, k]) for k in range(4)]
    for b, k, value in entries:
        meta = jnp.where((row8 == b) & (lane8 == k), value.astype(jnp.float32), meta)
    put(meta_out, 0, meta)


def fine_first_kernel(meta, pop, solid, coarse, post, mask, f_out, spot):
    s = jnp.where(solid[...] > 0, 1, 0)
    bits = s
    none = jnp.zeros_like(s)
    by_z = {0: lambda a: a}
    by_z[1] = lambda a: jnp.concatenate([a[-8:], a[:-8]], axis=0)
    by_z[-1] = lambda a: jnp.concatenate([a[8:], a[:8]], axis=0)
    by_y = {cy: move_y(s, cy, none, FB) for cy in (1, -1)}
    by_y[0] = s
    by_x = {(cx, cy): roll(by_y[cy], cx, 1) for cx in (1, -1) for cy in (-1, 0, 1)}
    for i in range(1, 19):
        cx, cy, cz = VELOCITIES[i]
        moved = by_z[cz](by_x[cx, cy] if cx else by_y[cy])
        bits = bits | (moved << i)
    put(mask, 0, bits)
    collide_rows(pop, post, FR, OMEGA_FINE, mask)
    put(f_out, ZS, at(coarse, 2 * FR, 8))
    put(f_out, ZS + 8, zeros(24))
    put(f_out, META, meta[...])
    send_faces(post, f_out, coarse, spot)


def onehot(rows, cols, source):
    row = lax.broadcasted_iota(jnp.int32, (rows, cols), 0)
    col = lax.broadcasted_iota(jnp.int32, (rows, cols), 1)
    return jnp.where(row == source(col), 1.0, 0.0).astype(jnp.bfloat16)


def exact_dot(a, b):
    result = None
    for _ in range(3):
        part = a.astype(jnp.bfloat16)
        a = a - part.astype(jnp.float32)
        term = jnp.dot(part, b, preferred_element_type=jnp.float32)
        result = term if result is None else result + term
    return result


def expand_kernel(f_own, e_own, e_two, x_in, e_halo, ez, gathered, meta, sem):
    device, _ = place()
    (fetch,) = fetch_meta(((f_own, meta),), sem)
    put(gathered, 0, e_own[...])
    put(gathered, E_ROWS, x_in[X_E : X_E + E_ROWS, :])
    put(gathered, 2 * E_ROWS, e_two[...])
    put(gathered, 3 * E_ROWS, x_in[X_E2 : X_E2 + E_ROWS, :])
    row, lane = iotas(16)
    x = lane & 15
    spread_x = onehot(128, 256, lambda m: ((m >> 7) * 4 + ((m & 127) >> 5)) * 16 + (m & 15))
    fetch.wait()
    for b in range(FB):
        p, q = number(meta, b, M_PARENT), number(meta, b, M_PARENT + 1)
        qy, qx = q >> 1, q & 1
        base = (((p >> 1) ^ device) & 3) * E_ROWS + qy * 2 + (p & 1)
        ex = exact_dot(gathered[pl.ds(base + qx * R, 8, stride=4), :], spread_x)
        spread_y = onehot(128, 128, lambda m: (m >> 4) * 16 + 8 * qx + ((m & 15) >> 1))
        ey = exact_dot(
            jnp.concatenate(
                [gathered[pl.ds(base + (2 + k) * R, 8, stride=4), :] for k in range(2)], axis=0
            ),
            spread_y,
        )
        for k in range(2):
            for yh in range(2):
                rows = pl.ds(8 * k + 4 * yh + b, 8, stride=16)
                e_halo[rows, :] = ex[:, 128 * yh : 128 * yh + 128]
                rows = pl.ds(PY_AT + 8 * k + 4 * yh + b, 8, stride=16)
                e_halo[rows, :] = ey[8 * yh : 8 * yh + 8]
        spread_z = onehot(
            128,
            256,
            lambda m: ((m >> 7) * 4 + ((m & 127) >> 5)) * 16 + 8 * qx + ((m & 15) >> 1),
        )
        ezs = exact_dot(gathered[pl.ds(base + 4 * R, 16, stride=4), :], spread_z)
        a0, a1 = ezs[:, :128], ezs[:, 128:]
        moves = {}
        moves[0, 0] = (a0, a1)
        moves[1, 0] = tuple(jnp.where(x == 0, a, roll(a, 1, 1)) for a in (a0, a1))
        moves[-1, 0] = tuple(jnp.where(x == 15, a, roll(a, -1, 1)) for a in (a0, a1))
        moves[0, 1] = (
            jnp.where(lane < 16, a0, roll(a0, 16, 1)),
            jnp.where(lane < 16, roll(a0, 16, 1), roll(a1, 16, 1)),
        )
        moves[0, -1] = (
            jnp.where(lane >= 112, roll(a1, -16, 1), roll(a0, -16, 1)),
            jnp.where(lane >= 112, a1, roll(a1, -16, 1)),
        )
        out = [a0, a1]
        for k, i in enumerate(ZP + ZM):
            moved = moves[VELOCITIES[i][:2]]
            out = [jnp.where(row == k, moved[h], out[h]) for h in range(2)]
        for h in range(2):
            ez[pl.ds(4 * h + b, 8, stride=8), :] = out[h][:8]
            ez[pl.ds(64 + 4 * h + b, 2, stride=8), :] = out[h][8:10]


def gather_halo(own, x_in, n_in, halo):
    for k, ref in enumerate((n_in, own, x_in)):
        put(halo, k * EDGES, ref[0:EDGES, :])


def gather_faces(meta, device, sign, e_halo, halo, faces):
    put(halo, 3 * EDGES, e_halo[...])
    for k in range(4):
        for b in range(FB):
            n = number(meta, b, k)
            safe = jnp.maximum(n, 0)
            which = jnp.clip(((safe >> 2) - device) * sign + 1, 0, 2)
            start = jnp.where(n >= 0, which * EDGES + (safe & 3), 3 * EDGES + b)
            start = start + (PY_AT if k >= 2 else 0)
            faces[pl.ds(k * FR + b, R, stride=FB), :] = halo[pl.ds(start, R, stride=FB), :]


def gather_edges(own, x_in, n_in, x_late, relayed, edges):
    for k, ref in enumerate((n_in, own, x_in)):
        put(edges, (k + 1) * R, ref[EDGES : EDGES + R, :])
    put(edges, 0, n_in[pl.ds(relayed, R), :])
    put(edges, 4 * R, x_late[...])


def corners(meta_n, meta_own, meta_x, device, sign, e_halo, edges, fixed, spot):
    row, lane = iotas()
    upper = (row & 1) == 1
    for b in range(FB):
        result = at(fixed, b * R)
        own_rows = e_halo[pl.ds(PY_AT + b, R, stride=FB), :]
        for side in range(2):
            n = number(meta_own, b, 2 + side)
            safe = jnp.maximum(n, 0)
            which = jnp.clip(((safe >> 2) - device) * sign + 1, 0, 2)
            row_n = safe & 3
            for end in range(2):
                i = ((7, 10), (9, 8))[side][end]
                p = (YP, YM)[side].index(i)
                edge_col = ((0, 1), (1, 0))[side][end]
                to = 112 * side + 15 * end
                m = jnp.where(
                    which == 0,
                    meta_n[row_n, end],
                    jnp.where(which == 1, meta_own[row_n, end], meta_x[row_n, end]),
                ).astype(jnp.int32)
                m_safe = jnp.maximum(m, 0)
                slot = jnp.clip(((m_safe >> 2) - device) * sign + 2, 0, 4)
                shift = (to - (2 * (m_safe & 3) + edge_col)) & 127
                sent = roll(at(edges, slot * R), shift, 1)
                own = roll(own_rows, to - (16 * p + 15 * end), 1)
                value = jnp.where(n < 0, own, sent)
                change = jnp.logical_or(n < 0, m >= 0)
                here = (lane == to) & (upper if side else jnp.logical_not(upper)) & change
                result = jnp.where(here, value, result)
        spot[pl.ds(b, R, stride=FB), :] = result


def with_corners(cells, i, corner):
    if i not in (7, 8, 9, 10):
        return cells
    row, lane = iotas(cells.shape[0])
    column, upper = {7: (0, 0), 10: (15, 0), 9: (112, 1), 8: (127, 1)}[i]
    return jnp.where((lane == column) & (((row // FB) & 1) == upper), corner, cells)


def fixed_corners(meta_n, meta_own, meta_x, device, sign, group, from_n, fixed, spare):
    _, lane = iotas()
    npart = device - sign
    for b in range(FB):
        result = zeros(R)
        for side in range(2):
            safe = jnp.maximum(number(meta_own, b, 2 + side), 0)
            which = jnp.clip(((safe >> 2) - device) * sign + 1, 0, 2)
            row_n = safe & 3
            p, q = (
                jnp.where(
                    which == 0,
                    meta_n[row_n, M_PARENT + k],
                    jnp.where(
                        which == 1, meta_own[row_n, M_PARENT + k], meta_x[row_n, M_PARENT + k]
                    ),
                ).astype(jnp.int32)
                for k in range(2)
            )
            near = ((p >> 1) ^ device) & 3
            far = ((p >> 1) ^ npart) & 3
            quad = jnp.where(which == 0, at(from_n, far * 8, 8), at(group, near * 8, 8))
            base = (2 * b + side) * R
            for k in range(4):
                spare[pl.ds(base + k, 8, stride=4), :] = quad
            rows = at(spare, base)
            for end in range(2):
                to = 112 * side + 15 * end
                source = ((p & 1) * 4 + q) * 4 + 2 * side + end
                result = jnp.where(lane == to, roll(rows, (to - source) & 127, 1), result)
        put(fixed, b * R, result)


def stream_fine(post, mask, faces, ez, dst):
    put(dst, 0, at(post, 0, FR))
    for h in range(2):
        bits = at(mask, h * 64, 64)
        solid = (bits & 1) > 0
        for i in range(1, 19):
            cx, cy, cz = VELOCITIES[i]
            start = max(h * 64 - 8 * cz, 0)
            stop = min(h * 64 + 64 - 8 * cz, FR)
            size = stop - start
            g = at(post, i * FR + start, size)
            if cx == 1:
                g = move_x(g, 1, roll(at(faces, start, size), -XP.index(i), 1))
            elif cx == -1:
                g = move_x(g, -1, roll(at(faces, FR + start, size), 10 - XM.index(i), 1))
            if cy == 1:
                side = roll(at(faces, 2 * FR + start, size), cx - 16 * YP.index(i), 1)
                g = move_y(g, 1, side, FB)
            elif cy == -1:
                side = roll(at(faces, 3 * FR + start, size), 112 + cx - 16 * YM.index(i), 1)
                g = move_y(g, -1, side, FB)
            if size < 64:
                k = ZP.index(i) if cz == 1 else 5 + ZM.index(i)
                layer = at(ez, 8 * k, 8)
                g = jnp.concatenate([layer, g] if cz == 1 else [g, layer], axis=0)
            here = h * 64
            g = jnp.where((bits & (1 << i)) > 0, at(post, OPPOSITE[i] * FR + here, 64), g)
            put(dst, i * FR + here, jnp.where(solid, at(post, i * FR + here, 64), g))


class CoarseSides:
    def __init__(self, meta, device, sign):
        self.has, self.which, self.slot = [], [], []
        for k in range(6):
            index = [number(meta, c, M_CNBR + k) for c in range(CB)]
            safe = [jnp.maximum(n, 0) for n in index]
            self.has.append(index)
            self.which.append(
                [jnp.clip(((n >> 1) - device) * sign + 1, 0, 2) * EDGES for n in safe]
            )
            self.slot.append([n & 1 for n in safe])

    def exists(self, k, rows):
        row, _ = iotas(rows)
        first, second = self.has[k]
        return jnp.where((row & 1) == 0, first, second) >= 0

    def face(self, k, halo, spot):
        for c in range(CB):
            if k < 2:
                start = self.which[k][c] + 2 * self.slot[k][c] + k
            else:
                start = self.which[k][c] + PY_AT + self.slot[k][c]
            spot[pl.ds(k * CR + c, R, stride=CB), :] = halo[pl.ds(start, R, stride=FB), :]

    def layers(self, k, halo, spot, count):
        for c in range(CB):
            for n in range(count):
                start = self.which[k][c] + ZS + 8 * n + 4 * (k - 4) + self.slot[k][c]
                spot[pl.ds(8 * n + 4 * (k - 4) + c, 2, stride=2), :] = halo[
                    pl.ds(start, 2, stride=2), :
                ]


def first_stream_kernel(
    post,
    mask,
    f_own,
    e_own,
    e_two,
    x_in,
    n_in,
    cpost,
    e_halo,
    ez,
    new,
    fixed,
    cmid,
    c_out,
    group,
    halo,
    faces,
    spare,
    cfaces,
    clayers,
    meta_n,
    meta_own,
    meta_x,
    sem,
):
    device, sign = place()
    copies = fetch_meta(((n_in, meta_n), (f_own, meta_own), (x_in, meta_x)), sem)
    put(group, 0, e_own[EC_AT:E_ROWS, :])
    put(group, 8, x_in[X_E + EC_AT : X_E + E_ROWS, :])
    put(group, 16, e_two[EC_AT:E_ROWS, :])
    put(group, 24, x_in[X_E2 + EC_AT : X_E2 + E_ROWS, :])
    gather_halo(f_own, x_in, n_in, halo)
    put(c_out, 0, zeros(2 * FR))
    for c in copies:
        c.wait()
    gather_faces(meta_own, device, sign, e_halo, halo, faces)

    row8, _ = iotas(8)
    sides = CoarseSides(meta_own, device, sign)
    for k in range(4):
        sides.face(k, halo, cfaces)
    for k in (4, 5):
        sides.layers(k, halo, clayers, 1)
    put(cmid, 0, at(cpost, 0, CR))
    for i in range(1, 19):
        cx, cy, cz = VELOCITIES[i]
        a = at(cpost, i * CR, CR)
        k = {1: 0, -1: 1}[cx] if cx else {1: 2, -1: 3}[cy] if cy else {1: 4, -1: 5}[cz]
        if cx:
            column = -10 - XP.index(i) if cx == 1 else 5 - XM.index(i)
            side = roll(at(cfaces, k * CR, CR), column, 1)
            g = move_x(a, cx, jnp.where(sides.exists(k, CR), side, a))
        elif cy:
            column = -16 * (5 + YP1.index(i)) if cy == 1 else 112 - 16 * (5 + YM1.index(i))
            side = roll(at(cfaces, k * CR, CR), column, 1)
            g = move_y(a, cy, jnp.where(sides.exists(k, CR), side, a), CB)
        else:
            own = a[:8] if cz == 1 else a[-8:]
            g = move_z_coarse(a, cz, jnp.where(sides.exists(k, 8), clayers[0:8, :], own))
        put(cmid, i * CR, g)
    put(cfaces, 0, pack_y(lambda i: at(cmid, i * CR, CR), YP2, YM2, 5, zeros(CR), CB))
    for c in range(CB):
        c_out[pl.ds(PY_AT + c, R, stride=FB), :] = cfaces[pl.ds(c, R, stride=CB), :]
    for k in range(4):
        top = roll(at(cmid, (ZP2[k] + 1) * CR - 8, 8), 4, 0)
        bottom = roll(at(cmid, ZM2[k] * CR, 8), 4, 0)
        put(c_out, 2 * FR + 8 * k, jnp.where(row8 < 4, top, bottom))

    fixed_corners(
        meta_n,
        meta_own,
        meta_x,
        device,
        sign,
        group,
        n_in.at[pl.ds(N_EC, 32)],
        fixed,
        spare,
    )
    stream_fine(post, mask, faces, ez, new)


def second_collision_kernel(
    new,
    mask,
    f_own,
    x_in,
    n_in,
    x_late,
    e_halo,
    fixed,
    coarse,
    post,
    f_out,
    spot,
    edges,
    meta_n,
    meta_own,
    meta_x,
    sem,
):
    device, sign = place()
    copies = fetch_meta(((n_in, meta_n), (f_own, meta_own), (x_in, meta_x)), sem)
    gather_edges(f_own, x_in, n_in, x_late, N_EDGE, edges)
    put(f_out, ZS, coarse[pl.ds(2 * FR, R), :])
    for c in copies:
        c.wait()
    corners(meta_n, meta_own, meta_x, device, sign, e_halo, edges, fixed, spot)
    collide_rows(new, post, FR, OMEGA_FINE, mask, spot)
    send_faces(post, f_out, coarse, spot)


def second_stream_kernel(
    post, mask, f_own, x_in, n_in, e_halo, ez, f_first, new, halo, faces, meta, sem
):
    device, sign = place()
    (fetch,) = fetch_meta(((f_first, meta),), sem)
    gather_halo(f_own, x_in, n_in, halo)
    fetch.wait()
    gather_faces(meta, device, sign, e_halo, halo, faces)
    stream_fine(post, mask, faces, ez, new)


def coarsen_kernel(
    new,
    f_own,
    x_in,
    n_in,
    x_late,
    e_halo,
    fixed,
    f_first,
    x_first,
    n_first,
    cornered,
    means,
    spot,
    edges,
    meta_n,
    meta_own,
    meta_x,
    sem,
):
    device, sign = place()
    copies = fetch_meta(((n_first, meta_n), (f_first, meta_own), (x_first, meta_x)), sem)
    gather_edges(f_own, x_in, n_in, x_late, F2_ROWS, edges)
    for c in copies:
        c.wait()
    corners(meta_n, meta_own, meta_x, device, sign, e_halo, edges, fixed, spot)
    for i in range(7, 11):
        put(cornered, (i - 7) * FR, with_corners(at(new, i * FR, FR), i, spot[...]))

    row = lax.broadcasted_iota(jnp.int32, (128, 128), 0)
    col = lax.broadcasted_iota(jnp.int32, (128, 128), 1)
    target = lambda yh, h: (yh * 4 + (row >> 5)) * 16 + ((row & 15) >> 1) + 8 * h
    mats = [
        [jnp.where(col == target(yh, h), 0.125, 0.0).astype(jnp.bfloat16) for yh in range(2)]
        for h in range(2)
    ]
    for pair in range(2):
        for ref, base, first, last in (
            (new, 0, 0, 7),
            (cornered, 7, 7, 11),
            (new, 0, 11, 19),
        ):
            rows = 8 * (last - first)
            total_rows = None
            for h in range(2):
                for yh in range(2):
                    start = (first - base) * FR + 4 * yh + 2 * pair + h
                    z0 = ref[pl.ds(start, rows, stride=16), :]
                    z1 = ref[pl.ds(start + 8, rows, stride=16), :]
                    part = exact_dot(z0 + z1, mats[h][yh])
                    total_rows = part if total_rows is None else total_rows + part
            put(means, pair * 19 * 8 + 8 * first, total_rows)


def tail_kernel(
    f_first,
    new,
    cornered,
    f_own,
    x_in,
    n_in,
    cmid,
    fine_out,
    cpassed,
    halo,
    cfaces,
    clayers,
    meta_own,
    sem,
    out_sem,
):
    device, sign = place()
    (fetch,) = fetch_meta(((f_first, meta_own),), sem)
    pieces = (
        (new, 0, 0, 7 * FR),
        (cornered, 0, 7 * FR, 4 * FR),
        (new, 11 * FR, 11 * FR, 8 * FR),
    )
    outs = [
        pltpu.make_async_copy(
            ref.at[pl.ds(source, rows)], fine_out.at[pl.ds(to, rows)], out_sem.at[k]
        )
        for k, (ref, source, to, rows) in enumerate(pieces)
    ]
    for c in outs:
        c.start()
    gather_halo(f_own, x_in, n_in, halo)
    fetch.wait()
    sides = CoarseSides(meta_own, device, sign)
    for k in (2, 3):
        sides.face(k, halo, cfaces)
    for k in (4, 5):
        sides.layers(k, halo, clayers, 4)
    for i in range(19):
        a = at(cmid, i * CR, CR)
        g = a
        if i in YP2 or i in YM2:
            cy = 1 if i in YP2 else -1
            k = 2 if cy == 1 else 3
            column = -16 * (5 + YP2.index(i)) if cy == 1 else 112 - 16 * (5 + YM2.index(i))
            side = roll(at(cfaces, k * CR, CR), column, 1)
            g = move_y(a, cy, jnp.where(sides.exists(k, CR), side, a), CB)
        elif i in ZP2 or i in ZM2:
            cz = 1 if i in ZP2 else -1
            k = 4 if cz == 1 else 5
            n = (ZP2 if cz == 1 else ZM2).index(i)
            own = a[:8] if cz == 1 else a[-8:]
            side = jnp.where(sides.exists(k, 8), at(clayers, 8 * n, 8), own)
            g = move_z_coarse(a, cz, side)
        put(cpassed, i * CR, g)
    for c in outs:
        c.wait()


def coarse_last_kernel(
    f_first, cpassed, own, two, x_in, coarse_out, gathered, meta, sem
):
    device, _ = place()
    (fetch,) = fetch_meta(((f_first, meta),), sem)
    put(gathered, 0, own[...])
    put(gathered, K_ROWS, x_in[0:K_ROWS, :])
    put(gathered, 2 * K_ROWS, two[...])
    put(gathered, 3 * K_ROWS, x_in[K_ROWS : 2 * K_ROWS, :])
    coarse_out[...] = cpassed[...]
    _, lane = iotas(8)
    x_half = (lane >> 3) & 1
    fetch.wait()
    for c in range(CB):
        for qy in range(2):
            children = [number(meta, c, M_CHILD + 2 * qy + qx) for qx in range(2)]
            starts, shifts = [], []
            for qx in range(2):
                child = jnp.maximum(children[qx], 0)
                slot = ((child >> 2) ^ device) & 3
                starts.append(slot * K_ROWS + ((child & 3) >> 1) * (19 * 8))
                shifts.append((8 * (qx - (child & 1))) & 127)
            index = jnp.where(x_half == 0, children[0], children[1])
            for i in range(19):
                rows = pl.ds(i * CR + 2 * qy + c, 8, stride=4)
                values = [roll(at(gathered, starts[qx] + 8 * i, 8), shifts[qx], 1) for qx in (0, 1)]
                value = jnp.where(x_half == 0, values[0], values[1])
                coarse_out[rows, :] = jnp.where(index >= 0, value, cpassed[rows, :])


VMEM = pl.BlockSpec(memory_space=pltpu.VMEM)
HBM = pl.BlockSpec(memory_space=pltpu.HBM)


def rows_of(n, dtype=jnp.float32):
    return jax.ShapeDtypeStruct((n, 128), dtype)


def scratch(n, dtype=jnp.float32):
    return pltpu.VMEM((n, 128), dtype)


def call(kernel, name, specs, outs, scratches, out_specs=None):
    return pl.pallas_call(
        kernel,
        name=name,
        in_specs=specs,
        out_specs=out_specs or [VMEM] * len(outs),
        out_shape=outs,
        scratch_shapes=scratches,
        cost_estimate=pl.CostEstimate(flops=1 << 20, bytes_accessed=4 << 20, transcendentals=0),
        compiler_params=pltpu.CompilerParams(vmem_limit_bytes=32 * 1024 * 1024),
    )


def meta_scratch(n=3):
    return [pltpu.SMEM((8, 128), jnp.float32)] * n + [pltpu.SemaphoreType.DMA((n,))]


def exchange(rows, devices, partner):
    return lax.ppermute(rows, AXES, [(i, partner(i)) for i in range(devices)])


def as_rows(cells, directions):
    blocks = cells.shape[0]
    cells = cells.reshape(blocks, directions, R, 128)
    return cells.transpose(1, 2, 0, 3).reshape(directions * R * blocks, 128)


def as_cells(rows, blocks):
    return rows.reshape(19, R, blocks, 128).transpose(2, 0, 1, 3).reshape(blocks, 19, R * 128)


def on_device(fine_pop, coarse_pop, fine_nbr, coarse_nbr, parent, children, solid):
    devices = lax.axis_size(AXES)
    by_one = lambda a: exchange(a, devices, lambda i: i ^ 1)
    by_two = lambda a: exchange(a, devices, lambda i: i ^ 2)
    odd_even = lambda a: exchange(a, devices, lambda i: (((i + 1) ^ 1) - 1) % devices)
    parent = parent.T
    small = lambda a: pltpu.SMEM(a.shape, jnp.int32)
    inputs = (
        as_rows(coarse_pop, 19),
        as_rows(fine_pop, 19),
        as_rows(solid, 1),
        fine_nbr,
        parent,
        coarse_nbr,
        children,
    )

    cpost, e_own, c_own, fine_raw, solid_raw, meta = call(
        coarse_first_kernel,
        "coarse_first",
        [HBM] * 7,
        [
            rows_of(C_ALL),
            rows_of(E_ROWS),
            rows_of(C_ROWS),
            rows_of(F_ALL),
            rows_of(FR, jnp.int32),
            rows_of(8),
        ],
        [
            scratch(C_ALL),
            scratch(CR),
            small(fine_nbr),
            small(parent),
            small(coarse_nbr),
            small(children),
            pltpu.SemaphoreType.DMA((7,)),
        ],
    )(*(pltpu.with_memory_space_constraint(a, pltpu.HBM) for a in inputs))
    e_two = by_two(e_own)
    post, mask, f_own = call(
        fine_first_kernel,
        "fine_first",
        [VMEM] * 4,
        [rows_of(F_ALL), rows_of(FR, jnp.int32), rows_of(F_ROWS)],
        [scratch(FR)],
    )(meta, fine_raw, solid_raw, c_own)

    x_in = by_one(jnp.concatenate([f_own, e_own, e_two]))
    n_in = odd_even(
        jnp.concatenate(
            [
                f_own,
                x_in[EDGES:META],
                e_own[EC_AT:],
                x_in[X_E + EC_AT : X_E2],
                e_two[EC_AT:],
                x_in[X_E2 + EC_AT :],
            ]
        )
    )
    e_halo, ez = call(
        expand_kernel,
        "expand",
        [VMEM] * 4,
        [rows_of(2 * FR), rows_of(80)],
        [scratch(4 * E_ROWS)] + meta_scratch(1),
    )(f_own, e_own, e_two, x_in)
    far_edges, ez = lax.optimization_barrier((n_in[EDGES:META], ez))
    x_late = by_one(far_edges)
    new, fixed, cmid, c2_own = call(
        first_stream_kernel,
        "first_stream",
        [VMEM] * 10,
        [rows_of(F_ALL), rows_of(FB * R), rows_of(C_ALL), rows_of(2 * FR + R)],
        [
            scratch(32),
            scratch(HALO),
            scratch(4 * FR),
            scratch(8 * R),
            scratch(4 * CR),
            scratch(8),
        ]
        + meta_scratch(),
    )(post, mask, f_own, e_own, e_two, x_in, n_in, cpost, e_halo, ez)
    post2, f2_own = call(
        second_collision_kernel,
        "second_collision",
        [VMEM] * 9,
        [rows_of(F_ALL), rows_of(F2_ROWS)],
        [scratch(FR), scratch(5 * R)] + meta_scratch(),
    )(new, mask, f_own, x_in, n_in, x_late, e_halo, fixed, c2_own)

    x2_in = by_one(f2_own)
    n2_in = odd_even(jnp.concatenate([f2_own, x2_in[EDGES:META]]))
    x2_late = by_one(n2_in[EDGES:META])
    (new2,) = call(
        second_stream_kernel,
        "second_stream",
        [VMEM] * 8,
        [rows_of(F_ALL)],
        [scratch(HALO), scratch(4 * FR)] + meta_scratch(1),
    )(post2, mask, f2_own, x2_in, n2_in, e_halo, ez, f_own)
    cornered, means = call(
        coarsen_kernel,
        "coarsen",
        [VMEM] * 10,
        [rows_of(4 * FR), rows_of(K_ROWS)],
        [scratch(FR), scratch(5 * R)] + meta_scratch(),
    )(new2, f2_own, x2_in, n2_in, x2_late, e_halo, fixed, f_own, x_in, n_in)

    k_two = by_two(means)
    fine_out, cpassed = call(
        tail_kernel,
        "tail",
        [VMEM] * 7,
        [rows_of(F_ALL), rows_of(C_ALL)],
        [scratch(3 * EDGES), scratch(4 * CR), scratch(R)]
        + meta_scratch(1)
        + [pltpu.SemaphoreType.DMA((3,))],
        [HBM, VMEM],
    )(f_own, new2, cornered, f2_own, x2_in, n2_in, cmid)
    k_two, cpassed = lax.optimization_barrier((k_two, cpassed))
    k_one = by_one(jnp.concatenate([means, k_two]))
    (coarse_out,) = call(
        coarse_last_kernel,
        "coarse_last",
        [VMEM] * 5,
        [rows_of(C_ALL)],
        [scratch(4 * K_ROWS)] + meta_scratch(1),
    )(f_own, cpassed, means, k_two, k_one)
    return as_cells(fine_out, FB), as_cells(coarse_out, CB)


def solution(mesh):
    rows = P(AXES, None)
    blocks = P(AXES, None, None)
    return jax.shard_map(
        on_device,
        mesh=mesh,
        in_specs=(blocks, blocks, rows, rows, rows, rows, rows),
        out_specs=(blocks, blocks),
        check_vma=False,
    )
```

time: 55.1 us -> 52.3 us (0.949)
  Pallas kernels: 21.5 us -> 15.1 us
  waiting for transfers between devices: 13.5 us -> 16.5 us
  starting transfers between devices: 19 us -> 19.7 us
    pallas_call x9, Pallas kernels: 21.5 us -> 15.1 us  [the longest x1 2.31 us: on_device(): call(first_stream_kernel, 'first_stream', [VMEM] * 10, [rows_of(F_ALL), r...]
    ppermute x9, waiting for transfers between devices: 13.5 us -> 16.5 us  [exchange(): return lax.ppermute(rows, AXES, [(i, partner(i)) for i in range(devices)])]
    ppermute x9, starting transfers between devices: 19 us -> 19.7 us  [exchange(): return lax.ppermute(rows, AXES, [(i, partner(i)) for i in range(devices)])]
  transfers between devices with their start and end apart: 9 -> 9, of which waited for: 6 -> 7; matrix products, arithmetic and copies ran while one was open for 0% -> 0% of each run, Pallas kernels for 21% -> 14%
where the time goes in v3:
time: 52.3 us; the launch traced here: 52.2 us
  starting transfers between devices  19.7 us (38%)
  waiting for transfers between devices  16.5 us (32%)
  Pallas kernels  15.1 us (29%)
  between operations  0.76 us (1%)
    ppermute x9, starting transfers between devices, exchange(): return lax.ppermute(rows, AXES, [(i, partner(i)) for i in range(devices)])  19.7 us
    ppermute x9, waiting for transfers between devices, exchange(): return lax.ppermute(rows, AXES, [(i, partner(i)) for i in range(devices)])  16.5 us
    pallas_call x1, Pallas kernels, on_device(): call(first_stream_kernel, 'first_stream', [VMEM] * 10, [rows_of(F_ALL), r...  2.31 us
    pallas_call x1, Pallas kernels, on_device(): call(second_collision_kernel, 'second_collision', [VMEM] * 9, [rows_of(F_...  2.1 us
    pallas_call x1, Pallas kernels, on_device(): call(coarse_first_kernel, 'coarse_first', [HBM] * 7, [rows_of(C_ALL), row...  1.9 us
    pallas_call x1, Pallas kernels, on_device(): call(coarsen_kernel, 'coarsen', [VMEM] * 10, [rows_of(4 * FR), rows_of(K_...  1.88 us
    pallas_call x1, Pallas kernels, on_device(): call(second_stream_kernel, 'second_stream', [VMEM] * 8, [rows_of(F_ALL)],...  1.76 us
    pallas_call x1, Pallas kernels, on_device(): call(coarse_last_kernel, 'coarse_last', [VMEM] * 5, [rows_of(C_ALL)], [sc...  1.67 us
  transfers between devices with their start and end apart: 9, of which 7 were waited for; matrix products, arithmetic and copies ran while one was open for 0% of the time, Pallas kernels for 14%

profile of v3, /device:TPU:1, one launch (start us, length us, event | category | flops | bytes accessed | tf_op | source)
XLA Modules:
  0.0 52.2 jit_solution(3887496160699938450)
XLA Ops:
  0.6 1.9 %coarse_first.1 = (f32[1216,128]{1,0:T(8,128)S(1)}, f32[200,128]{1,0:T(8,128)S(1)}, f32[264,128]{1,0:T(8,128)S(1)}, f32[2432,128]{1,0:T(8,128)S(1)}, s32[128,128]{1,0:T(8,128)S(1)}, /*index=5*/f32[8,128]{1,0:T(8,128)S(1)}) custom-call(f32[1216,128]{1,0:T(8,128)} %bitcast.27, f32[2432,128]{1,0:T(8,128)} %bitcast.26, s32[128,128]{1,0:T(8,128)} %bitcast.29, ...), custom_call_target="tpu_custom_call" | custom-call | flops 1048576 | bytes 4194304 | tf_op jit(solution)/shard_map/coarse_first/pallas_call | solution.py:944
  2.5 2.2 %collective-permute-start = (f32[200,128]{1,0:T(8,128)S(1)}, f32[200,128]{1,0:T(8,128)S(1)}, u32[]{:S(2)}, u32[]{:S(2)}) collective-permute-start(f32[200,128]{1,0:T(8,128)S(1)} %get-tuple-element.34.e_own), channel_id=1, source_target_pairs={{0,2},{1,3},{2,0},{3,1},{4,6},{5,7},{6,4},{7,5},{8,10},{9,11},{10,... | collective-permute-start | bytes 307208 | tf_op jit(solution)/shard_map/ppermute | solution.py:914
  4.7 1.3 %fine_first.1 = (f32[2432,128]{1,0:T(8,128)S(1)}, s32[128,128]{1,0:T(8,128)S(1)}, f32[328,128]{1,0:T(8,128)S(1)}) custom-call(f32[8,128]{1,0:T(8,128)S(1)} %get-tuple-element.27.meta, f32[2432,128]{1,0:T(8,128)S(1)} %get-tuple-element.28.pop, s32[128,128]{1,0:T(8,128)S(1)} %get-tuple-element.29.solid, f32[264,128]{1,0:T(8,128)S(1)} %get-tuple-element.30.coarse), custom_call_target="tpu_custom_call" | custom-call | flops 1048576 | bytes 4194304 | tf_op jit(solution)/shard_map/fine_first/pallas_call | solution.py:967
  6.0 0.8 %collective-permute-done.e_two = f32[200,128]{1,0:T(8,128)S(1)} collective-permute-done((f32[200,128]{1,0:T(8,128)S(1)}, f32[200,128]{1,0:T(8,128)S(1)}, u32[]{:S(2)}, u32[]{:S(2)}) %collective-permute-start) | collective-permute-done | bytes 102432 | tf_op jit(solution)/shard_map/ppermute | solution.py:914
  6.8 2.0 %collective-permute-start.1 = (f32[728,128]{1,0:T(8,128)S(1)}, f32[728,128]{1,0:T(8,128)S(1)}, u32[]{:S(2)}, u32[]{:S(2)}) collective-permute-start(f32[728,128]{1,0:T(8,128)S(1)} %pad_maximum_fusion), channel_id=1, source_target_pairs={{0,1},{1,0},{2,3},{3,2},{4,5},{5,4},{6,7},{7,6},{8,9},{9,8},{10,11... | collective-permute-start | bytes 1118216 | tf_op jit(solution)/shard_map/ppermute | solution.py:914
  8.8 1.3 %collective-permute-done.1.x_in.x_first = f32[728,128]{1,0:T(8,128)S(1)} collective-permute-done((f32[728,128]{1,0:T(8,128)S(1)}, f32[728,128]{1,0:T(8,128)S(1)}, u32[]{:S(2)}, u32[]{:S(2)}) %collective-permute-start.1) | collective-permute-done | bytes 372768 | tf_op jit(solution)/shard_map/ppermute | solution.py:914
  10.2 1.7 %collective-permute-start.2 = (f32[392,128]{1,0:T(8,128)S(1)}, f32[392,128]{1,0:T(8,128)S(1)}, u32[]{:S(2)}, u32[]{:S(2)}) collective-permute-start(f32[392,128]{1,0:T(8,128)S(1)} %constant_dynamic-update-slice_fusion), channel_id=1, source_target_pairs={{0,127},{1,2},{2,1},{3,4},{4,3},{5,6},{6,5},{7,8},{8,7},{9,10},{10... | collective-permute-start | bytes 602120 | tf_op jit(solution)/shard_map/ppermute | solution.py:914
  11.9 1.1 %expand.1 = (f32[256,128]{1,0:T(8,128)S(1)}, f32[80,128]{1,0:T(8,128)S(1)}) custom-call(f32[328,128]{1,0:T(8,128)S(1)} %get-tuple-element.31.f_own.f_first, f32[200,128]{1,0:T(8,128)S(1)} %get-tuple-element.34.e_own, f32[200,128]{1,0:T(8,128)S(1)} %collective-permute-done.e_two, f32[728,128]{1,0:T(8,128)S(1)} %collective-permute-done.1.x_in.x_first), custom_call_target="tpu_custom_call" | custom-call | flops 1048576 | bytes 4194304 | tf_op jit(solution)/shard_map/expand/pallas_call | solution.py:988
  13.0 2.4 %collective-permute-done.2.n_in.n_first = f32[392,128]{1,0:T(8,128)S(1)} collective-permute-done((f32[392,128]{1,0:T(8,128)S(1)}, f32[392,128]{1,0:T(8,128)S(1)}, u32[]{:S(2)}, u32[]{:S(2)}) %collective-permute-start.2) | collective-permute-done | bytes 200736 | tf_op jit(solution)/shard_map/ppermute | solution.py:914
  15.4 7.1 %collective-permute-start.3 = (f32[32,128]{1,0:T(8,128)S(1)}, f32[32,128]{1,0:T(8,128)S(1)}, u32[]{:S(2)}, u32[]{:S(2)}) collective-permute-start(f32[32,128]{1,0:T(8,128)S(1)} %slice.36), channel_id=1, source_target_pairs={{0,1},{1,0},{2,3},{3,2},{4,5},{5,4},{6,7},{7,6},{8,9},{9,8},{10,11... | collective-permute-start | bytes 49160 | tf_op jit(solution)/shard_map/ppermute | solution.py:914
  22.5 2.3 %first_stream.1 = (f32[2432,128]{1,0:T(8,128)S(1)}, f32[128,128]{1,0:T(8,128)S(1)}, f32[1216,128]{1,0:T(8,128)S(1)}, f32[288,128]{1,0:T(8,128)S(1)}) custom-call(f32[2432,128]{1,0:T(8,128)S(1)} %get-tuple-element.32.post, s32[128,128]{1,0:T(8,128)S(1)} %get-tuple-element.33.mask, f32[328,128]{1,0:T(8,128)S(1)} %get-tuple-element.31.f_own.f_first, ...), custom_call_target="tpu_custom_call" | custom-call | flops 1048576 | bytes 4194304 | tf_op jit(solution)/shard_map/first_stream/pallas_call | solution.py:997
  24.8 0.0 collective-permute-done.3.x_late
  24.8 2.1 %second_collision.1 = (f32[2432,128]{1,0:T(8,128)S(1)}, f32[320,128]{1,0:T(8,128)S(1)}) custom-call(f32[2432,128]{1,0:T(8,128)S(1)} %get-tuple-element.39.new, s32[128,128]{1,0:T(8,128)S(1)} %get-tuple-element.33.mask, f32[328,128]{1,0:T(8,128)S(1)} %get-tuple-element.31.f_own.f_first, f32[728,128]{1,0:T(8,128)S(1)} %collective-permute-done.1.x_in.x_first, ...), custom_call_target="tpu_custom_call" | custom-call | flops 1048576 | bytes 4194304 | tf_op jit(solution)/shard_map/second_collision/pallas_call | solution.py:1012
  27.0 0.1 collective-permute-start.4
  27.0 1.4 %collective-permute-done.4.x_in = f32[320,128]{1,0:T(8,128)S(1)} collective-permute-done((f32[320,128]{1,0:T(8,128)S(1)}, f32[320,128]{1,0:T(8,128)S(1)}, u32[]{:S(2)}, u32[]{:S(2)}) %collective-permute-start.4) | collective-permute-done | bytes 163872 | tf_op jit(solution)/shard_map/ppermute | solution.py:914
  28.4 0.1 collective-permute-start.5
  28.5 4.9 %collective-permute-done.5.n_in = f32[352,128]{1,0:T(8,128)S(1)} collective-permute-done((f32[352,128]{1,0:T(8,128)S(1)}, f32[352,128]{1,0:T(8,128)S(1)}, u32[]{:S(2)}, u32[]{:S(2)}) %collective-permute-start.5) | collective-permute-done | bytes 180256 | tf_op jit(solution)/shard_map/ppermute | solution.py:914
  33.4 5.6 %collective-permute-start.6 = (f32[32,128]{1,0:T(8,128)S(1)}, f32[32,128]{1,0:T(8,128)S(1)}, u32[]{:S(2)}, u32[]{:S(2)}) collective-permute-start(f32[32,128]{1,0:T(8,128)S(1)} %slice.38), channel_id=1, source_target_pairs={{0,1},{1,0},{2,3},{3,2},{4,5},{5,4},{6,7},{7,6},{8,9},{9,8},{10,11... | collective-permute-start | bytes 49160 | tf_op jit(solution)/shard_map/ppermute | solution.py:914
  39.0 1.8 %second_stream.1.new = f32[2432,128]{1,0:T(8,128)S(1)} custom-call(f32[2432,128]{1,0:T(8,128)S(1)} %get-tuple-element.43.post, s32[128,128]{1,0:T(8,128)S(1)} %get-tuple-element.33.mask, f32[320,128]{1,0:T(8,128)S(1)} %get-tuple-element.44.f_own, f32[320,128]{1,0:T(8,128)S(1)} %collective-permute-done.4.x_in, f32[352,128]{1,0:T(8,128)S(1)} %collective-permute-done.5.n_in, ...), custom_call_target="tpu_custom_call" | custom-call | flops 1048576 | bytes 4194304 | tf_op jit(solution)/shard_map/second_stream/pallas_call | solution.py:1023
  40.8 0.0 collective-permute-done.6.x_late
  40.8 1.9 %coarsen.1 = (f32[512,128]{1,0:T(8,128)S(1)}, f32[304,128]{1,0:T(8,128)S(1)}) custom-call(f32[2432,128]{1,0:T(8,128)S(1)} %second_stream.1.new, f32[320,128]{1,0:T(8,128)S(1)} %get-tuple-element.44.f_own, f32[320,128]{1,0:T(8,128)S(1)} %collective-permute-done.4.x_in, f32[352,128]{1,0:T(8,128)S(1)} %collective-permute-done.5.n_in, ...), custom_call_target="tpu_custom_call" | custom-call | flops 1048576 | bytes 4194304 | tf_op jit(solution)/shard_map/coarsen/pallas_call | solution.py:1030
  42.7 0.1 collective-permute-start.7
  42.8 1.1 %tail.1 = (f32[2432,128]{1,0:T(8,128)}, f32[1216,128]{1,0:T(8,128)S(1)}) custom-call(f32[328,128]{1,0:T(8,128)S(1)} %get-tuple-element.31.f_own.f_first, f32[2432,128]{1,0:T(8,128)S(1)} %second_stream.1.new, f32[512,128]{1,0:T(8,128)S(1)} %get-tuple-element.45.cornered, f32[320,128]{1,0:T(8,128)S(1)} %get-tuple-element.44.f_own, ...), custom_call_target="tpu_custom_call" | custom-call | flops 1048576 | bytes 4194304 | tf_op jit(solution)/shard_map/tail/pallas_call | solution.py:1039
  43.9 4.6 %collective-permute-done.7.two = f32[304,128]{1,0:T(8,128)S(1)} collective-permute-done((f32[304,128]{1,0:T(8,128)S(1)}, f32[304,128]{1,0:T(8,128)S(1)}, u32[]{:S(2)}, u32[]{:S(2)}) %collective-permute-start.7) | collective-permute-done | bytes 155680 | tf_op jit(solution)/shard_map/ppermute | solution.py:914
  48.4 0.9 %collective-permute-start.8 = (f32[608,128]{1,0:T(8,128)S(1)}, f32[608,128]{1,0:T(8,128)S(1)}, u32[]{:S(2)}, u32[]{:S(2)}) collective-permute-start(f32[608,128]{1,0:T(8,128)S(1)} %pad_maximum_fusion.1), channel_id=1, source_target_pairs={{0,1},{1,0},{2,3},{3,2},{4,5},{5,4},{6,7},{7,6},{8,9},{9,8},{10,11... | collective-permute-start | bytes 933896 | tf_op jit(solution)/shard_map/ppermute | solution.py:914
  49.3 1.2 %collective-permute-done.8.x_in = f32[608,128]{1,0:T(8,128)S(1)} collective-permute-done((f32[608,128]{1,0:T(8,128)S(1)}, f32[608,128]{1,0:T(8,128)S(1)}, u32[]{:S(2)}, u32[]{:S(2)}) %collective-permute-start.8) | collective-permute-done | bytes 311328 | tf_op jit(solution)/shard_map/ppermute | solution.py:914
  50.5 1.7 %coarse_last.1 = f32[1216,128]{1,0:T(8,128)} custom-call(f32[328,128]{1,0:T(8,128)S(1)} %get-tuple-element.31.f_own.f_first, f32[1216,128]{1,0:T(8,128)S(1)} %get-tuple-element.50.cpassed, f32[304,128]{1,0:T(8,128)S(1)} %get-tuple-element.48.own, f32[304,128]{1,0:T(8,128)S(1)} %collective-permute-done.7.two, f32[608,128]{1,0:T(8,128)S(1)} %collective-permute-done.8.x_in), custom_call_target="tpu_custom_call" | custom-call | flops 1048576 | bytes 4194304 | tf_op jit(solution)/shard_map/coarse_last/pallas_call | solution.py:1051
  (12 shorter events, 0.1 us)
Async XLA Ops:
  2.5 4.3 %collective-permute-start = (f32[200,128]{1,0:T(8,128)S(1)}, f32[200,128]{1,0:T(8,128)S(1)}, u32[]{:S(2)}, u32[]{:S(2)}) collective-permute-start(f32[200,128]{1,0:T(8,128)S(1)} %get-tuple-element.34.e_own), channel_id=1, source_target_pairs={{0,2},{1,3},{2,0},{3,1},{4,6},{5,7},{6,4},{7,5},{8,10},{9,11},{10,... | collective-permute-start | bytes 307208 | tf_op jit(solution)/shard_map/ppermute | solution.py:914
  6.8 3.3 %collective-permute-start.1 = (f32[728,128]{1,0:T(8,128)S(1)}, f32[728,128]{1,0:T(8,128)S(1)}, u32[]{:S(2)}, u32[]{:S(2)}) collective-permute-start(f32[728,128]{1,0:T(8,128)S(1)} %pad_maximum_fusion), channel_id=1, source_target_pairs={{0,1},{1,0},{2,3},{3,2},{4,5},{5,4},{6,7},{7,6},{8,9},{9,8},{10,11... | collective-permute-start | bytes 1118216 | tf_op jit(solution)/shard_map/ppermute | solution.py:914
  10.2 5.2 %collective-permute-start.2 = (f32[392,128]{1,0:T(8,128)S(1)}, f32[392,128]{1,0:T(8,128)S(1)}, u32[]{:S(2)}, u32[]{:S(2)}) collective-permute-start(f32[392,128]{1,0:T(8,128)S(1)} %constant_dynamic-update-slice_fusion), channel_id=1, source_target_pairs={{0,127},{1,2},{2,1},{3,4},{4,3},{5,6},{6,5},{7,8},{8,7},{9,10},{10... | collective-permute-start | bytes 602120 | tf_op jit(solution)/shard_map/ppermute | solution.py:914
  15.4 9.5 %collective-permute-start.3 = (f32[32,128]{1,0:T(8,128)S(1)}, f32[32,128]{1,0:T(8,128)S(1)}, u32[]{:S(2)}, u32[]{:S(2)}) collective-permute-start(f32[32,128]{1,0:T(8,128)S(1)} %slice.36), channel_id=1, source_target_pairs={{0,1},{1,0},{2,3},{3,2},{4,5},{5,4},{6,7},{7,6},{8,9},{9,8},{10,11... | collective-permute-start | bytes 49160 | tf_op jit(solution)/shard_map/ppermute | solution.py:914
  27.0 1.5 %collective-permute-start.4 = (f32[320,128]{1,0:T(8,128)S(1)}, f32[320,128]{1,0:T(8,128)S(1)}, u32[]{:S(2)}, u32[]{:S(2)}) collective-permute-start(f32[320,128]{1,0:T(8,128)S(1)} %get-tuple-element.44.f_own), channel_id=1, source_target_pairs={{0,1},{1,0},{2,3},{3,2},{4,5},{5,4},{6,7},{7,6},{8,9},{9,8},{10,11... | collective-permute-start | bytes 491528 | tf_op jit(solution)/shard_map/ppermute | solution.py:914
  28.4 5.0 %collective-permute-start.5 = (f32[352,128]{1,0:T(8,128)S(1)}, f32[352,128]{1,0:T(8,128)S(1)}, u32[]{:S(2)}, u32[]{:S(2)}) collective-permute-start(f32[352,128]{1,0:T(8,128)S(1)} %pad_maximum_fusion.2), channel_id=1, source_target_pairs={{0,127},{1,2},{2,1},{3,4},{4,3},{5,6},{6,5},{7,8},{8,7},{9,10},{10... | collective-permute-start | bytes 540680 | tf_op jit(solution)/shard_map/ppermute | solution.py:914
  33.4 7.3 %collective-permute-start.6 = (f32[32,128]{1,0:T(8,128)S(1)}, f32[32,128]{1,0:T(8,128)S(1)}, u32[]{:S(2)}, u32[]{:S(2)}) collective-permute-start(f32[32,128]{1,0:T(8,128)S(1)} %slice.38), channel_id=1, source_target_pairs={{0,1},{1,0},{2,3},{3,2},{4,5},{5,4},{6,7},{7,6},{8,9},{9,8},{10,11... | collective-permute-start | bytes 49160 | tf_op jit(solution)/shard_map/ppermute | solution.py:914
  42.7 5.7 %collective-permute-start.7 = (f32[304,128]{1,0:T(8,128)S(1)}, f32[304,128]{1,0:T(8,128)S(1)}, u32[]{:S(2)}, u32[]{:S(2)}) collective-permute-start(f32[304,128]{1,0:T(8,128)S(1)} %get-tuple-element.48.own), channel_id=1, source_target_pairs={{0,2},{1,3},{2,0},{3,1},{4,6},{5,7},{6,4},{7,5},{8,10},{9,11},{10,... | collective-permute-start | bytes 466952 | tf_op jit(solution)/shard_map/ppermute | solution.py:914
  48.4 2.1 %collective-permute-start.8 = (f32[608,128]{1,0:T(8,128)S(1)}, f32[608,128]{1,0:T(8,128)S(1)}, u32[]{:S(2)}, u32[]{:S(2)}) collective-permute-start(f32[608,128]{1,0:T(8,128)S(1)} %pad_maximum_fusion.1), channel_id=1, source_target_pairs={{0,1},{1,0},{2,3},{3,2},{4,5},{5,4},{6,7},{7,6},{8,9},{9,8},{10,11... | collective-permute-start | bytes 933896 | tf_op jit(solution)/shard_map/ppermute | solution.py:914

commit v4 on v3

--- a/solution.py
+++ b/solution.py
@@ -49,19 +49,18 @@
 F_ALL, C_ALL = 19 * FR, 19 * CR
 PY_AT = FR
 ZS = 2 * FR
-EDGES = ZS + R
+EDGES = ZS + 8
 META = EDGES + R
 F_ROWS = META + 8
-F2_ROWS = META
-EC_AT = 6 * R
+EDGES2 = ZS + R
+F2_ROWS = EDGES2 + R
+N_EC = F_ROWS
+EC_AT = 4 * R + 40
 E_ROWS = EC_AT + 8
-C_ROWS = 2 * FR + 8
 K_ROWS = 2 * 19 * 8
-HALO = 3 * EDGES + 2 * FR
+HALO = 3 * EDGES2 + 2 * FR
 X_E = F_ROWS
 X_E2 = X_E + E_ROWS
-N_EDGE = F_ROWS
-N_EC = N_EDGE + R
 M_PARENT, M_CNBR, M_CHILD = 4, 8, 16
 
 
@@ -219,7 +218,7 @@
     return jnp.concatenate([near[:-8], jnp.where(row >= 4, halo8, near[-8:])], axis=0)
 
 
-def send_faces(post, out, coarse, spot):
+def send_faces(post, out, edges, coarse, spot):
     for h in range(2):
         rows = h * 64
         get = lambda i: at(post, i * FR + rows, 64)
@@ -227,10 +226,13 @@
         put(out, PY_AT + rows, pack_y(get, YP, YM, 0, at(coarse, PY_AT + rows, 64), FB))
         put(spot, rows, pack_edges(get, 64))
     _, lane = iotas()
-    edges = zeros(R)
+    device, _ = place()
+    first = 8 * (device & 1)
+    packed = zeros(R)
     for b in range(FB):
-        edges = jnp.where((lane >> 1) == b, roll(spot[pl.ds(b, R, stride=FB), :], 2 * b, 1), edges)
-    put(out, EDGES, edges)
+        one = roll(spot[pl.ds(b, R, stride=FB), :], first + 2 * b, 1)
+        packed = jnp.where((lane >> 1) == (first >> 1) + b, one, packed)
+    put(out, edges, packed)
 
 
 def place():
@@ -243,9 +245,9 @@
     return meta[row, column].astype(jnp.int32)
 
 
-def fetch_meta(pairs, sem):
+def fetch_meta(pairs, sem, start=META):
     copies = [
-        pltpu.make_async_copy(ref.at[pl.ds(META, 8)], dst, sem.at[k])
+        pltpu.make_async_copy(ref.at[pl.ds(start, 8)], dst, sem.at[k])
         for k, (ref, dst) in enumerate(pairs)
     ]
     for c in copies:
@@ -255,20 +257,13 @@
 
 def coarse_first_kernel(
     pop_hbm,
-    fine_hbm,
-    solid_hbm,
     nbr_hbm,
     parent_hbm,
     cnbr_hbm,
     children_hbm,
-    post,
+    raw,
     e_out,
-    c_out,
-    fine_out,
-    solid_out,
     meta_out,
-    raw,
-    spot,
     nbr,
     parent,
     cnbr,
@@ -284,8 +279,6 @@
                 (parent_hbm, parent),
                 (cnbr_hbm, cnbr),
                 (children_hbm, children),
-                (fine_hbm, fine_out),
-                (solid_hbm, solid_out),
             )
         )
     ]
@@ -308,7 +301,6 @@
         high = jnp.where((lane >> 4) == p, roll(half(YM[p]), 16 * p - 112, 1), high)
     put(e_out, 2 * R, low)
     put(e_out, 3 * R, high)
-    put(e_out, 4 * R, zeros(2 * R))
     for k in range(5):
         e_out[pl.ds(4 * R + 4 * k, 4), :] = raw[pl.ds(ZP[k] * CR, 4), :]
         e_out[pl.ds(4 * R + 20 + 4 * k, 4), :] = raw[pl.ds(ZM[k] * CR + 28, 4), :]
@@ -320,26 +312,8 @@
                 rows = raw[pl.ds(i * CR + (q // 2) * 2 + c, 8, stride=4), :]
                 rows = roll(rows, to - (yq * 16 + 8 * (q % 2) + xq), 1)
                 corner = jnp.where(lane8 == to, rows, corner)
-    put(e_out, EC_AT, corner)
-
-    collide_rows(raw, post, CR, OMEGA_COARSE)
-    get = lambda i: at(post, i * CR, CR)
-    _, wide = iotas(CR)
-    ahead, back = zeros(CR), zeros(CR)
-    for j in range(5):
-        ahead = jnp.where((wide & 15) == 10 + j, roll(get(XP[j]), 10 + j - 15, 1), ahead)
-        back = jnp.where((wide & 15) == 10 + j, roll(get(XM[j]), 10 + j, 1), back)
-    for k, packed in enumerate((ahead, back)):
-        put(spot, 0, packed)
-        for c in range(CB):
-            c_out[pl.ds(2 * c + k, R, stride=FB), :] = spot[pl.ds(c, R, stride=CB), :]
-    put(spot, 0, pack_y(get, YP1, YM1, 5, zeros(CR), CB))
-    for c in range(CB):
-        c_out[pl.ds(PY_AT + c, R, stride=FB), :] = spot[pl.ds(c, R, stride=CB), :]
-        c_out[pl.ds(PY_AT + 2 + c, R, stride=FB), :] = zeros(R)
-    top = roll(at(post, 6 * CR - 8, 8), 4, 0)
-    bottom = roll(at(post, 6 * CR, 8), 4, 0)
-    put(c_out, 2 * FR, jnp.where(row8 < 4, top, bottom))
+    device, _ = place()
+    put(e_out, EC_AT, roll(corner, 32 * (device & 3), 1))
 
     for c in copies[1:]:
         c.wait()
@@ -356,7 +330,49 @@
     put(meta_out, 0, meta)
 
 
-def fine_first_kernel(meta, pop, solid, coarse, post, mask, f_out, spot):
+def fine_first_kernel(
+    meta,
+    raw,
+    pop_hbm,
+    solid_hbm,
+    cpost,
+    post,
+    mask,
+    f_out,
+    pop,
+    solid,
+    coarse,
+    spot,
+    sem,
+):
+    copies = [
+        pltpu.make_async_copy(pop_hbm, pop, sem.at[0]),
+        pltpu.make_async_copy(solid_hbm, solid, sem.at[1]),
+    ]
+    for c in copies:
+        c.start()
+    row8, _ = iotas(8)
+    collide_rows(raw, cpost, CR, OMEGA_COARSE)
+    get = lambda i: at(cpost, i * CR, CR)
+    _, wide = iotas(CR)
+    ahead, back = zeros(CR), zeros(CR)
+    for j in range(5):
+        ahead = jnp.where((wide & 15) == 10 + j, roll(get(XP[j]), 10 + j - 15, 1), ahead)
+        back = jnp.where((wide & 15) == 10 + j, roll(get(XM[j]), 10 + j, 1), back)
+    for k, packed in enumerate((ahead, back)):
+        put(spot, 0, packed)
+        for c in range(CB):
+            coarse[pl.ds(2 * c + k, R, stride=FB), :] = spot[pl.ds(c, R, stride=CB), :]
+    put(spot, 0, pack_y(get, YP1, YM1, 5, zeros(CR), CB))
+    for c in range(CB):
+        coarse[pl.ds(PY_AT + c, R, stride=FB), :] = spot[pl.ds(c, R, stride=CB), :]
+        coarse[pl.ds(PY_AT + 2 + c, R, stride=FB), :] = zeros(R)
+    top = roll(at(cpost, 6 * CR - 8, 8), 4, 0)
+    bottom = roll(at(cpost, 6 * CR, 8), 4, 0)
+    put(coarse, 2 * FR, jnp.where(row8 < 4, top, bottom))
+
+    for c in copies:
+        c.wait()
     s = jnp.where(solid[...] > 0, 1, 0)
     bits = s
     none = jnp.zeros_like(s)
@@ -373,9 +389,8 @@
     put(mask, 0, bits)
     collide_rows(pop, post, FR, OMEGA_FINE, mask)
     put(f_out, ZS, at(coarse, 2 * FR, 8))
-    put(f_out, ZS + 8, zeros(24))
     put(f_out, META, meta[...])
-    send_faces(post, f_out, coarse, spot)
+    send_faces(post, f_out, EDGES, coarse, spot)
 
 
 def onehot(rows, cols, source):
@@ -394,7 +409,9 @@
     return result
 
 
-def expand_kernel(f_own, e_own, e_two, x_in, e_halo, ez, gathered, meta, sem):
+def first_local_kernel(
+    f_own, e_own, e_two, x_in, post, mask, e_halo, ez, local, gathered, meta, sem
+):
     device, _ = place()
     (fetch,) = fetch_meta(((f_own, meta),), sem)
     put(gathered, 0, e_own[...])
@@ -449,61 +466,90 @@
         for h in range(2):
             ez[pl.ds(4 * h + b, 8, stride=8), :] = out[h][:8]
             ez[pl.ds(64 + 4 * h + b, 2, stride=8), :] = out[h][8:10]
-
-
-def gather_halo(own, x_in, n_in, halo):
+    stream_local(post, mask, ez, local)
+
+
+def second_local_kernel(post, mask, ez, local):
+    stream_local(post, mask, ez, local)
+
+
+def gather_halo(own, x_in, n_in, rows, halo):
     for k, ref in enumerate((n_in, own, x_in)):
-        put(halo, k * EDGES, ref[0:EDGES, :])
+        put(halo, k * EDGES2, ref[0:rows, :])
 
 
 def gather_faces(meta, device, sign, e_halo, halo, faces):
-    put(halo, 3 * EDGES, e_halo[...])
+    put(halo, 3 * EDGES2, e_halo[...])
     for k in range(4):
         for b in range(FB):
             n = number(meta, b, k)
             safe = jnp.maximum(n, 0)
             which = jnp.clip(((safe >> 2) - device) * sign + 1, 0, 2)
-            start = jnp.where(n >= 0, which * EDGES + (safe & 3), 3 * EDGES + b)
+            start = jnp.where(n >= 0, which * EDGES2 + (safe & 3), 3 * EDGES2 + b)
             start = start + (PY_AT if k >= 2 else 0)
             faces[pl.ds(k * FR + b, R, stride=FB), :] = halo[pl.ds(start, R, stride=FB), :]
 
 
-def gather_edges(own, x_in, n_in, x_late, relayed, edges):
-    for k, ref in enumerate((n_in, own, x_in)):
-        put(edges, (k + 1) * R, ref[EDGES : EDGES + R, :])
-    put(edges, 0, n_in[pl.ds(relayed, R), :])
-    put(edges, 4 * R, x_late[...])
-
-
-def corners(meta_n, meta_own, meta_x, device, sign, e_halo, edges, fixed, spot):
-    row, lane = iotas()
-    upper = (row & 1) == 1
+def plan_corners(meta_n, meta_own, meta_x, device, sign, e_halo, group, from_n, fixed, spare):
+    _, lane = iotas()
+    for k in range(4):
+        spare[pl.ds(k, 8, stride=4), :] = group
+        spare[pl.ds(R + k, 8, stride=4), :] = from_n
+    near_rows, far_rows = spare[0:R, :], spare[R : 2 * R, :]
+    row8, lane8 = iotas(8)
+    plan = zeros(8)
+
+    def pick(which, row, column):
+        return jnp.where(
+            which == 0,
+            meta_n[row, column],
+            jnp.where(which == 1, meta_own[row, column], meta_x[row, column]),
+        ).astype(jnp.int32)
+
     for b in range(FB):
-        result = at(fixed, b * R)
+        result = zeros(R)
         own_rows = e_halo[pl.ds(PY_AT + b, R, stride=FB), :]
         for side in range(2):
             n = number(meta_own, b, 2 + side)
             safe = jnp.maximum(n, 0)
             which = jnp.clip(((safe >> 2) - device) * sign + 1, 0, 2)
-            row_n = safe & 3
+            p, q = (pick(which, safe & 3, M_PARENT + k) for k in range(2))
+            rows = jnp.where(which == 0, far_rows, near_rows)
             for end in range(2):
                 i = ((7, 10), (9, 8))[side][end]
-                p = (YP, YM)[side].index(i)
-                edge_col = ((0, 1), (1, 0))[side][end]
+                own_column = 16 * (YP, YM)[side].index(i) + 15 * end
+                edge_column = ((0, 1), (1, 0))[side][end]
                 to = 112 * side + 15 * end
-                m = jnp.where(
-                    which == 0,
-                    meta_n[row_n, end],
-                    jnp.where(which == 1, meta_own[row_n, end], meta_x[row_n, end]),
-                ).astype(jnp.int32)
-                m_safe = jnp.maximum(m, 0)
-                slot = jnp.clip(((m_safe >> 2) - device) * sign + 2, 0, 4)
-                shift = (to - (2 * (m_safe & 3) + edge_col)) & 127
-                sent = roll(at(edges, slot * R), shift, 1)
-                own = roll(own_rows, to - (16 * p + 15 * end), 1)
-                value = jnp.where(n < 0, own, sent)
-                change = jnp.logical_or(n < 0, m >= 0)
-                here = (lane == to) & (upper if side else jnp.logical_not(upper)) & change
+                source = 32 * ((p >> 1) & 3) + ((p & 1) * 4 + q) * 4 + 2 * side + end
+                value = jnp.where(
+                    n < 0, roll(own_rows, to - own_column, 1), roll(rows, (to - source) & 127, 1)
+                )
+                result = jnp.where(lane == to, value, result)
+                m = pick(which, safe & 3, end)
+                there = jnp.maximum(m, 0) >> 2
+                far = (there - device) * sign
+                pair = jnp.where(far >= 2, 2, jnp.where(far < 0, 1, 0))
+                column = 16 * pair + 8 * (there & 1) + 2 * (m & 3) + edge_column
+                shift = jnp.where((n >= 0) & (m >= 0), (to - column) & 127, -1)
+                spot = (row8 == b) & (lane8 == 2 * side + end)
+                plan = jnp.where(spot, shift.astype(jnp.float32), plan)
+        put(fixed, b * R, result)
+    return plan
+
+
+def corners(plan, own, x_in, n_in, x_late, at_row, fixed, spot):
+    row, lane = iotas()
+    upper = (row & 1) == 1
+    table = at(own, at_row) + at(x_in, at_row)
+    table = table + roll(at(n_in, at_row), 16, 1) + roll(x_late[...], 32, 1)
+    for b in range(FB):
+        result = at(fixed, b * R)
+        for side in range(2):
+            for end in range(2):
+                to = 112 * side + 15 * end
+                shift = number(plan, b, 2 * side + end)
+                value = roll(table, shift & 127, 1)
+                here = (lane == to) & (upper if side else jnp.logical_not(upper)) & (shift >= 0)
                 result = jnp.where(here, value, result)
         spot[pl.ds(b, R, stride=FB), :] = result
 
@@ -516,40 +562,7 @@
     return jnp.where((lane == column) & (((row // FB) & 1) == upper), corner, cells)
 
 
-def fixed_corners(meta_n, meta_own, meta_x, device, sign, group, from_n, fixed, spare):
-    _, lane = iotas()
-    npart = device - sign
-    for b in range(FB):
-        result = zeros(R)
-        for side in range(2):
-            safe = jnp.maximum(number(meta_own, b, 2 + side), 0)
-            which = jnp.clip(((safe >> 2) - device) * sign + 1, 0, 2)
-            row_n = safe & 3
-            p, q = (
-                jnp.where(
-                    which == 0,
-                    meta_n[row_n, M_PARENT + k],
-                    jnp.where(
-                        which == 1, meta_own[row_n, M_PARENT + k], meta_x[row_n, M_PARENT + k]
-                    ),
-                ).astype(jnp.int32)
-                for k in range(2)
-            )
-            near = ((p >> 1) ^ device) & 3
-            far = ((p >> 1) ^ npart) & 3
-            quad = jnp.where(which == 0, at(from_n, far * 8, 8), at(group, near * 8, 8))
-            base = (2 * b + side) * R
-            for k in range(4):
-                spare[pl.ds(base + k, 8, stride=4), :] = quad
-            rows = at(spare, base)
-            for end in range(2):
-                to = 112 * side + 15 * end
-                source = ((p & 1) * 4 + q) * 4 + 2 * side + end
-                result = jnp.where(lane == to, roll(rows, (to - source) & 127, 1), result)
-        put(fixed, b * R, result)
-
-
-def stream_fine(post, mask, faces, ez, dst):
+def stream_local(post, mask, ez, dst):
     put(dst, 0, at(post, 0, FR))
     for h in range(2):
         bits = at(mask, h * 64, 64)
@@ -560,16 +573,12 @@
             stop = min(h * 64 + 64 - 8 * cz, FR)
             size = stop - start
             g = at(post, i * FR + start, size)
-            if cx == 1:
-                g = move_x(g, 1, roll(at(faces, start, size), -XP.index(i), 1))
-            elif cx == -1:
-                g = move_x(g, -1, roll(at(faces, FR + start, size), 10 - XM.index(i), 1))
-            if cy == 1:
-                side = roll(at(faces, 2 * FR + start, size), cx - 16 * YP.index(i), 1)
-                g = move_y(g, 1, side, FB)
-            elif cy == -1:
-                side = roll(at(faces, 3 * FR + start, size), 112 + cx - 16 * YM.index(i), 1)
-                g = move_y(g, -1, side, FB)
+            if cx:
+                g = roll(g, cx, 1)
+            if cy:
+                _, lane = iotas(size)
+                g = roll(g, 16 * cy, 1)
+                g = jnp.where(lane < 16 if cy == 1 else lane >= 112, swap_halves(g, FB), g)
             if size < 64:
                 k = ZP.index(i) if cz == 1 else 5 + ZM.index(i)
                 layer = at(ez, 8 * k, 8)
@@ -577,6 +586,44 @@
             here = h * 64
             g = jnp.where((bits & (1 << i)) > 0, at(post, OPPOSITE[i] * FR + here, 64), g)
             put(dst, i * FR + here, jnp.where(solid, at(post, i * FR + here, 64), g))
+
+
+def stream_sides(local, faces, dst):
+    for i in range(19):
+        cx, cy, cz = VELOCITIES[i]
+        for h in range(2):
+            here = h * 64
+            g = at(local, i * FR + here, 64)
+            start = max(here - 8 * cz, 0)
+            stop = min(here + 64 - 8 * cz, FR)
+            size = stop - start
+            if not (cx or cy):
+                put(dst, i * FR + here, g)
+                continue
+            layer = None
+            if size < 64:
+                layer = g[:8] if cz == 1 else g[-8:]
+                g = g[8:] if cz == 1 else g[:-8]
+            _, lane = iotas(size)
+            if cx:
+                face, column = (0, -XP.index(i)) if cx == 1 else (FR, 10 - XM.index(i))
+                side = roll(at(faces, face + start, size), column, 1)
+                if cy:
+                    side = roll(side, 16 * cy, 1)
+                    edge = lane < 16 if cy == 1 else lane >= 112
+                    side = jnp.where(edge, swap_halves(side, FB), side)
+                g = jnp.where((lane & 15) == (0 if cx == 1 else 15), side, g)
+            if cy:
+                upper = upper_of(size, FB)
+                if cy == 1:
+                    side = roll(at(faces, 2 * FR + start, size), cx - 16 * YP.index(i), 1)
+                    g = jnp.where((lane < 16) & jnp.logical_not(upper), side, g)
+                else:
+                    side = roll(at(faces, 3 * FR + start, size), 112 + cx - 16 * YM.index(i), 1)
+                    g = jnp.where((lane >= 112) & upper, side, g)
+            if layer is not None:
+                g = jnp.concatenate([layer, g] if cz == 1 else [g, layer], axis=0)
+            put(dst, i * FR + here, g)
 
 
 class CoarseSides:
@@ -587,7 +634,7 @@
             safe = [jnp.maximum(n, 0) for n in index]
             self.has.append(index)
             self.which.append(
-                [jnp.clip(((n >> 1) - device) * sign + 1, 0, 2) * EDGES for n in safe]
+                [jnp.clip(((n >> 1) - device) * sign + 1, 0, 2) * EDGES2 for n in safe]
             )
             self.slot.append([n & 1 for n in safe])
 
@@ -613,22 +660,19 @@
                 ]
 
 
-def first_stream_kernel(
-    post,
-    mask,
+def first_sides_kernel(
+    local,
     f_own,
-    e_own,
-    e_two,
     x_in,
     n_in,
+    group,
     cpost,
     e_halo,
-    ez,
     new,
     fixed,
+    plan,
     cmid,
     c_out,
-    group,
     halo,
     faces,
     spare,
@@ -641,11 +685,7 @@
 ):
     device, sign = place()
     copies = fetch_meta(((n_in, meta_n), (f_own, meta_own), (x_in, meta_x)), sem)
-    put(group, 0, e_own[EC_AT:E_ROWS, :])
-    put(group, 8, x_in[X_E + EC_AT : X_E + E_ROWS, :])
-    put(group, 16, e_two[EC_AT:E_ROWS, :])
-    put(group, 24, x_in[X_E2 + EC_AT : X_E2 + E_ROWS, :])
-    gather_halo(f_own, x_in, n_in, halo)
+    gather_halo(f_own, x_in, n_in, EDGES, halo)
     put(c_out, 0, zeros(2 * FR))
     for c in copies:
         c.wait()
@@ -682,87 +722,41 @@
         bottom = roll(at(cmid, ZM2[k] * CR, 8), 4, 0)
         put(c_out, 2 * FR + 8 * k, jnp.where(row8 < 4, top, bottom))
 
-    fixed_corners(
-        meta_n,
-        meta_own,
-        meta_x,
-        device,
-        sign,
-        group,
-        n_in.at[pl.ds(N_EC, 32)],
-        fixed,
-        spare,
+    from_n = at(n_in, N_EC, 8)
+    plan[...] = plan_corners(
+        meta_n, meta_own, meta_x, device, sign, e_halo, group[...], from_n, fixed, spare
     )
-    stream_fine(post, mask, faces, ez, new)
+    stream_sides(local, faces, new)
 
 
 def second_collision_kernel(
-    new,
-    mask,
-    f_own,
-    x_in,
-    n_in,
-    x_late,
-    e_halo,
-    fixed,
-    coarse,
-    post,
-    f_out,
-    spot,
-    edges,
-    meta_n,
-    meta_own,
-    meta_x,
-    sem,
+    new, mask, f_own, x_in, n_in, x_late, fixed, plan, coarse, post, f_out, spot, plan_s, sem
 ):
-    device, sign = place()
-    copies = fetch_meta(((n_in, meta_n), (f_own, meta_own), (x_in, meta_x)), sem)
-    gather_edges(f_own, x_in, n_in, x_late, N_EDGE, edges)
+    (fetch,) = fetch_meta(((plan, plan_s),), sem, 0)
     put(f_out, ZS, coarse[pl.ds(2 * FR, R), :])
-    for c in copies:
-        c.wait()
-    corners(meta_n, meta_own, meta_x, device, sign, e_halo, edges, fixed, spot)
+    fetch.wait()
+    corners(plan_s, f_own, x_in, n_in, x_late, EDGES, fixed, spot)
     collide_rows(new, post, FR, OMEGA_FINE, mask, spot)
-    send_faces(post, f_out, coarse, spot)
-
-
-def second_stream_kernel(
-    post, mask, f_own, x_in, n_in, e_halo, ez, f_first, new, halo, faces, meta, sem
+    send_faces(post, f_out, EDGES2, coarse, spot)
+
+
+def second_sides_kernel(
+    local, f_own, x_in, n_in, e_halo, f_first, new, halo, faces, meta, sem
 ):
     device, sign = place()
     (fetch,) = fetch_meta(((f_first, meta),), sem)
-    gather_halo(f_own, x_in, n_in, halo)
+    gather_halo(f_own, x_in, n_in, EDGES2, halo)
     fetch.wait()
     gather_faces(meta, device, sign, e_halo, halo, faces)
-    stream_fine(post, mask, faces, ez, new)
+    stream_sides(local, faces, new)
 
 
 def coarsen_kernel(
-    new,
-    f_own,
-    x_in,
-    n_in,
-    x_late,
-    e_halo,
-    fixed,
-    f_first,
-    x_first,
-    n_first,
-    cornered,
-    means,
-    spot,
-    edges,
-    meta_n,
-    meta_own,
-    meta_x,
-    sem,
+    new, f_own, x_in, n_in, x_late, fixed, plan, cornered, means, spot, plan_s, sem
 ):
-    device, sign = place()
-    copies = fetch_meta(((n_first, meta_n), (f_first, meta_own), (x_first, meta_x)), sem)
-    gather_edges(f_own, x_in, n_in, x_late, F2_ROWS, edges)
-    for c in copies:
-        c.wait()
-    corners(meta_n, meta_own, meta_x, device, sign, e_halo, edges, fixed, spot)
+    (fetch,) = fetch_meta(((plan, plan_s),), sem, 0)
+    fetch.wait()
+    corners(plan_s, f_own, x_in, n_in, x_late, EDGES2, fixed, spot)
     for i in range(7, 11):
         put(cornered, (i - 7) * FR, with_corners(at(new, i * FR, FR), i, spot[...]))
 
@@ -823,7 +817,7 @@
     ]
     for c in outs:
         c.start()
-    gather_halo(f_own, x_in, n_in, halo)
+    gather_halo(f_own, x_in, n_in, EDGES2, halo)
     fetch.wait()
     sides = CoarseSides(meta_own, device, sign)
     for k in (2, 3):
@@ -931,109 +925,105 @@
     odd_even = lambda a: exchange(a, devices, lambda i: (((i + 1) ^ 1) - 1) % devices)
     parent = parent.T
     small = lambda a: pltpu.SMEM(a.shape, jnp.int32)
-    inputs = (
-        as_rows(coarse_pop, 19),
-        as_rows(fine_pop, 19),
-        as_rows(solid, 1),
-        fine_nbr,
-        parent,
-        coarse_nbr,
-        children,
-    )
-
-    cpost, e_own, c_own, fine_raw, solid_raw, meta = call(
+    in_hbm = lambda a: pltpu.with_memory_space_constraint(a, pltpu.HBM)
+
+    raw, e_own, meta = call(
         coarse_first_kernel,
         "coarse_first",
-        [HBM] * 7,
+        [HBM] * 5,
+        [rows_of(C_ALL), rows_of(E_ROWS), rows_of(8)],
         [
-            rows_of(C_ALL),
-            rows_of(E_ROWS),
-            rows_of(C_ROWS),
-            rows_of(F_ALL),
-            rows_of(FR, jnp.int32),
-            rows_of(8),
-        ],
-        [
-            scratch(C_ALL),
-            scratch(CR),
             small(fine_nbr),
             small(parent),
             small(coarse_nbr),
             small(children),
-            pltpu.SemaphoreType.DMA((7,)),
+            pltpu.SemaphoreType.DMA((5,)),
         ],
-    )(*(pltpu.with_memory_space_constraint(a, pltpu.HBM) for a in inputs))
+    )(
+        in_hbm(as_rows(coarse_pop, 19)),
+        in_hbm(fine_nbr),
+        in_hbm(parent),
+        in_hbm(coarse_nbr),
+        in_hbm(children),
+    )
     e_two = by_two(e_own)
-    post, mask, f_own = call(
+    cpost, post, mask, f_own = call(
         fine_first_kernel,
         "fine_first",
-        [VMEM] * 4,
-        [rows_of(F_ALL), rows_of(FR, jnp.int32), rows_of(F_ROWS)],
-        [scratch(FR)],
-    )(meta, fine_raw, solid_raw, c_own)
+        [VMEM, VMEM, HBM, HBM],
+        [rows_of(C_ALL), rows_of(F_ALL), rows_of(FR, jnp.int32), rows_of(F_ROWS)],
+        [
+            scratch(F_ALL),
+            scratch(FR, jnp.int32),
+            scratch(2 * FR + 8),
+            scratch(FR),
+            pltpu.SemaphoreType.DMA((2,)),
+        ],
+    )(meta, raw, in_hbm(as_rows(fine_pop, 19)), in_hbm(as_rows(solid, 1)))
 
     x_in = by_one(jnp.concatenate([f_own, e_own, e_two]))
+    group = (
+        e_own[EC_AT:] + x_in[X_E + EC_AT : X_E2] + e_two[EC_AT:] + x_in[X_E2 + EC_AT :]
+    )
     n_in = odd_even(
         jnp.concatenate(
-            [
-                f_own,
-                x_in[EDGES:META],
-                e_own[EC_AT:],
-                x_in[X_E + EC_AT : X_E2],
-                e_two[EC_AT:],
-                x_in[X_E2 + EC_AT :],
-            ]
+            [f_own[:EDGES], f_own[EDGES:META] + x_in[EDGES:META], f_own[META:], group]
         )
     )
-    e_halo, ez = call(
-        expand_kernel,
-        "expand",
-        [VMEM] * 4,
-        [rows_of(2 * FR), rows_of(80)],
-        [scratch(4 * E_ROWS)] + meta_scratch(1),
-    )(f_own, e_own, e_two, x_in)
+    e_halo, ez, local = call(
+        first_local_kernel,
+        "first_local",
+        [VMEM] * 6,
+        [rows_of(2 * FR), rows_of(80), rows_of(F_ALL)],
+        [scratch(4 * E_ROWS + R)] + meta_scratch(1),
+    )(f_own, e_own, e_two, x_in, post, mask)
     far_edges, ez = lax.optimization_barrier((n_in[EDGES:META], ez))
     x_late = by_one(far_edges)
-    new, fixed, cmid, c2_own = call(
-        first_stream_kernel,
-        "first_stream",
-        [VMEM] * 10,
-        [rows_of(F_ALL), rows_of(FB * R), rows_of(C_ALL), rows_of(2 * FR + R)],
+    new, fixed, plan, cmid, c2_own = call(
+        first_sides_kernel,
+        "first_sides",
+        [VMEM] * 7,
         [
-            scratch(32),
-            scratch(HALO),
-            scratch(4 * FR),
-            scratch(8 * R),
-            scratch(4 * CR),
-            scratch(8),
-        ]
+            rows_of(F_ALL),
+            rows_of(FB * R),
+            rows_of(8),
+            rows_of(C_ALL),
+            rows_of(2 * FR + R),
+        ],
+        [scratch(HALO), scratch(4 * FR), scratch(2 * R), scratch(4 * CR), scratch(8)]
         + meta_scratch(),
-    )(post, mask, f_own, e_own, e_two, x_in, n_in, cpost, e_halo, ez)
+    )(local, f_own, x_in, n_in, group, cpost, e_halo)
     post2, f2_own = call(
         second_collision_kernel,
         "second_collision",
         [VMEM] * 9,
         [rows_of(F_ALL), rows_of(F2_ROWS)],
-        [scratch(FR), scratch(5 * R)] + meta_scratch(),
-    )(new, mask, f_own, x_in, n_in, x_late, e_halo, fixed, c2_own)
+        [scratch(FR)] + meta_scratch(1),
+    )(new, mask, f_own, x_in, n_in, x_late, fixed, plan, c2_own)
 
     x2_in = by_one(f2_own)
-    n2_in = odd_even(jnp.concatenate([f2_own, x2_in[EDGES:META]]))
-    x2_late = by_one(n2_in[EDGES:META])
+    n2_in = odd_even(
+        jnp.concatenate([f2_own[:EDGES2], f2_own[EDGES2:] + x2_in[EDGES2:]])
+    )
+    (local2,) = call(
+        second_local_kernel, "second_local", [VMEM] * 3, [rows_of(F_ALL)], []
+    )(post2, mask, ez)
+    far_edges2, local2 = lax.optimization_barrier((n2_in[EDGES2:], local2))
+    x2_late = by_one(far_edges2)
     (new2,) = call(
-        second_stream_kernel,
-        "second_stream",
-        [VMEM] * 8,
+        second_sides_kernel,
+        "second_sides",
+        [VMEM] * 6,
         [rows_of(F_ALL)],
         [scratch(HALO), scratch(4 * FR)] + meta_scratch(1),
-    )(post2, mask, f2_own, x2_in, n2_in, e_halo, ez, f_own)
+    )(local2, f2_own, x2_in, n2_in, e_halo, f_own)
     cornered, means = call(
         coarsen_kernel,
         "coarsen",
-        [VMEM] * 10,
+        [VMEM] * 7,
         [rows_of(4 * FR), rows_of(K_ROWS)],
-        [scratch(FR), scratch(5 * R)] + meta_scratch(),
-    )(new2, f2_own, x2_in, n2_in, x2_late, e_halo, fixed, f_own, x_in, n_in)
+        [scratch(FR)] + meta_scratch(1),
+    )(new2, f2_own, x2_in, n2_in, x2_late, fixed, plan)
 
     k_two = by_two(means)
     fine_out, cpassed = call(
@@ -1041,7 +1031,7 @@
         "tail",
         [VMEM] * 7,
         [rows_of(F_ALL), rows_of(C_ALL)],
-        [scratch(3 * EDGES), scratch(4 * CR), scratch(R)]
+        [scratch(3 * EDGES2), scratch(4 * CR), scratch(R)]
         + meta_scratch(1)
         + [pltpu.SemaphoreType.DMA((3,))],
         [HBM, VMEM],

time: 52.3 us -> 50.3 us (0.962)
  waiting for transfers between devices: 16.5 us -> 13.9 us
  Pallas kernels: 15.1 us -> 16.4 us
  starting transfers between devices: 19.7 us -> 19 us
    ppermute x9, waiting for transfers between devices: 16.5 us -> 13.9 us  [exchange(): return lax.ppermute(rows, AXES, [(i, partner(i)) for i in range(devices)])]
    pallas_call x6 -> x7, Pallas kernels: 10.2 us -> 11.7 us  [the longest x1 2.61 us: on_device(): call(fine_first_kernel, 'fine_first', [VMEM, VMEM, HBM, HBM], [rows_of(C_...]
    ppermute x9, starting transfers between devices: 19.7 us -> 19 us  [exchange(): return lax.ppermute(rows, AXES, [(i, partner(i)) for i in range(devices)])]
  transfers between devices with their start and end apart: 9 -> 9, of which waited for: 7 -> 6; matrix products, arithmetic and copies ran while one was open for 0% -> 0% of each run, Pallas kernels for 14% -> 19%
where the time goes in v4:
time: 50.3 us; the launch traced here: 50.2 us
  starting transfers between devices  19 us (38%)
  Pallas kernels  16.4 us (33%)
  waiting for transfers between devices  13.9 us (28%)
  between operations  0.79 us (2%)
    ppermute x9, starting transfers between devices, exchange(): return lax.ppermute(rows, AXES, [(i, partner(i)) for i in range(devices)])  19 us
    ppermute x9, waiting for transfers between devices, exchange(): return lax.ppermute(rows, AXES, [(i, partner(i)) for i in range(devices)])  13.9 us
    pallas_call x1, Pallas kernels, on_device(): call(fine_first_kernel, 'fine_first', [VMEM, VMEM, HBM, HBM], [rows_of(C_...  2.61 us
    pallas_call x1, Pallas kernels, on_device(): call(first_sides_kernel, 'first_sides', [VMEM] * 7, [rows_of(F_ALL), rows...  2.25 us
    pallas_call x1, Pallas kernels, on_device(): call(second_collision_kernel, 'second_collision', [VMEM] * 9, [rows_of(F_...  1.9 us
    pallas_call x1, Pallas kernels, on_device(): call(coarse_last_kernel, 'coarse_last', [VMEM] * 5, [rows_of(C_ALL)], [sc...  1.67 us
    pallas_call x1, Pallas kernels, on_device(): call(coarsen_kernel, 'coarsen', [VMEM] * 7, [rows_of(4 * FR), rows_of(K_R...  1.6 us
    pallas_call x1, Pallas kernels, on_device(): call(first_local_kernel, 'first_local', [VMEM] * 6, [rows_of(2 * FR), row...  1.5 us
  transfers between devices with their start and end apart: 9, of which 6 were waited for; matrix products, arithmetic and copies ran while one was open for 0% of the time, Pallas kernels for 19%

profile of v4, /device:TPU:1, one launch (start us, length us, event | category | flops | bytes accessed | tf_op | source)
XLA Modules:
  0.0 50.2 jit_solution(8667001060726216941)
XLA Ops:
  0.6 1.4 %coarse_first.1 = (f32[1216,128]{1,0:T(8,128)S(1)}, f32[176,128]{1,0:T(8,128)S(1)}, f32[8,128]{1,0:T(8,128)S(1)}) custom-call(f32[1216,128]{1,0:T(8,128)} %bitcast.27, s32[4,4]{1,0:T(4,128)} %nbr_hbm.1, s32[2,4]{1,0:T(2,128)} %bitcast.30, s32[2,6]{1,0:T(2,128)} %cnbr_hbm.1, s32[2,4]{1,0:T(2,128)} %children_hbm.1), custom_call_target="tpu_custom_call" | custom-call | flops 1048576 | bytes 4194304 | tf_op jit(solution)/shard_map/coarse_first/pallas_call | solution.py:930
  2.1 2.2 %collective-permute-start = (f32[176,128]{1,0:T(8,128)S(1)}, f32[176,128]{1,0:T(8,128)S(1)}, u32[]{:S(2)}, u32[]{:S(2)}) collective-permute-start(f32[176,128]{1,0:T(8,128)S(1)} %get-tuple-element.32.e_own), channel_id=1, source_target_pairs={{0,2},{1,3},{2,0},{3,1},{4,6},{5,7},{6,4},{7,5},{8,10},{9,11},{10,... | collective-permute-start | bytes 270344 | tf_op jit(solution)/shard_map/ppermute | solution.py:908
  4.3 2.6 %fine_first.1 = (f32[1216,128]{1,0:T(8,128)S(1)}, f32[2432,128]{1,0:T(8,128)S(1)}, s32[128,128]{1,0:T(8,128)S(1)}, f32[304,128]{1,0:T(8,128)S(1)}) custom-call(f32[8,128]{1,0:T(8,128)S(1)} %get-tuple-element.29.meta, f32[1216,128]{1,0:T(8,128)S(1)} %get-tuple-element.30.raw, f32[2432,128]{1,0:T(8,128)} %bitcast.26, s32[128,128]{1,0:T(8,128)} %bitcast.29), custom_call_target="tpu_custom_call" | custom-call | flops 1048576 | bytes 4194304 | tf_op jit(solution)/shard_map/fine_first/pallas_call | solution.py:950
  6.9 0.0 collective-permute-done.e_two
  6.9 1.3 %collective-permute-start.1 = (f32[656,128]{1,0:T(8,128)S(1)}, f32[656,128]{1,0:T(8,128)S(1)}, u32[]{:S(2)}, u32[]{:S(2)}) collective-permute-start(f32[656,128]{1,0:T(8,128)S(1)} %pad_maximum_fusion), channel_id=1, source_target_pairs={{0,1},{1,0},{2,3},{3,2},{4,5},{5,4},{6,7},{7,6},{8,9},{9,8},{10,11... | collective-permute-start | bytes 1007624 | tf_op jit(solution)/shard_map/ppermute | solution.py:908
  8.2 1.3 %collective-permute-done.1.x_in = f32[656,128]{1,0:T(8,128)S(1)} collective-permute-done((f32[656,128]{1,0:T(8,128)S(1)}, f32[656,128]{1,0:T(8,128)S(1)}, u32[]{:S(2)}, u32[]{:S(2)}) %collective-permute-start.1) | collective-permute-done | bytes 335904 | tf_op jit(solution)/shard_map/ppermute | solution.py:908
  9.5 1.7 %collective-permute-start.2 = (f32[312,128]{1,0:T(8,128)S(1)}, f32[312,128]{1,0:T(8,128)S(1)}, u32[]{:S(2)}, u32[]{:S(2)}) collective-permute-start(f32[312,128]{1,0:T(8,128)S(1)} %pad_maximum_fusion.3), channel_id=1, source_target_pairs={{0,127},{1,2},{2,1},{3,4},{4,3},{5,6},{6,5},{7,8},{8,7},{9,10},{10... | collective-permute-start | bytes 479240 | tf_op jit(solution)/shard_map/ppermute | solution.py:908
  11.2 1.5 %first_local.1 = (f32[256,128]{1,0:T(8,128)S(1)}, f32[80,128]{1,0:T(8,128)S(1)}, f32[2432,128]{1,0:T(8,128)S(1)}) custom-call(f32[304,128]{1,0:T(8,128)S(1)} %get-tuple-element.31.f_own.f_first, f32[176,128]{1,0:T(8,128)S(1)} %get-tuple-element.32.e_own, f32[176,128]{1,0:T(8,128)S(1)} %collective-permute-done.e_two, ...), custom_call_target="tpu_custom_call" | custom-call | flops 1048576 | bytes 4194304 | tf_op jit(solution)/shard_map/first_local/pallas_call | solution.py:973
  12.7 1.6 %collective-permute-done.2.n_in = f32[312,128]{1,0:T(8,128)S(1)} collective-permute-done((f32[312,128]{1,0:T(8,128)S(1)}, f32[312,128]{1,0:T(8,128)S(1)}, u32[]{:S(2)}, u32[]{:S(2)}) %collective-permute-start.2) | collective-permute-done | bytes 159776 | tf_op jit(solution)/shard_map/ppermute | solution.py:908
  14.3 7.1 %collective-permute-start.3 = (f32[32,128]{1,0:T(8,128)S(1)}, f32[32,128]{1,0:T(8,128)S(1)}, u32[]{:S(2)}, u32[]{:S(2)}) collective-permute-start(f32[32,128]{1,0:T(8,128)S(1)} %slice.56), channel_id=1, source_target_pairs={{0,1},{1,0},{2,3},{3,2},{4,5},{5,4},{6,7},{7,6},{8,9},{9,8},{10,11... | collective-permute-start | bytes 49160 | tf_op jit(solution)/shard_map/ppermute | solution.py:908
  21.4 2.3 %first_sides.1 = (f32[2432,128]{1,0:T(8,128)S(1)}, f32[128,128]{1,0:T(8,128)S(1)}, f32[8,128]{1,0:T(8,128)S(1)}, f32[1216,128]{1,0:T(8,128)S(1)}, f32[288,128]{1,0:T(8,128)S(1)}) custom-call(f32[2432,128]{1,0:T(8,128)S(1)} %get-tuple-element.35.local, f32[304,128]{1,0:T(8,128)S(1)} %get-tuple-element.31.f_own.f_first, ...), custom_call_target="tpu_custom_call" | custom-call | flops 1048576 | bytes 4194304 | tf_op jit(solution)/shard_map/first_sides/pallas_call | solution.py:982
  23.7 0.0 collective-permute-done.3.x_late
  23.7 1.9 %second_collision.1 = (f32[2432,128]{1,0:T(8,128)S(1)}, f32[320,128]{1,0:T(8,128)S(1)}) custom-call(f32[2432,128]{1,0:T(8,128)S(1)} %get-tuple-element.38.new, s32[128,128]{1,0:T(8,128)S(1)} %get-tuple-element.34.mask, f32[304,128]{1,0:T(8,128)S(1)} %get-tuple-element.31.f_own.f_first, f32[656,128]{1,0:T(8,128)S(1)} %collective-permute-done.1.x_in, ...), custom_call_target="tpu_custom_call" | custom-call | flops 1048576 | bytes 4194304 | tf_op jit(solution)/shard_map/second_collision/pallas_call | solution.py:996
  25.6 0.1 collective-permute-start.4
  25.7 1.4 %collective-permute-done.4.x_in = f32[320,128]{1,0:T(8,128)S(1)} collective-permute-done((f32[320,128]{1,0:T(8,128)S(1)}, f32[320,128]{1,0:T(8,128)S(1)}, u32[]{:S(2)}, u32[]{:S(2)}) %collective-permute-start.4) | collective-permute-done | bytes 163872 | tf_op jit(solution)/shard_map/ppermute | solution.py:908
  27.1 0.1 collective-permute-start.5
  27.2 0.8 %second_local.1.local = f32[2432,128]{1,0:T(8,128)S(1)} custom-call(f32[2432,128]{1,0:T(8,128)S(1)} %get-tuple-element.45.post, s32[128,128]{1,0:T(8,128)S(1)} %get-tuple-element.34.mask, f32[80,128]{1,0:T(8,128)S(1)} %get-tuple-element.46.ez), custom_call_target="tpu_custom_call" | custom-call | flops 1048576 | bytes 4194304 | tf_op jit(solution)/shard_map/second_local/pallas_call | solution.py:1008
  28.0 3.9 %collective-permute-done.5.n_in = f32[320,128]{1,0:T(8,128)S(1)} collective-permute-done((f32[320,128]{1,0:T(8,128)S(1)}, f32[320,128]{1,0:T(8,128)S(1)}, u32[]{:S(2)}, u32[]{:S(2)}) %collective-permute-start.5) | collective-permute-done | bytes 163872 | tf_op jit(solution)/shard_map/ppermute | solution.py:908
  31.9 5.6 %collective-permute-start.6 = (f32[32,128]{1,0:T(8,128)S(1)}, f32[32,128]{1,0:T(8,128)S(1)}, u32[]{:S(2)}, u32[]{:S(2)}) collective-permute-start(f32[32,128]{1,0:T(8,128)S(1)} %slice.58), channel_id=1, source_target_pairs={{0,1},{1,0},{2,3},{3,2},{4,5},{5,4},{6,7},{7,6},{8,9},{9,8},{10,11... | collective-permute-start | bytes 49160 | tf_op jit(solution)/shard_map/ppermute | solution.py:908
  37.5 1.5 %second_sides.1.new = f32[2432,128]{1,0:T(8,128)S(1)} custom-call(f32[2432,128]{1,0:T(8,128)S(1)} %second_local.1.local, f32[320,128]{1,0:T(8,128)S(1)} %get-tuple-element.44.f_own, f32[320,128]{1,0:T(8,128)S(1)} %collective-permute-done.4.x_in, f32[320,128]{1,0:T(8,128)S(1)} %collective-permute-done.5.n_in, f32[256,128]{1,0:T(8,128)S(1)} %get-tuple-element.37.e_halo, ...), custom_call_target="tpu_custom_call" | custom-call | flops 1048576 | bytes 4194304 | tf_op jit(solution)/shard_map/second_sides/pallas_call | solution.py:1013
  39.0 0.0 collective-permute-done.6.x_late
  39.0 1.6 %coarsen.1 = (f32[512,128]{1,0:T(8,128)S(1)}, f32[304,128]{1,0:T(8,128)S(1)}) custom-call(f32[2432,128]{1,0:T(8,128)S(1)} %second_sides.1.new, f32[320,128]{1,0:T(8,128)S(1)} %get-tuple-element.44.f_own, f32[320,128]{1,0:T(8,128)S(1)} %collective-permute-done.4.x_in, f32[320,128]{1,0:T(8,128)S(1)} %collective-permute-done.5.n_in, ...), custom_call_target="tpu_custom_call" | custom-call | flops 1048576 | bytes 4194304 | tf_op jit(solution)/shard_map/coarsen/pallas_call | solution.py:1020
  40.6 0.1 collective-permute-start.7
  40.7 1.1 %tail.1 = (f32[2432,128]{1,0:T(8,128)}, f32[1216,128]{1,0:T(8,128)S(1)}) custom-call(f32[304,128]{1,0:T(8,128)S(1)} %get-tuple-element.31.f_own.f_first, f32[2432,128]{1,0:T(8,128)S(1)} %second_sides.1.new, f32[512,128]{1,0:T(8,128)S(1)} %get-tuple-element.49.cornered, f32[320,128]{1,0:T(8,128)S(1)} %get-tuple-element.44.f_own, ...), custom_call_target="tpu_custom_call" | custom-call | flops 1048576 | bytes 4194304 | tf_op jit(solution)/shard_map/tail/pallas_call | solution.py:1029
  41.8 4.6 %collective-permute-done.7.two = f32[304,128]{1,0:T(8,128)S(1)} collective-permute-done((f32[304,128]{1,0:T(8,128)S(1)}, f32[304,128]{1,0:T(8,128)S(1)}, u32[]{:S(2)}, u32[]{:S(2)}) %collective-permute-start.7) | collective-permute-done | bytes 155680 | tf_op jit(solution)/shard_map/ppermute | solution.py:908
  46.4 0.9 %collective-permute-start.8 = (f32[608,128]{1,0:T(8,128)S(1)}, f32[608,128]{1,0:T(8,128)S(1)}, u32[]{:S(2)}, u32[]{:S(2)}) collective-permute-start(f32[608,128]{1,0:T(8,128)S(1)} %pad_maximum_fusion.1), channel_id=1, source_target_pairs={{0,1},{1,0},{2,3},{3,2},{4,5},{5,4},{6,7},{7,6},{8,9},{9,8},{10,11... | collective-permute-start | bytes 933896 | tf_op jit(solution)/shard_map/ppermute | solution.py:908
  47.3 1.2 %collective-permute-done.8.x_in = f32[608,128]{1,0:T(8,128)S(1)} collective-permute-done((f32[608,128]{1,0:T(8,128)S(1)}, f32[608,128]{1,0:T(8,128)S(1)}, u32[]{:S(2)}, u32[]{:S(2)}) %collective-permute-start.8) | collective-permute-done | bytes 311328 | tf_op jit(solution)/shard_map/ppermute | solution.py:908
  48.5 1.7 %coarse_last.1 = f32[1216,128]{1,0:T(8,128)} custom-call(f32[304,128]{1,0:T(8,128)S(1)} %get-tuple-element.31.f_own.f_first, f32[1216,128]{1,0:T(8,128)S(1)} %get-tuple-element.54.cpassed, f32[304,128]{1,0:T(8,128)S(1)} %get-tuple-element.52.own, f32[304,128]{1,0:T(8,128)S(1)} %collective-permute-done.7.two, f32[608,128]{1,0:T(8,128)S(1)} %collective-permute-done.8.x_in), custom_call_target="tpu_custom_call" | custom-call | flops 1048576 | bytes 4194304 | tf_op jit(solution)/shard_map/coarse_last/pallas_call | solution.py:1041
  (12 shorter events, 0.1 us)
Async XLA Ops:
  2.1 4.8 %collective-permute-start = (f32[176,128]{1,0:T(8,128)S(1)}, f32[176,128]{1,0:T(8,128)S(1)}, u32[]{:S(2)}, u32[]{:S(2)}) collective-permute-start(f32[176,128]{1,0:T(8,128)S(1)} %get-tuple-element.32.e_own), channel_id=1, source_target_pairs={{0,2},{1,3},{2,0},{3,1},{4,6},{5,7},{6,4},{7,5},{8,10},{9,11},{10,... | collective-permute-start | bytes 270344 | tf_op jit(solution)/shard_map/ppermute | solution.py:908
  6.9 2.5 %collective-permute-start.1 = (f32[656,128]{1,0:T(8,128)S(1)}, f32[656,128]{1,0:T(8,128)S(1)}, u32[]{:S(2)}, u32[]{:S(2)}) collective-permute-start(f32[656,128]{1,0:T(8,128)S(1)} %pad_maximum_fusion), channel_id=1, source_target_pairs={{0,1},{1,0},{2,3},{3,2},{4,5},{5,4},{6,7},{7,6},{8,9},{9,8},{10,11... | collective-permute-start | bytes 1007624 | tf_op jit(solution)/shard_map/ppermute | solution.py:908
  9.5 4.8 %collective-permute-start.2 = (f32[312,128]{1,0:T(8,128)S(1)}, f32[312,128]{1,0:T(8,128)S(1)}, u32[]{:S(2)}, u32[]{:S(2)}) collective-permute-start(f32[312,128]{1,0:T(8,128)S(1)} %pad_maximum_fusion.3), channel_id=1, source_target_pairs={{0,127},{1,2},{2,1},{3,4},{4,3},{5,6},{6,5},{7,8},{8,7},{9,10},{10... | collective-permute-start | bytes 479240 | tf_op jit(solution)/shard_map/ppermute | solution.py:908
  14.3 9.4 %collective-permute-start.3 = (f32[32,128]{1,0:T(8,128)S(1)}, f32[32,128]{1,0:T(8,128)S(1)}, u32[]{:S(2)}, u32[]{:S(2)}) collective-permute-start(f32[32,128]{1,0:T(8,128)S(1)} %slice.56), channel_id=1, source_target_pairs={{0,1},{1,0},{2,3},{3,2},{4,5},{5,4},{6,7},{7,6},{8,9},{9,8},{10,11... | collective-permute-start | bytes 49160 | tf_op jit(solution)/shard_map/ppermute | solution.py:908
  25.6 1.5 %collective-permute-start.4 = (f32[320,128]{1,0:T(8,128)S(1)}, f32[320,128]{1,0:T(8,128)S(1)}, u32[]{:S(2)}, u32[]{:S(2)}) collective-permute-start(f32[320,128]{1,0:T(8,128)S(1)} %get-tuple-element.44.f_own), channel_id=1, source_target_pairs={{0,1},{1,0},{2,3},{3,2},{4,5},{5,4},{6,7},{7,6},{8,9},{9,8},{10,11... | collective-permute-start | bytes 491528 | tf_op jit(solution)/shard_map/ppermute | solution.py:908
  27.1 4.8 %collective-permute-start.5 = (f32[320,128]{1,0:T(8,128)S(1)}, f32[320,128]{1,0:T(8,128)S(1)}, u32[]{:S(2)}, u32[]{:S(2)}) collective-permute-start(f32[320,128]{1,0:T(8,128)S(1)} %pad_maximum_fusion.2), channel_id=1, source_target_pairs={{0,127},{1,2},{2,1},{3,4},{4,3},{5,6},{6,5},{7,8},{8,7},{9,10},{10... | collective-permute-start | bytes 491528 | tf_op jit(solution)/shard_map/ppermute | solution.py:908
  31.9 7.1 %collective-permute-start.6 = (f32[32,128]{1,0:T(8,128)S(1)}, f32[32,128]{1,0:T(8,128)S(1)}, u32[]{:S(2)}, u32[]{:S(2)}) collective-permute-start(f32[32,128]{1,0:T(8,128)S(1)} %slice.58), channel_id=1, source_target_pairs={{0,1},{1,0},{2,3},{3,2},{4,5},{5,4},{6,7},{7,6},{8,9},{9,8},{10,11... | collective-permute-start | bytes 49160 | tf_op jit(solution)/shard_map/ppermute | solution.py:908
  40.6 5.7 %collective-permute-start.7 = (f32[304,128]{1,0:T(8,128)S(1)}, f32[304,128]{1,0:T(8,128)S(1)}, u32[]{:S(2)}, u32[]{:S(2)}) collective-permute-start(f32[304,128]{1,0:T(8,128)S(1)} %get-tuple-element.52.own), channel_id=1, source_target_pairs={{0,2},{1,3},{2,0},{3,1},{4,6},{5,7},{6,4},{7,5},{8,10},{9,11},{10,... | collective-permute-start | bytes 466952 | tf_op jit(solution)/shard_map/ppermute | solution.py:908
  46.4 2.1 %collective-permute-start.8 = (f32[608,128]{1,0:T(8,128)S(1)}, f32[608,128]{1,0:T(8,128)S(1)}, u32[]{:S(2)}, u32[]{:S(2)}) collective-permute-start(f32[608,128]{1,0:T(8,128)S(1)} %pad_maximum_fusion.1), channel_id=1, source_target_pairs={{0,1},{1,0},{2,3},{3,2},{4,5},{5,4},{6,7},{7,6},{8,9},{9,8},{10,11... | collective-permute-start | bytes 933896 | tf_op jit(solution)/shard_map/ppermute | solution.py:908

commit v5 on v4

--- a/solution.py
+++ b/solution.py
@@ -58,6 +58,7 @@
 EC_AT = 4 * R + 40
 E_ROWS = EC_AT + 8
 K_ROWS = 2 * 19 * 8
+S_ROWS = 2 * 32
 HALO = 3 * EDGES2 + 2 * FR
 X_E = F_ROWS
 X_E2 = X_E + E_ROWS
@@ -469,8 +470,49 @@
     stream_local(post, mask, ez, local)
 
 
-def second_local_kernel(post, mask, ez, local):
+def coarse_means(pieces, means):
+    row = lax.broadcasted_iota(jnp.int32, (128, 128), 0)
+    col = lax.broadcasted_iota(jnp.int32, (128, 128), 1)
+    target = lambda yh, h: (yh * 4 + (row >> 5)) * 16 + ((row & 15) >> 1) + 8 * h
+    mats = [
+        [jnp.where(col == target(yh, h), 0.125, 0.0).astype(jnp.bfloat16) for yh in range(2)]
+        for h in range(2)
+    ]
+    for pair in range(2):
+        for ref, base, first, last in pieces:
+            rows = 8 * (last - first)
+            total_rows = None
+            for h in range(2):
+                for yh in range(2):
+                    start = (first - base) * FR + 4 * yh + 2 * pair + h
+                    z0 = ref[pl.ds(start, rows, stride=16), :]
+                    z1 = ref[pl.ds(start + 8, rows, stride=16), :]
+                    part = exact_dot(z0 + z1, mats[h][yh])
+                    total_rows = part if total_rows is None else total_rows + part
+            put(means, pair * 19 * 8 + 8 * first, total_rows)
+
+
+def pack_side_means(means, out):
+    _, lane = iotas(8)
+    x = lane & 15
+    for pair in range(2):
+        get = lambda i: at(means, pair * 19 * 8 + 8 * i, 8)
+        packed = [zeros(8) for _ in range(4)]
+        for j in range(5):
+            for h in range(2):
+                to = 2 * j + h
+                packed[0] = jnp.where(x == to, roll(get(XP[j]), to - 8 * h, 1), packed[0])
+                packed[1] = jnp.where(x == to, roll(get(XM[j]), to - 8 * h - 7, 1), packed[1])
+            group = (lane >> 4) == j
+            packed[2] = jnp.where(group, roll(get(YP[j]), 16 * j, 1), packed[2])
+            packed[3] = jnp.where(group, roll(get(YM[j]), 16 * j - 112, 1), packed[3])
+        for k in range(4):
+            put(out, pair * 32 + 8 * k, packed[k])
+
+
+def second_local_kernel(post, mask, ez, local, means):
     stream_local(post, mask, ez, local)
+    coarse_means(((local, 0, 0, 19),), means)
 
 
 def gather_halo(own, x_in, n_in, rows, halo):
@@ -752,7 +794,19 @@
 
 
 def coarsen_kernel(
-    new, f_own, x_in, n_in, x_late, fixed, plan, cornered, means, spot, plan_s, sem
+    new,
+    f_own,
+    x_in,
+    n_in,
+    x_late,
+    fixed,
+    plan,
+    cornered,
+    side_means,
+    means,
+    spot,
+    plan_s,
+    sem,
 ):
     (fetch,) = fetch_meta(((plan, plan_s),), sem, 0)
     fetch.wait()
@@ -760,29 +814,8 @@
     for i in range(7, 11):
         put(cornered, (i - 7) * FR, with_corners(at(new, i * FR, FR), i, spot[...]))
 
-    row = lax.broadcasted_iota(jnp.int32, (128, 128), 0)
-    col = lax.broadcasted_iota(jnp.int32, (128, 128), 1)
-    target = lambda yh, h: (yh * 4 + (row >> 5)) * 16 + ((row & 15) >> 1) + 8 * h
-    mats = [
-        [jnp.where(col == target(yh, h), 0.125, 0.0).astype(jnp.bfloat16) for yh in range(2)]
-        for h in range(2)
-    ]
-    for pair in range(2):
-        for ref, base, first, last in (
-            (new, 0, 0, 7),
-            (cornered, 7, 7, 11),
-            (new, 0, 11, 19),
-        ):
-            rows = 8 * (last - first)
-            total_rows = None
-            for h in range(2):
-                for yh in range(2):
-                    start = (first - base) * FR + 4 * yh + 2 * pair + h
-                    z0 = ref[pl.ds(start, rows, stride=16), :]
-                    z1 = ref[pl.ds(start + 8, rows, stride=16), :]
-                    part = exact_dot(z0 + z1, mats[h][yh])
-                    total_rows = part if total_rows is None else total_rows + part
-            put(means, pair * 19 * 8 + 8 * first, total_rows)
+    coarse_means(((new, 0, 0, 7), (cornered, 7, 7, 11), (new, 0, 11, 19)), means)
+    pack_side_means(means, side_means)
 
 
 def tail_kernel(
@@ -846,7 +879,19 @@
 
 
 def coarse_last_kernel(
-    f_first, cpassed, own, two, x_in, coarse_out, gathered, meta, sem
+    f_first,
+    cpassed,
+    own,
+    two,
+    x_in,
+    own_sides,
+    two_sides,
+    x_sides,
+    coarse_out,
+    gathered,
+    sides,
+    meta,
+    sem,
 ):
     device, _ = place()
     (fetch,) = fetch_meta(((f_first, meta),), sem)
@@ -854,24 +899,44 @@
     put(gathered, K_ROWS, x_in[0:K_ROWS, :])
     put(gathered, 2 * K_ROWS, two[...])
     put(gathered, 3 * K_ROWS, x_in[K_ROWS : 2 * K_ROWS, :])
+    put(sides, 0, own_sides[...])
+    put(sides, S_ROWS, x_sides[0:S_ROWS, :])
+    put(sides, 2 * S_ROWS, two_sides[...])
+    put(sides, 3 * S_ROWS, x_sides[S_ROWS : 2 * S_ROWS, :])
     coarse_out[...] = cpassed[...]
     _, lane = iotas(8)
+    x = lane & 15
     x_half = (lane >> 3) & 1
     fetch.wait()
     for c in range(CB):
         for qy in range(2):
             children = [number(meta, c, M_CHILD + 2 * qy + qx) for qx in range(2)]
-            starts, shifts = [], []
+            found = []
             for qx in range(2):
                 child = jnp.maximum(children[qx], 0)
                 slot = ((child >> 2) ^ device) & 3
-                starts.append(slot * K_ROWS + ((child & 3) >> 1) * (19 * 8))
-                shifts.append((8 * (qx - (child & 1))) & 127)
+                pair, h = (child & 3) >> 1, child & 1
+                start = slot * K_ROWS + pair * (19 * 8)
+                layers = [at(sides, slot * S_ROWS + pair * 32 + 8 * k, 8) for k in range(4)]
+                values = []
+                for i in range(19):
+                    value = roll(at(gathered, start + 8 * i, 8), (8 * (qx - h)) & 127, 1)
+                    for k, group in enumerate((XP, XM)):
+                        if i in group:
+                            to = 8 * qx + 7 * k
+                            shift = (to - 2 * group.index(i) - h) & 127
+                            value = jnp.where(x == to, roll(layers[k], shift, 1), value)
+                    for k, group in enumerate((YP, YM)):
+                        if i in group:
+                            shift = (112 * k + 8 * (qx - h) - 16 * group.index(i)) & 127
+                            edge = (lane >> 4) == 7 * k
+                            value = jnp.where(edge, roll(layers[2 + k], shift, 1), value)
+                    values.append(value)
+                found.append(values)
             index = jnp.where(x_half == 0, children[0], children[1])
             for i in range(19):
                 rows = pl.ds(i * CR + 2 * qy + c, 8, stride=4)
-                values = [roll(at(gathered, starts[qx] + 8 * i, 8), shifts[qx], 1) for qx in (0, 1)]
-                value = jnp.where(x_half == 0, values[0], values[1])
+                value = jnp.where(x_half == 0, found[0][i], found[1][i])
                 coarse_out[rows, :] = jnp.where(index >= 0, value, cpassed[rows, :])
 
 
@@ -1005,9 +1070,14 @@
     n2_in = odd_even(
         jnp.concatenate([f2_own[:EDGES2], f2_own[EDGES2:] + x2_in[EDGES2:]])
     )
-    (local2,) = call(
-        second_local_kernel, "second_local", [VMEM] * 3, [rows_of(F_ALL)], []
+    local2, means = call(
+        second_local_kernel,
+        "second_local",
+        [VMEM] * 3,
+        [rows_of(F_ALL), rows_of(K_ROWS)],
+        [],
     )(post2, mask, ez)
+    k_two = by_two(means)
     far_edges2, local2 = lax.optimization_barrier((n2_in[EDGES2:], local2))
     x2_late = by_one(far_edges2)
     (new2,) = call(
@@ -1017,15 +1087,16 @@
         [rows_of(F_ALL)],
         [scratch(HALO), scratch(4 * FR)] + meta_scratch(1),
     )(local2, f2_own, x2_in, n2_in, e_halo, f_own)
-    cornered, means = call(
+    cornered, sides = call(
         coarsen_kernel,
         "coarsen",
         [VMEM] * 7,
-        [rows_of(4 * FR), rows_of(K_ROWS)],
-        [scratch(FR)] + meta_scratch(1),
+        [rows_of(4 * FR), rows_of(S_ROWS)],
+        [scratch(K_ROWS), scratch(FR)] + meta_scratch(1),
     )(new2, f2_own, x2_in, n2_in, x2_late, fixed, plan)
 
-    k_two = by_two(means)
+    k_two, sides = lax.optimization_barrier((k_two, sides))
+    sides_two = by_two(sides)
     fine_out, cpassed = call(
         tail_kernel,
         "tail",
@@ -1036,15 +1107,16 @@
         + [pltpu.SemaphoreType.DMA((3,))],
         [HBM, VMEM],
     )(f_own, new2, cornered, f2_own, x2_in, n2_in, cmid)
-    k_two, cpassed = lax.optimization_barrier((k_two, cpassed))
     k_one = by_one(jnp.concatenate([means, k_two]))
+    sides_two, cpassed, k_one = lax.optimization_barrier((sides_two, cpassed, k_one))
+    sides_one = by_one(jnp.concatenate([sides, sides_two]))
     (coarse_out,) = call(
         coarse_last_kernel,
         "coarse_last",
-        [VMEM] * 5,
+        [VMEM] * 8,
         [rows_of(C_ALL)],
-        [scratch(4 * K_ROWS)] + meta_scratch(1),
-    )(f_own, cpassed, means, k_two, k_one)
+        [scratch(4 * K_ROWS), scratch(4 * S_ROWS)] + meta_scratch(1),
+    )(f_own, cpassed, means, k_two, k_one, sides, sides_two, sides_one)
     return as_cells(fine_out, FB), as_cells(coarse_out, CB)
 
 

time: 50.3 us -> 48.3 us (0.960)
  waiting for transfers between devices: 13.9 us -> 11.7 us
    ppermute x9 -> x11, waiting for transfers between devices: 13.9 us -> 11.7 us  [exchange(): return lax.ppermute(rows, AXES, [(i, partner(i)) for i in range(devices)])]
    ppermute x9 -> x11, starting transfers between devices: 19 us -> 18.7 us  [exchange(): return lax.ppermute(rows, AXES, [(i, partner(i)) for i in range(devices)])]
  transfers between devices with their start and end apart: 9 -> 11, of which waited for: 6 -> 6; matrix products, arithmetic and copies ran while one was open for 0% -> 0% of each run, Pallas kernels for 19% -> 24%
where the time goes in v5:
time: 48.3 us; the launch traced here: 48.2 us
  starting transfers between devices  18.7 us (39%)
  Pallas kernels  16.8 us (35%)
  waiting for transfers between devices  11.7 us (24%)
  between operations  0.82 us (2%)
    ppermute x11, starting transfers between devices, exchange(): return lax.ppermute(rows, AXES, [(i, partner(i)) for i in range(devices)])  18.7 us
    ppermute x11, waiting for transfers between devices, exchange(): return lax.ppermute(rows, AXES, [(i, partner(i)) for i in range(devices)])  11.7 us
    pallas_call x1, Pallas kernels, on_device(): call(fine_first_kernel, 'fine_first', [VMEM, VMEM, HBM, HBM], [rows_of(C_...  2.61 us
    pallas_call x1, Pallas kernels, on_device(): call(first_sides_kernel, 'first_sides', [VMEM] * 7, [rows_of(F_ALL), rows...  2.26 us
    pallas_call x1, Pallas kernels, on_device(): call(second_collision_kernel, 'second_collision', [VMEM] * 9, [rows_of(F_...  1.9 us
    pallas_call x1, Pallas kernels, on_device(): call(coarse_last_kernel, 'coarse_last', [VMEM] * 8, [rows_of(C_ALL)], [sc...  1.84 us
    pallas_call x1, Pallas kernels, on_device(): call(coarsen_kernel, 'coarsen', [VMEM] * 7, [rows_of(4 * FR), rows_of(S_R...  1.74 us
    pallas_call x1, Pallas kernels, on_device(): call(first_local_kernel, 'first_local', [VMEM] * 6, [rows_of(2 * FR), row...  1.5 us
  transfers between devices with their start and end apart: 11, of which 6 were waited for; matrix products, arithmetic and copies ran while one was open for 0% of the time, Pallas kernels for 24%

profile of v5, /device:TPU:1, one launch (start us, length us, event | category | flops | bytes accessed | tf_op | source)
XLA Modules:
  0.0 48.2 jit_solution(7702553651080127826)
XLA Ops:
  0.6 1.4 %coarse_first.1 = (f32[1216,128]{1,0:T(8,128)S(1)}, f32[176,128]{1,0:T(8,128)S(1)}, f32[8,128]{1,0:T(8,128)S(1)}) custom-call(f32[1216,128]{1,0:T(8,128)} %bitcast.27, s32[4,4]{1,0:T(4,128)} %nbr_hbm.1, s32[2,4]{1,0:T(2,128)} %bitcast.30, s32[2,6]{1,0:T(2,128)} %cnbr_hbm.1, s32[2,4]{1,0:T(2,128)} %children_hbm.1), custom_call_target="tpu_custom_call" | custom-call | flops 1048576 | bytes 4194304 | tf_op jit(solution)/shard_map/coarse_first/pallas_call | solution.py:995
  2.1 2.2 %collective-permute-start = (f32[176,128]{1,0:T(8,128)S(1)}, f32[176,128]{1,0:T(8,128)S(1)}, u32[]{:S(2)}, u32[]{:S(2)}) collective-permute-start(f32[176,128]{1,0:T(8,128)S(1)} %get-tuple-element.37.e_own), channel_id=1, source_target_pairs={{0,2},{1,3},{2,0},{3,1},{4,6},{5,7},{6,4},{7,5},{8,10},{9,11},{10,... | collective-permute-start | bytes 270344 | tf_op jit(solution)/shard_map/ppermute | solution.py:973
  4.3 2.6 %fine_first.1 = (f32[1216,128]{1,0:T(8,128)S(1)}, f32[2432,128]{1,0:T(8,128)S(1)}, s32[128,128]{1,0:T(8,128)S(1)}, f32[304,128]{1,0:T(8,128)S(1)}) custom-call(f32[8,128]{1,0:T(8,128)S(1)} %get-tuple-element.34.meta, f32[1216,128]{1,0:T(8,128)S(1)} %get-tuple-element.35.raw, f32[2432,128]{1,0:T(8,128)} %bitcast.26, s32[128,128]{1,0:T(8,128)} %bitcast.29), custom_call_target="tpu_custom_call" | custom-call | flops 1048576 | bytes 4194304 | tf_op jit(solution)/shard_map/fine_first/pallas_call | solution.py:1015
  6.9 0.0 collective-permute-done.e_two
  6.9 1.3 %collective-permute-start.1 = (f32[656,128]{1,0:T(8,128)S(1)}, f32[656,128]{1,0:T(8,128)S(1)}, u32[]{:S(2)}, u32[]{:S(2)}) collective-permute-start(f32[656,128]{1,0:T(8,128)S(1)} %pad_maximum_fusion), channel_id=1, source_target_pairs={{0,1},{1,0},{2,3},{3,2},{4,5},{5,4},{6,7},{7,6},{8,9},{9,8},{10,11... | collective-permute-start | bytes 1007624 | tf_op jit(solution)/shard_map/ppermute | solution.py:973
  8.2 1.3 %collective-permute-done.1.x_in = f32[656,128]{1,0:T(8,128)S(1)} collective-permute-done((f32[656,128]{1,0:T(8,128)S(1)}, f32[656,128]{1,0:T(8,128)S(1)}, u32[]{:S(2)}, u32[]{:S(2)}) %collective-permute-start.1) | collective-permute-done | bytes 335904 | tf_op jit(solution)/shard_map/ppermute | solution.py:973
  9.5 1.7 %collective-permute-start.2 = (f32[312,128]{1,0:T(8,128)S(1)}, f32[312,128]{1,0:T(8,128)S(1)}, u32[]{:S(2)}, u32[]{:S(2)}) collective-permute-start(f32[312,128]{1,0:T(8,128)S(1)} %pad_maximum_fusion.3), channel_id=1, source_target_pairs={{0,127},{1,2},{2,1},{3,4},{4,3},{5,6},{6,5},{7,8},{8,7},{9,10},{10... | collective-permute-start | bytes 479240 | tf_op jit(solution)/shard_map/ppermute | solution.py:973
  11.2 1.5 %first_local.1 = (f32[256,128]{1,0:T(8,128)S(1)}, f32[80,128]{1,0:T(8,128)S(1)}, f32[2432,128]{1,0:T(8,128)S(1)}) custom-call(f32[304,128]{1,0:T(8,128)S(1)} %get-tuple-element.36.f_own.f_first, f32[176,128]{1,0:T(8,128)S(1)} %get-tuple-element.37.e_own, f32[176,128]{1,0:T(8,128)S(1)} %collective-permute-done.e_two, ...), custom_call_target="tpu_custom_call" | custom-call | flops 1048576 | bytes 4194304 | tf_op jit(solution)/shard_map/first_local/pallas_call | solution.py:1038
  12.7 1.6 %collective-permute-done.2.n_in = f32[312,128]{1,0:T(8,128)S(1)} collective-permute-done((f32[312,128]{1,0:T(8,128)S(1)}, f32[312,128]{1,0:T(8,128)S(1)}, u32[]{:S(2)}, u32[]{:S(2)}) %collective-permute-start.2) | collective-permute-done | bytes 159776 | tf_op jit(solution)/shard_map/ppermute | solution.py:973
  14.3 7.1 %collective-permute-start.3 = (f32[32,128]{1,0:T(8,128)S(1)}, f32[32,128]{1,0:T(8,128)S(1)}, u32[]{:S(2)}, u32[]{:S(2)}) collective-permute-start(f32[32,128]{1,0:T(8,128)S(1)} %slice.56), channel_id=1, source_target_pairs={{0,1},{1,0},{2,3},{3,2},{4,5},{5,4},{6,7},{7,6},{8,9},{9,8},{10,11... | collective-permute-start | bytes 49160 | tf_op jit(solution)/shard_map/ppermute | solution.py:973
  21.4 2.3 %first_sides.1 = (f32[2432,128]{1,0:T(8,128)S(1)}, f32[128,128]{1,0:T(8,128)S(1)}, f32[8,128]{1,0:T(8,128)S(1)}, f32[1216,128]{1,0:T(8,128)S(1)}, f32[288,128]{1,0:T(8,128)S(1)}) custom-call(f32[2432,128]{1,0:T(8,128)S(1)} %get-tuple-element.40.local, f32[304,128]{1,0:T(8,128)S(1)} %get-tuple-element.36.f_own.f_first, ...), custom_call_target="tpu_custom_call" | custom-call | flops 1048576 | bytes 4194304 | tf_op jit(solution)/shard_map/first_sides/pallas_call | solution.py:1047
  23.7 0.0 collective-permute-done.3.x_late
  23.7 1.9 %second_collision.1 = (f32[2432,128]{1,0:T(8,128)S(1)}, f32[320,128]{1,0:T(8,128)S(1)}) custom-call(f32[2432,128]{1,0:T(8,128)S(1)} %get-tuple-element.43.new, s32[128,128]{1,0:T(8,128)S(1)} %get-tuple-element.39.mask, f32[304,128]{1,0:T(8,128)S(1)} %get-tuple-element.36.f_own.f_first, f32[656,128]{1,0:T(8,128)S(1)} %collective-permute-done.1.x_in, ...), custom_call_target="tpu_custom_call" | custom-call | flops 1048576 | bytes 4194304 | tf_op jit(solution)/shard_map/second_collision/pallas_call | solution.py:1061
  25.6 0.1 collective-permute-start.4
  25.7 1.4 %collective-permute-done.4.x_in = f32[320,128]{1,0:T(8,128)S(1)} collective-permute-done((f32[320,128]{1,0:T(8,128)S(1)}, f32[320,128]{1,0:T(8,128)S(1)}, u32[]{:S(2)}, u32[]{:S(2)}) %collective-permute-start.4) | collective-permute-done | bytes 163872 | tf_op jit(solution)/shard_map/ppermute | solution.py:973
  27.1 0.1 collective-permute-start.5
  27.2 1.0 %second_local.1 = (f32[2432,128]{1,0:T(8,128)S(1)}, f32[304,128]{1,0:T(8,128)S(1)}) custom-call(f32[2432,128]{1,0:T(8,128)S(1)} %get-tuple-element.50.post, s32[128,128]{1,0:T(8,128)S(1)} %get-tuple-element.39.mask, f32[80,128]{1,0:T(8,128)S(1)} %get-tuple-element.51.ez), custom_call_target="tpu_custom_call" | custom-call | flops 1048576 | bytes 4194304 | tf_op jit(solution)/shard_map/second_local/pallas_call | solution.py:1073
  28.2 0.1 collective-permute-start.7
  28.3 4.9 %collective-permute-done.5.n_in = f32[320,128]{1,0:T(8,128)S(1)} collective-permute-done((f32[320,128]{1,0:T(8,128)S(1)}, f32[320,128]{1,0:T(8,128)S(1)}, u32[]{:S(2)}, u32[]{:S(2)}) %collective-permute-start.5) | collective-permute-done | bytes 163872 | tf_op jit(solution)/shard_map/ppermute | solution.py:973
  33.2 4.3 %collective-permute-start.6 = (f32[32,128]{1,0:T(8,128)S(1)}, f32[32,128]{1,0:T(8,128)S(1)}, u32[]{:S(2)}, u32[]{:S(2)}) collective-permute-start(f32[32,128]{1,0:T(8,128)S(1)} %slice.58), channel_id=1, source_target_pairs={{0,1},{1,0},{2,3},{3,2},{4,5},{5,4},{6,7},{7,6},{8,9},{9,8},{10,11... | collective-permute-start | bytes 49160 | tf_op jit(solution)/shard_map/ppermute | solution.py:973
  37.5 1.5 %second_sides.1.new = f32[2432,128]{1,0:T(8,128)S(1)} custom-call(f32[2432,128]{1,0:T(8,128)S(1)} %get-tuple-element.53.local, f32[320,128]{1,0:T(8,128)S(1)} %get-tuple-element.49.f_own, f32[320,128]{1,0:T(8,128)S(1)} %collective-permute-done.4.x_in, f32[320,128]{1,0:T(8,128)S(1)} %collective-permute-done.5.n_in, f32[256,128]{1,0:T(8,128)S(1)} %get-tuple-element.42.e_halo, ...), custom_call_target="tpu_custom_call" | custom-call | flops 1048576 | bytes 4194304 | tf_op jit(solution)/shard_map/second_sides/pallas_call | solution.py:1083
  39.0 0.0 collective-permute-done.6.x_late
  39.0 1.7 %coarsen.1 = (f32[512,128]{1,0:T(8,128)S(1)}, f32[64,128]{1,0:T(8,128)S(1)}) custom-call(f32[2432,128]{1,0:T(8,128)S(1)} %second_sides.1.new, f32[320,128]{1,0:T(8,128)S(1)} %get-tuple-element.49.f_own, f32[320,128]{1,0:T(8,128)S(1)} %collective-permute-done.4.x_in, f32[320,128]{1,0:T(8,128)S(1)} %collective-permute-done.5.n_in, ...), custom_call_target="tpu_custom_call" | custom-call | flops 1048576 | bytes 4194304 | tf_op jit(solution)/shard_map/coarsen/pallas_call | solution.py:1090
  40.8 0.0 collective-permute-done.7.two
  40.8 0.1 collective-permute-start.9
  40.9 0.1 collective-permute-start.8
  41.0 1.1 %tail.1 = (f32[2432,128]{1,0:T(8,128)}, f32[1216,128]{1,0:T(8,128)S(1)}) custom-call(f32[304,128]{1,0:T(8,128)S(1)} %get-tuple-element.36.f_own.f_first, f32[2432,128]{1,0:T(8,128)S(1)} %second_sides.1.new, f32[512,128]{1,0:T(8,128)S(1)} %get-tuple-element.55.cornered, f32[320,128]{1,0:T(8,128)S(1)} %get-tuple-element.49.f_own, ...), custom_call_target="tpu_custom_call" | custom-call | flops 1048576 | bytes 4194304 | tf_op jit(solution)/shard_map/tail/pallas_call | solution.py:1100
  42.1 1.7 %collective-permute-done.8.two_sides = f32[64,128]{1,0:T(8,128)S(1)} collective-permute-done((f32[64,128]{1,0:T(8,128)S(1)}, f32[64,128]{1,0:T(8,128)S(1)}, u32[]{:S(2)}, u32[]{:S(2)}) %collective-permute-start.8) | collective-permute-done | bytes 32800 | tf_op jit(solution)/shard_map/ppermute | solution.py:973
  43.8 0.0 collective-permute-done.9.x_in
  43.8 1.6 %collective-permute-start.10 = (f32[128,128]{1,0:T(8,128)S(1)}, f32[128,128]{1,0:T(8,128)S(1)}, u32[]{:S(2)}, u32[]{:S(2)}) collective-permute-start(f32[128,128]{1,0:T(8,128)S(1)} %pad_maximum_fusion.4), channel_id=1, source_target_pairs={{0,1},{1,0},{2,3},{3,2},{4,5},{5,4},{6,7},{7,6},{8,9},{9,8},{10,11... | collective-permute-start | bytes 196616 | tf_op jit(solution)/shard_map/ppermute | solution.py:973
  45.4 0.9 %collective-permute-done.10.x_sides = f32[128,128]{1,0:T(8,128)S(1)} collective-permute-done((f32[128,128]{1,0:T(8,128)S(1)}, f32[128,128]{1,0:T(8,128)S(1)}, u32[]{:S(2)}, u32[]{:S(2)}) %collective-permute-start.10) | collective-permute-done | bytes 65568 | tf_op jit(solution)/shard_map/ppermute | solution.py:973
  46.3 1.8 %coarse_last.1 = f32[1216,128]{1,0:T(8,128)} custom-call(f32[304,128]{1,0:T(8,128)S(1)} %get-tuple-element.36.f_own.f_first, f32[1216,128]{1,0:T(8,128)S(1)} %get-tuple-element.63.cpassed, f32[304,128]{1,0:T(8,128)S(1)} %get-tuple-element.58.own, f32[304,128]{1,0:T(8,128)S(1)} %collective-permute-done.7.two, f32[608,128]{1,0:T(8,128)S(1)} %collective-permute-done.9.x_in, ...), custom_call_target="tpu_custom_call" | custom-call | flops 1048576 | bytes 4194304 | tf_op jit(solution)/shard_map/coarse_last/pallas_call | solution.py:1113
  (13 shorter events, 0.1 us)
Async XLA Ops:
  2.1 4.8 %collective-permute-start = (f32[176,128]{1,0:T(8,128)S(1)}, f32[176,128]{1,0:T(8,128)S(1)}, u32[]{:S(2)}, u32[]{:S(2)}) collective-permute-start(f32[176,128]{1,0:T(8,128)S(1)} %get-tuple-element.37.e_own), channel_id=1, source_target_pairs={{0,2},{1,3},{2,0},{3,1},{4,6},{5,7},{6,4},{7,5},{8,10},{9,11},{10,... | collective-permute-start | bytes 270344 | tf_op jit(solution)/shard_map/ppermute | solution.py:973
  6.9 2.5 %collective-permute-start.1 = (f32[656,128]{1,0:T(8,128)S(1)}, f32[656,128]{1,0:T(8,128)S(1)}, u32[]{:S(2)}, u32[]{:S(2)}) collective-permute-start(f32[656,128]{1,0:T(8,128)S(1)} %pad_maximum_fusion), channel_id=1, source_target_pairs={{0,1},{1,0},{2,3},{3,2},{4,5},{5,4},{6,7},{7,6},{8,9},{9,8},{10,11... | collective-permute-start | bytes 1007624 | tf_op jit(solution)/shard_map/ppermute | solution.py:973
  9.5 4.8 %collective-permute-start.2 = (f32[312,128]{1,0:T(8,128)S(1)}, f32[312,128]{1,0:T(8,128)S(1)}, u32[]{:S(2)}, u32[]{:S(2)}) collective-permute-start(f32[312,128]{1,0:T(8,128)S(1)} %pad_maximum_fusion.3), channel_id=1, source_target_pairs={{0,127},{1,2},{2,1},{3,4},{4,3},{5,6},{6,5},{7,8},{8,7},{9,10},{10... | collective-permute-start | bytes 479240 | tf_op jit(solution)/shard_map/ppermute | solution.py:973
  14.3 9.4 %collective-permute-start.3 = (f32[32,128]{1,0:T(8,128)S(1)}, f32[32,128]{1,0:T(8,128)S(1)}, u32[]{:S(2)}, u32[]{:S(2)}) collective-permute-start(f32[32,128]{1,0:T(8,128)S(1)} %slice.56), channel_id=1, source_target_pairs={{0,1},{1,0},{2,3},{3,2},{4,5},{5,4},{6,7},{7,6},{8,9},{9,8},{10,11... | collective-permute-start | bytes 49160 | tf_op jit(solution)/shard_map/ppermute | solution.py:973
  25.6 1.5 %collective-permute-start.4 = (f32[320,128]{1,0:T(8,128)S(1)}, f32[320,128]{1,0:T(8,128)S(1)}, u32[]{:S(2)}, u32[]{:S(2)}) collective-permute-start(f32[320,128]{1,0:T(8,128)S(1)} %get-tuple-element.49.f_own), channel_id=1, source_target_pairs={{0,1},{1,0},{2,3},{3,2},{4,5},{5,4},{6,7},{7,6},{8,9},{9,8},{10,11... | collective-permute-start | bytes 491528 | tf_op jit(solution)/shard_map/ppermute | solution.py:973
  27.1 6.1 %collective-permute-start.5 = (f32[320,128]{1,0:T(8,128)S(1)}, f32[320,128]{1,0:T(8,128)S(1)}, u32[]{:S(2)}, u32[]{:S(2)}) collective-permute-start(f32[320,128]{1,0:T(8,128)S(1)} %pad_maximum_fusion.2), channel_id=1, source_target_pairs={{0,127},{1,2},{2,1},{3,4},{4,3},{5,6},{6,5},{7,8},{8,7},{9,10},{10... | collective-permute-start | bytes 491528 | tf_op jit(solution)/shard_map/ppermute | solution.py:973
  28.2 12.6 %collective-permute-start.7 = (f32[304,128]{1,0:T(8,128)S(1)}, f32[304,128]{1,0:T(8,128)S(1)}, u32[]{:S(2)}, u32[]{:S(2)}) collective-permute-start(f32[304,128]{1,0:T(8,128)S(1)} %get-tuple-element.58.own), channel_id=1, source_target_pairs={{0,2},{1,3},{2,0},{3,1},{4,6},{5,7},{6,4},{7,5},{8,10},{9,11},{10,... | collective-permute-start | bytes 466952 | tf_op jit(solution)/shard_map/ppermute | solution.py:973
  33.2 5.8 %collective-permute-start.6 = (f32[32,128]{1,0:T(8,128)S(1)}, f32[32,128]{1,0:T(8,128)S(1)}, u32[]{:S(2)}, u32[]{:S(2)}) collective-permute-start(f32[32,128]{1,0:T(8,128)S(1)} %slice.58), channel_id=1, source_target_pairs={{0,1},{1,0},{2,3},{3,2},{4,5},{5,4},{6,7},{7,6},{8,9},{9,8},{10,11... | collective-permute-start | bytes 49160 | tf_op jit(solution)/shard_map/ppermute | solution.py:973
  40.8 2.9 %collective-permute-start.9 = (f32[608,128]{1,0:T(8,128)S(1)}, f32[608,128]{1,0:T(8,128)S(1)}, u32[]{:S(2)}, u32[]{:S(2)}) collective-permute-start(f32[608,128]{1,0:T(8,128)S(1)} %pad_maximum_fusion.1), channel_id=1, source_target_pairs={{0,1},{1,0},{2,3},{3,2},{4,5},{5,4},{6,7},{7,6},{8,9},{9,8},{10,11... | collective-permute-start | bytes 933896 | tf_op jit(solution)/shard_map/ppermute | solution.py:973
  40.9 2.8 %collective-permute-start.8 = (f32[64,128]{1,0:T(8,128)S(1)}, f32[64,128]{1,0:T(8,128)S(1)}, u32[]{:S(2)}, u32[]{:S(2)}) collective-permute-start(f32[64,128]{1,0:T(8,128)S(1)} %get-tuple-element.60.own_sides), channel_id=1, source_target_pairs={{0,2},{1,3},{2,0},{3,1},{4,6},{5,7},{6,4},{7,5},{8,10},{9,11},{10,... | collective-permute-start | bytes 98312 | tf_op jit(solution)/shard_map/ppermute | solution.py:973
  43.8 2.5 %collective-permute-start.10 = (f32[128,128]{1,0:T(8,128)S(1)}, f32[128,128]{1,0:T(8,128)S(1)}, u32[]{:S(2)}, u32[]{:S(2)}) collective-permute-start(f32[128,128]{1,0:T(8,128)S(1)} %pad_maximum_fusion.4), channel_id=1, source_target_pairs={{0,1},{1,0},{2,3},{3,2},{4,5},{5,4},{6,7},{7,6},{8,9},{9,8},{10,11... | collective-permute-start | bytes 196616 | tf_op jit(solution)/shard_map/ppermute | solution.py:973

commit v6 on v5

--- a/solution.py
+++ b/solution.py
@@ -59,7 +59,7 @@
 E_ROWS = EC_AT + 8
 K_ROWS = 2 * 19 * 8
 S_ROWS = 2 * 32
-HALO = 3 * EDGES2 + 2 * FR
+HALO = 3 * EDGES2
 X_E = F_ROWS
 X_E2 = X_E + E_ROWS
 M_PARENT, M_CNBR, M_CHILD = 4, 8, 16
@@ -246,9 +246,9 @@
     return meta[row, column].astype(jnp.int32)
 
 
-def fetch_meta(pairs, sem, start=META):
+def fetch_meta(pairs, sem):
     copies = [
-        pltpu.make_async_copy(ref.at[pl.ds(start, 8)], dst, sem.at[k])
+        pltpu.make_async_copy(ref.at[pl.ds(META, 8)], dst, sem.at[k])
         for k, (ref, dst) in enumerate(pairs)
     ]
     for c in copies:
@@ -411,9 +411,9 @@
 
 
 def first_local_kernel(
-    f_own, e_own, e_two, x_in, post, mask, e_halo, ez, local, gathered, meta, sem
+    f_own, e_own, e_two, x_in, post, mask, e_halo, ez, local, route, gathered, meta, sem
 ):
-    device, _ = place()
+    device, sign = place()
     (fetch,) = fetch_meta(((f_own, meta),), sem)
     put(gathered, 0, e_own[...])
     put(gathered, E_ROWS, x_in[X_E : X_E + E_ROWS, :])
@@ -467,6 +467,7 @@
         for h in range(2):
             ez[pl.ds(4 * h + b, 8, stride=8), :] = out[h][:8]
             ez[pl.ds(64 + 4 * h + b, 2, stride=8), :] = out[h][8:10]
+    plan_faces(meta, device, sign, route)
     stream_local(post, mask, ez, local)
 
 
@@ -520,26 +521,43 @@
         put(halo, k * EDGES2, ref[0:rows, :])
 
 
-def gather_faces(meta, device, sign, e_halo, halo, faces):
-    put(halo, 3 * EDGES2, e_halo[...])
+def plan_faces(meta, device, sign, route):
+    row, _ = iotas(8)
     for k in range(4):
+        slot = jnp.zeros((8, 128), jnp.int32)
+        source = jnp.zeros((8, 128), jnp.int32)
         for b in range(FB):
             n = number(meta, b, k)
             safe = jnp.maximum(n, 0)
             which = jnp.clip(((safe >> 2) - device) * sign + 1, 0, 2)
-            start = jnp.where(n >= 0, which * EDGES2 + (safe & 3), 3 * EDGES2 + b)
-            start = start + (PY_AT if k >= 2 else 0)
-            faces[pl.ds(k * FR + b, R, stride=FB), :] = halo[pl.ds(start, R, stride=FB), :]
-
-
-def plan_corners(meta_n, meta_own, meta_x, device, sign, e_halo, group, from_n, fixed, spare):
-    _, lane = iotas()
+            mine = (row & 3) == b
+            slot = jnp.where(mine, safe & 3, slot)
+            source = jnp.where(mine, jnp.where(n >= 0, which, 3), source)
+        put(route, 16 * k, slot + (row & 4))
+        put(route, 16 * k + 8, source)
+
+
+def gather_faces(route, own, x_in, n_in, e_halo, faces):
+    for k in range(4):
+        rows, source = at(route, 16 * k, 8), at(route, 16 * k + 8, 8)
+        first = PY_AT if k >= 2 else 0
+        for v in range(0, FR, 8):
+            n, o, x = (
+                jnp.take_along_axis(at(ref, first + v, 8), rows, axis=0, mode="promise_in_bounds")
+                for ref in (n_in, own, x_in)
+            )
+            side = jnp.where(source == 0, n, jnp.where(source == 1, o, x))
+            put(faces, k * FR + v, jnp.where(source == 3, at(e_halo, first + v, 8), side))
+
+
+def plan_corners(
+    meta_n, meta_own, meta_x, device, sign, e_halo, group, from_n, fixed, plan, spare
+):
+    row, lane = iotas()
     for k in range(4):
         spare[pl.ds(k, 8, stride=4), :] = group
         spare[pl.ds(R + k, 8, stride=4), :] = from_n
     near_rows, far_rows = spare[0:R, :], spare[R : 2 * R, :]
-    row8, lane8 = iotas(8)
-    plan = zeros(8)
 
     def pick(which, row, column):
         return jnp.where(
@@ -550,6 +568,7 @@
 
     for b in range(FB):
         result = zeros(R)
+        source_lanes = jnp.full((R, 128), -1, jnp.int32)
         own_rows = e_halo[pl.ds(PY_AT + b, R, stride=FB), :]
         for side in range(2):
             n = number(meta_own, b, 2 + side)
@@ -572,28 +591,24 @@
                 far = (there - device) * sign
                 pair = jnp.where(far >= 2, 2, jnp.where(far < 0, 1, 0))
                 column = 16 * pair + 8 * (there & 1) + 2 * (m & 3) + edge_column
-                shift = jnp.where((n >= 0) & (m >= 0), (to - column) & 127, -1)
-                spot = (row8 == b) & (lane8 == 2 * side + end)
-                plan = jnp.where(spot, shift.astype(jnp.float32), plan)
-        put(fixed, b * R, result)
-    return plan
+                column = jnp.where((n >= 0) & (m >= 0), column, -1)
+                here = (lane == to) & ((row & 1) == side)
+                source_lanes = jnp.where(here, column, source_lanes)
+        fixed[pl.ds(b, R, stride=FB), :] = result
+        plan[pl.ds(b, R, stride=FB), :] = source_lanes
 
 
 def corners(plan, own, x_in, n_in, x_late, at_row, fixed, spot):
-    row, lane = iotas()
-    upper = (row & 1) == 1
     table = at(own, at_row) + at(x_in, at_row)
     table = table + roll(at(n_in, at_row), 16, 1) + roll(x_late[...], 32, 1)
     for b in range(FB):
-        result = at(fixed, b * R)
-        for side in range(2):
-            for end in range(2):
-                to = 112 * side + 15 * end
-                shift = number(plan, b, 2 * side + end)
-                value = roll(table, shift & 127, 1)
-                here = (lane == to) & (upper if side else jnp.logical_not(upper)) & (shift >= 0)
-                result = jnp.where(here, value, result)
-        spot[pl.ds(b, R, stride=FB), :] = result
+        spot[pl.ds(b, R, stride=FB), :] = table
+    for v in range(0, FR, 8):
+        lanes = at(plan, v, 8)
+        sent = jnp.take_along_axis(
+            at(spot, v, 8), jnp.maximum(lanes, 0), axis=1, mode="promise_in_bounds"
+        )
+        put(spot, v, jnp.where(lanes >= 0, sent, at(fixed, v, 8)))
 
 
 def with_corners(cells, i, corner):
@@ -710,6 +725,7 @@
     group,
     cpost,
     e_halo,
+    route,
     new,
     fixed,
     plan,
@@ -729,9 +745,10 @@
     copies = fetch_meta(((n_in, meta_n), (f_own, meta_own), (x_in, meta_x)), sem)
     gather_halo(f_own, x_in, n_in, EDGES, halo)
     put(c_out, 0, zeros(2 * FR))
+    gather_faces(route, f_own, x_in, n_in, e_halo, faces)
+    stream_sides(local, faces, new)
     for c in copies:
         c.wait()
-    gather_faces(meta_own, device, sign, e_halo, halo, faces)
 
     row8, _ = iotas(8)
     sides = CoarseSides(meta_own, device, sign)
@@ -765,31 +782,22 @@
         put(c_out, 2 * FR + 8 * k, jnp.where(row8 < 4, top, bottom))
 
     from_n = at(n_in, N_EC, 8)
-    plan[...] = plan_corners(
-        meta_n, meta_own, meta_x, device, sign, e_halo, group[...], from_n, fixed, spare
+    plan_corners(
+        meta_n, meta_own, meta_x, device, sign, e_halo, group[...], from_n, fixed, plan, spare
     )
-    stream_sides(local, faces, new)
 
 
 def second_collision_kernel(
-    new, mask, f_own, x_in, n_in, x_late, fixed, plan, coarse, post, f_out, spot, plan_s, sem
+    new, mask, f_own, x_in, n_in, x_late, fixed, plan, coarse, post, f_out, spot
 ):
-    (fetch,) = fetch_meta(((plan, plan_s),), sem, 0)
     put(f_out, ZS, coarse[pl.ds(2 * FR, R), :])
-    fetch.wait()
-    corners(plan_s, f_own, x_in, n_in, x_late, EDGES, fixed, spot)
+    corners(plan, f_own, x_in, n_in, x_late, EDGES, fixed, spot)
     collide_rows(new, post, FR, OMEGA_FINE, mask, spot)
     send_faces(post, f_out, EDGES2, coarse, spot)
 
 
-def second_sides_kernel(
-    local, f_own, x_in, n_in, e_halo, f_first, new, halo, faces, meta, sem
-):
-    device, sign = place()
-    (fetch,) = fetch_meta(((f_first, meta),), sem)
-    gather_halo(f_own, x_in, n_in, EDGES2, halo)
-    fetch.wait()
-    gather_faces(meta, device, sign, e_halo, halo, faces)
+def second_sides_kernel(local, f_own, x_in, n_in, e_halo, route, new, faces):
+    gather_faces(route, f_own, x_in, n_in, e_halo, faces)
     stream_sides(local, faces, new)
 
 
@@ -805,12 +813,8 @@
     side_means,
     means,
     spot,
-    plan_s,
-    sem,
 ):
-    (fetch,) = fetch_meta(((plan, plan_s),), sem, 0)
-    fetch.wait()
-    corners(plan_s, f_own, x_in, n_in, x_late, EDGES2, fixed, spot)
+    corners(plan, f_own, x_in, n_in, x_late, EDGES2, fixed, spot)
     for i in range(7, 11):
         put(cornered, (i - 7) * FR, with_corners(at(new, i * FR, FR), i, spot[...]))
 
@@ -1035,11 +1039,11 @@
             [f_own[:EDGES], f_own[EDGES:META] + x_in[EDGES:META], f_own[META:], group]
         )
     )
-    e_halo, ez, local = call(
+    e_halo, ez, local, route = call(
         first_local_kernel,
         "first_local",
         [VMEM] * 6,
-        [rows_of(2 * FR), rows_of(80), rows_of(F_ALL)],
+        [rows_of(2 * FR), rows_of(80), rows_of(F_ALL), rows_of(64, jnp.int32)],
         [scratch(4 * E_ROWS + R)] + meta_scratch(1),
     )(f_own, e_own, e_two, x_in, post, mask)
     far_edges, ez = lax.optimization_barrier((n_in[EDGES:META], ez))
@@ -1047,23 +1051,23 @@
     new, fixed, plan, cmid, c2_own = call(
         first_sides_kernel,
         "first_sides",
-        [VMEM] * 7,
+        [VMEM] * 8,
         [
             rows_of(F_ALL),
-            rows_of(FB * R),
-            rows_of(8),
+            rows_of(FR),
+            rows_of(FR, jnp.int32),
             rows_of(C_ALL),
             rows_of(2 * FR + R),
         ],
         [scratch(HALO), scratch(4 * FR), scratch(2 * R), scratch(4 * CR), scratch(8)]
         + meta_scratch(),
-    )(local, f_own, x_in, n_in, group, cpost, e_halo)
+    )(local, f_own, x_in, n_in, group, cpost, e_halo, route)
     post2, f2_own = call(
         second_collision_kernel,
         "second_collision",
         [VMEM] * 9,
         [rows_of(F_ALL), rows_of(F2_ROWS)],
-        [scratch(FR)] + meta_scratch(1),
+        [scratch(FR)],
     )(new, mask, f_own, x_in, n_in, x_late, fixed, plan, c2_own)
 
     x2_in = by_one(f2_own)
@@ -1085,14 +1089,14 @@
         "second_sides",
         [VMEM] * 6,
         [rows_of(F_ALL)],
-        [scratch(HALO), scratch(4 * FR)] + meta_scratch(1),
-    )(local2, f2_own, x2_in, n2_in, e_halo, f_own)
+        [scratch(4 * FR)],
+    )(local2, f2_own, x2_in, n2_in, e_halo, route)
     cornered, sides = call(
         coarsen_kernel,
         "coarsen",
         [VMEM] * 7,
         [rows_of(4 * FR), rows_of(S_ROWS)],
-        [scratch(K_ROWS), scratch(FR)] + meta_scratch(1),
+        [scratch(K_ROWS), scratch(FR)],
     )(new2, f2_own, x2_in, n2_in, x2_late, fixed, plan)
 
     k_two, sides = lax.optimization_barrier((k_two, sides))

time: 48.3 us -> 47.2 us (0.977)
  Pallas kernels: 16.8 us -> 14.7 us
  starting transfers between devices: 18.7 us -> 19.7 us
    ppermute x11, starting transfers between devices: 18.7 us -> 19.7 us  [exchange(): return lax.ppermute(rows, AXES, [(i, partner(i)) for i in range(devices)])]
    pallas_call x1, Pallas kernels: 1.74 us -> 1 us  [on_device(): call(coarsen_kernel, 'coarsen', [VMEM] * 7, [rows_of(4 * FR), rows_of(S_R...]
    pallas_call x1, Pallas kernels: 1.5 us -> 0.85 us  [on_device(): call(second_sides_kernel, 'second_sides', [VMEM] * 6, [rows_of(F_ALL)], [...]
    pallas_call x1, Pallas kernels: 1.9 us -> 1.28 us  [on_device(): call(second_collision_kernel, 'second_collision', [VMEM] * 9, [rows_of(F_...]
  transfers between devices with their start and end apart: 11 -> 11, of which waited for: 6 -> 6; matrix products, arithmetic and copies ran while one was open for 0% -> 0% of each run, Pallas kernels for 24% -> 22%
where the time goes in v6:
time: 47.2 us; the launch traced here: 47 us
  starting transfers between devices  19.7 us (42%)
  Pallas kernels  14.7 us (31%)
  waiting for transfers between devices  11.7 us (25%)
  between operations  0.8 us (2%)
    ppermute x11, starting transfers between devices, exchange(): return lax.ppermute(rows, AXES, [(i, partner(i)) for i in range(devices)])  19.7 us
    ppermute x11, waiting for transfers between devices, exchange(): return lax.ppermute(rows, AXES, [(i, partner(i)) for i in range(devices)])  11.7 us
    pallas_call x1, Pallas kernels, on_device(): call(fine_first_kernel, 'fine_first', [VMEM, VMEM, HBM, HBM], [rows_of(C_...  2.61 us
    pallas_call x1, Pallas kernels, on_device(): call(first_sides_kernel, 'first_sides', [VMEM] * 8, [rows_of(F_ALL), rows...  2.14 us
    pallas_call x1, Pallas kernels, on_device(): call(coarse_last_kernel, 'coarse_last', [VMEM] * 8, [rows_of(C_ALL)], [sc...  1.84 us
    pallas_call x1, Pallas kernels, on_device(): call(first_local_kernel, 'first_local', [VMEM] * 6, [rows_of(2 * FR), row...  1.51 us
    pallas_call x1, Pallas kernels, on_device(): call(coarse_first_kernel, 'coarse_first', [HBM] * 5, [rows_of(C_ALL), row...  1.44 us
    pallas_call x1, Pallas kernels, on_device(): call(second_collision_kernel, 'second_collision', [VMEM] * 9, [rows_of(F_...  1.28 us
  transfers between devices with their start and end apart: 11, of which 6 were waited for; matrix products, arithmetic and copies ran while one was open for 0% of the time, Pallas kernels for 22%

profile of v6, /device:TPU:1, one launch (start us, length us, event | category | flops | bytes accessed | tf_op | source)
XLA Modules:
  0.0 47.0 jit_solution(15534769723208341110)
XLA Ops:
  0.6 1.4 %coarse_first.1 = (f32[1216,128]{1,0:T(8,128)S(1)}, f32[176,128]{1,0:T(8,128)S(1)}, f32[8,128]{1,0:T(8,128)S(1)}) custom-call(f32[1216,128]{1,0:T(8,128)} %bitcast.27, s32[4,4]{1,0:T(4,128)} %nbr_hbm.1, s32[2,4]{1,0:T(2,128)} %bitcast.30, s32[2,6]{1,0:T(2,128)} %cnbr_hbm.1, s32[2,4]{1,0:T(2,128)} %children_hbm.1), custom_call_target="tpu_custom_call" | custom-call | flops 1048576 | bytes 4194304 | tf_op jit(solution)/shard_map/coarse_first/pallas_call | solution.py:999
  2.1 2.2 %collective-permute-start = (f32[176,128]{1,0:T(8,128)S(1)}, f32[176,128]{1,0:T(8,128)S(1)}, u32[]{:S(2)}, u32[]{:S(2)}) collective-permute-start(f32[176,128]{1,0:T(8,128)S(1)} %get-tuple-element.38.e_own), channel_id=1, source_target_pairs={{0,2},{1,3},{2,0},{3,1},{4,6},{5,7},{6,4},{7,5},{8,10},{9,11},{10,... | collective-permute-start | bytes 270344 | tf_op jit(solution)/shard_map/ppermute | solution.py:977
  4.3 2.6 %fine_first.1 = (f32[1216,128]{1,0:T(8,128)S(1)}, f32[2432,128]{1,0:T(8,128)S(1)}, s32[128,128]{1,0:T(8,128)S(1)}, f32[304,128]{1,0:T(8,128)S(1)}) custom-call(f32[8,128]{1,0:T(8,128)S(1)} %get-tuple-element.35.meta, f32[1216,128]{1,0:T(8,128)S(1)} %get-tuple-element.36.raw, f32[2432,128]{1,0:T(8,128)} %bitcast.26, s32[128,128]{1,0:T(8,128)} %bitcast.29), custom_call_target="tpu_custom_call" | custom-call | flops 1048576 | bytes 4194304 | tf_op jit(solution)/shard_map/fine_first/pallas_call | solution.py:1019
  6.9 0.0 collective-permute-done.e_two
  6.9 1.3 %collective-permute-start.1 = (f32[656,128]{1,0:T(8,128)S(1)}, f32[656,128]{1,0:T(8,128)S(1)}, u32[]{:S(2)}, u32[]{:S(2)}) collective-permute-start(f32[656,128]{1,0:T(8,128)S(1)} %pad_maximum_fusion), channel_id=1, source_target_pairs={{0,1},{1,0},{2,3},{3,2},{4,5},{5,4},{6,7},{7,6},{8,9},{9,8},{10,11... | collective-permute-start | bytes 1007624 | tf_op jit(solution)/shard_map/ppermute | solution.py:977
  8.2 1.3 %collective-permute-done.1.x_in = f32[656,128]{1,0:T(8,128)S(1)} collective-permute-done((f32[656,128]{1,0:T(8,128)S(1)}, f32[656,128]{1,0:T(8,128)S(1)}, u32[]{:S(2)}, u32[]{:S(2)}) %collective-permute-start.1) | collective-permute-done | bytes 335904 | tf_op jit(solution)/shard_map/ppermute | solution.py:977
  9.5 1.7 %collective-permute-start.2 = (f32[312,128]{1,0:T(8,128)S(1)}, f32[312,128]{1,0:T(8,128)S(1)}, u32[]{:S(2)}, u32[]{:S(2)}) collective-permute-start(f32[312,128]{1,0:T(8,128)S(1)} %pad_maximum_fusion.3), channel_id=1, source_target_pairs={{0,127},{1,2},{2,1},{3,4},{4,3},{5,6},{6,5},{7,8},{8,7},{9,10},{10... | collective-permute-start | bytes 479240 | tf_op jit(solution)/shard_map/ppermute | solution.py:977
  11.2 1.5 %first_local.1 = (f32[256,128]{1,0:T(8,128)S(1)}, f32[80,128]{1,0:T(8,128)S(1)}, f32[2432,128]{1,0:T(8,128)S(1)}, s32[64,128]{1,0:T(8,128)S(1)}) custom-call(f32[304,128]{1,0:T(8,128)S(1)} %get-tuple-element.37.f_own.f_first, f32[176,128]{1,0:T(8,128)S(1)} %get-tuple-element.38.e_own, f32[176,128]{1,0:T(8,128)S(1)} %collective-permute-done.e_two, ...), custom_call_target="tpu_custom_call" | custom-call | flops 1048576 | bytes 4194304 | tf_op jit(solution)/shard_map/first_local/pallas_call | solution.py:1042
  12.8 1.5 %collective-permute-done.2.n_in = f32[312,128]{1,0:T(8,128)S(1)} collective-permute-done((f32[312,128]{1,0:T(8,128)S(1)}, f32[312,128]{1,0:T(8,128)S(1)}, u32[]{:S(2)}, u32[]{:S(2)}) %collective-permute-start.2) | collective-permute-done | bytes 159776 | tf_op jit(solution)/shard_map/ppermute | solution.py:977
  14.3 7.1 %collective-permute-start.3 = (f32[32,128]{1,0:T(8,128)S(1)}, f32[32,128]{1,0:T(8,128)S(1)}, u32[]{:S(2)}, u32[]{:S(2)}) collective-permute-start(f32[32,128]{1,0:T(8,128)S(1)} %slice.56), channel_id=1, source_target_pairs={{0,1},{1,0},{2,3},{3,2},{4,5},{5,4},{6,7},{7,6},{8,9},{9,8},{10,11... | collective-permute-start | bytes 49160 | tf_op jit(solution)/shard_map/ppermute | solution.py:977
  21.4 2.1 %first_sides.1 = (f32[2432,128]{1,0:T(8,128)S(1)}, f32[128,128]{1,0:T(8,128)S(1)}, s32[128,128]{1,0:T(8,128)S(1)}, f32[1216,128]{1,0:T(8,128)S(1)}, f32[288,128]{1,0:T(8,128)S(1)}) custom-call(f32[2432,128]{1,0:T(8,128)S(1)} %get-tuple-element.41.local, f32[304,128]{1,0:T(8,128)S(1)} %get-tuple-element.37.f_own.f_first, ...), custom_call_target="tpu_custom_call" | custom-call | flops 1048576 | bytes 4194304 | tf_op jit(solution)/shard_map/first_sides/pallas_call | solution.py:1051
  23.6 0.0 collective-permute-done.3.x_late
  23.6 1.3 %second_collision.1 = (f32[2432,128]{1,0:T(8,128)S(1)}, f32[320,128]{1,0:T(8,128)S(1)}) custom-call(f32[2432,128]{1,0:T(8,128)S(1)} %get-tuple-element.45.new, s32[128,128]{1,0:T(8,128)S(1)} %get-tuple-element.40.mask, f32[304,128]{1,0:T(8,128)S(1)} %get-tuple-element.37.f_own.f_first, f32[656,128]{1,0:T(8,128)S(1)} %collective-permute-done.1.x_in, ...), custom_call_target="tpu_custom_call" | custom-call | flops 1048576 | bytes 4194304 | tf_op jit(solution)/shard_map/second_collision/pallas_call | solution.py:1065
  24.9 0.1 collective-permute-start.4
  25.0 1.4 %collective-permute-done.4.x_in = f32[320,128]{1,0:T(8,128)S(1)} collective-permute-done((f32[320,128]{1,0:T(8,128)S(1)}, f32[320,128]{1,0:T(8,128)S(1)}, u32[]{:S(2)}, u32[]{:S(2)}) %collective-permute-start.4) | collective-permute-done | bytes 163872 | tf_op jit(solution)/shard_map/ppermute | solution.py:977
  26.4 0.1 collective-permute-start.5
  26.5 1.0 %second_local.1 = (f32[2432,128]{1,0:T(8,128)S(1)}, f32[304,128]{1,0:T(8,128)S(1)}) custom-call(f32[2432,128]{1,0:T(8,128)S(1)} %get-tuple-element.52.post, s32[128,128]{1,0:T(8,128)S(1)} %get-tuple-element.40.mask, f32[80,128]{1,0:T(8,128)S(1)} %get-tuple-element.53.ez), custom_call_target="tpu_custom_call" | custom-call | flops 1048576 | bytes 4194304 | tf_op jit(solution)/shard_map/second_local/pallas_call | solution.py:1077
  27.5 0.1 collective-permute-start.7
  27.6 4.9 %collective-permute-done.5.n_in = f32[320,128]{1,0:T(8,128)S(1)} collective-permute-done((f32[320,128]{1,0:T(8,128)S(1)}, f32[320,128]{1,0:T(8,128)S(1)}, u32[]{:S(2)}, u32[]{:S(2)}) %collective-permute-start.5) | collective-permute-done | bytes 163872 | tf_op jit(solution)/shard_map/ppermute | solution.py:977
  32.5 4.3 %collective-permute-start.6 = (f32[32,128]{1,0:T(8,128)S(1)}, f32[32,128]{1,0:T(8,128)S(1)}, u32[]{:S(2)}, u32[]{:S(2)}) collective-permute-start(f32[32,128]{1,0:T(8,128)S(1)} %slice.58), channel_id=1, source_target_pairs={{0,1},{1,0},{2,3},{3,2},{4,5},{5,4},{6,7},{7,6},{8,9},{9,8},{10,11... | collective-permute-start | bytes 49160 | tf_op jit(solution)/shard_map/ppermute | solution.py:977
  36.8 0.9 %second_sides.1.new = f32[2432,128]{1,0:T(8,128)S(1)} custom-call(f32[2432,128]{1,0:T(8,128)S(1)} %get-tuple-element.55.local, f32[320,128]{1,0:T(8,128)S(1)} %get-tuple-element.51.f_own, f32[320,128]{1,0:T(8,128)S(1)} %collective-permute-done.4.x_in, f32[320,128]{1,0:T(8,128)S(1)} %collective-permute-done.5.n_in, f32[256,128]{1,0:T(8,128)S(1)} %get-tuple-element.43.e_halo, ...), custom_call_target="tpu_custom_call" | custom-call | flops 1048576 | bytes 4194304 | tf_op jit(solution)/shard_map/second_sides/pallas_call | solution.py:1087
  37.6 0.0 collective-permute-done.6.x_late
  37.6 1.0 %coarsen.1 = (f32[512,128]{1,0:T(8,128)S(1)}, f32[64,128]{1,0:T(8,128)S(1)}) custom-call(f32[2432,128]{1,0:T(8,128)S(1)} %second_sides.1.new, f32[320,128]{1,0:T(8,128)S(1)} %get-tuple-element.51.f_own, f32[320,128]{1,0:T(8,128)S(1)} %collective-permute-done.4.x_in, f32[320,128]{1,0:T(8,128)S(1)} %collective-permute-done.5.n_in, ...), custom_call_target="tpu_custom_call" | custom-call | flops 1048576 | bytes 4194304 | tf_op jit(solution)/shard_map/coarsen/pallas_call | solution.py:1094
  38.7 0.0 collective-permute-done.7.two
  38.7 1.5 %collective-permute-start.9 = (f32[608,128]{1,0:T(8,128)S(1)}, f32[608,128]{1,0:T(8,128)S(1)}, u32[]{:S(2)}, u32[]{:S(2)}) collective-permute-start(f32[608,128]{1,0:T(8,128)S(1)} %pad_maximum_fusion.1), channel_id=1, source_target_pairs={{0,1},{1,0},{2,3},{3,2},{4,5},{5,4},{6,7},{7,6},{8,9},{9,8},{10,11... | collective-permute-start | bytes 933896 | tf_op jit(solution)/shard_map/ppermute | solution.py:977
  40.2 0.0 collective-permute-start.8
  40.2 1.1 %tail.1 = (f32[2432,128]{1,0:T(8,128)}, f32[1216,128]{1,0:T(8,128)S(1)}) custom-call(f32[304,128]{1,0:T(8,128)S(1)} %get-tuple-element.37.f_own.f_first, f32[2432,128]{1,0:T(8,128)S(1)} %second_sides.1.new, f32[512,128]{1,0:T(8,128)S(1)} %get-tuple-element.57.cornered, f32[320,128]{1,0:T(8,128)S(1)} %get-tuple-element.51.f_own, ...), custom_call_target="tpu_custom_call" | custom-call | flops 1048576 | bytes 4194304 | tf_op jit(solution)/shard_map/tail/pallas_call | solution.py:1104
  41.3 1.7 %collective-permute-done.8.two_sides = f32[64,128]{1,0:T(8,128)S(1)} collective-permute-done((f32[64,128]{1,0:T(8,128)S(1)}, f32[64,128]{1,0:T(8,128)S(1)}, u32[]{:S(2)}, u32[]{:S(2)}) %collective-permute-start.8) | collective-permute-done | bytes 32800 | tf_op jit(solution)/shard_map/ppermute | solution.py:977
  43.0 0.0 collective-permute-done.9.x_in
  43.0 1.3 %collective-permute-start.10 = (f32[128,128]{1,0:T(8,128)S(1)}, f32[128,128]{1,0:T(8,128)S(1)}, u32[]{:S(2)}, u32[]{:S(2)}) collective-permute-start(f32[128,128]{1,0:T(8,128)S(1)} %pad_maximum_fusion.4), channel_id=1, source_target_pairs={{0,1},{1,0},{2,3},{3,2},{4,5},{5,4},{6,7},{7,6},{8,9},{9,8},{10,11... | collective-permute-start | bytes 196616 | tf_op jit(solution)/shard_map/ppermute | solution.py:977
  44.3 0.9 %collective-permute-done.10.x_sides = f32[128,128]{1,0:T(8,128)S(1)} collective-permute-done((f32[128,128]{1,0:T(8,128)S(1)}, f32[128,128]{1,0:T(8,128)S(1)}, u32[]{:S(2)}, u32[]{:S(2)}) %collective-permute-start.10) | collective-permute-done | bytes 65568 | tf_op jit(solution)/shard_map/ppermute | solution.py:977
  45.2 1.8 %coarse_last.1 = f32[1216,128]{1,0:T(8,128)} custom-call(f32[304,128]{1,0:T(8,128)S(1)} %get-tuple-element.37.f_own.f_first, f32[1216,128]{1,0:T(8,128)S(1)} %get-tuple-element.65.cpassed, f32[304,128]{1,0:T(8,128)S(1)} %get-tuple-element.60.own, f32[304,128]{1,0:T(8,128)S(1)} %collective-permute-done.7.two, f32[608,128]{1,0:T(8,128)S(1)} %collective-permute-done.9.x_in, ...), custom_call_target="tpu_custom_call" | custom-call | flops 1048576 | bytes 4194304 | tf_op jit(solution)/shard_map/coarse_last/pallas_call | solution.py:1117
  (13 shorter events, 0.1 us)
Async XLA Ops:
  2.1 4.8 %collective-permute-start = (f32[176,128]{1,0:T(8,128)S(1)}, f32[176,128]{1,0:T(8,128)S(1)}, u32[]{:S(2)}, u32[]{:S(2)}) collective-permute-start(f32[176,128]{1,0:T(8,128)S(1)} %get-tuple-element.38.e_own), channel_id=1, source_target_pairs={{0,2},{1,3},{2,0},{3,1},{4,6},{5,7},{6,4},{7,5},{8,10},{9,11},{10,... | collective-permute-start | bytes 270344 | tf_op jit(solution)/shard_map/ppermute | solution.py:977
  6.9 2.5 %collective-permute-start.1 = (f32[656,128]{1,0:T(8,128)S(1)}, f32[656,128]{1,0:T(8,128)S(1)}, u32[]{:S(2)}, u32[]{:S(2)}) collective-permute-start(f32[656,128]{1,0:T(8,128)S(1)} %pad_maximum_fusion), channel_id=1, source_target_pairs={{0,1},{1,0},{2,3},{3,2},{4,5},{5,4},{6,7},{7,6},{8,9},{9,8},{10,11... | collective-permute-start | bytes 1007624 | tf_op jit(solution)/shard_map/ppermute | solution.py:977
  9.5 4.8 %collective-permute-start.2 = (f32[312,128]{1,0:T(8,128)S(1)}, f32[312,128]{1,0:T(8,128)S(1)}, u32[]{:S(2)}, u32[]{:S(2)}) collective-permute-start(f32[312,128]{1,0:T(8,128)S(1)} %pad_maximum_fusion.3), channel_id=1, source_target_pairs={{0,127},{1,2},{2,1},{3,4},{4,3},{5,6},{6,5},{7,8},{8,7},{9,10},{10... | collective-permute-start | bytes 479240 | tf_op jit(solution)/shard_map/ppermute | solution.py:977
  14.3 9.3 %collective-permute-start.3 = (f32[32,128]{1,0:T(8,128)S(1)}, f32[32,128]{1,0:T(8,128)S(1)}, u32[]{:S(2)}, u32[]{:S(2)}) collective-permute-start(f32[32,128]{1,0:T(8,128)S(1)} %slice.56), channel_id=1, source_target_pairs={{0,1},{1,0},{2,3},{3,2},{4,5},{5,4},{6,7},{7,6},{8,9},{9,8},{10,11... | collective-permute-start | bytes 49160 | tf_op jit(solution)/shard_map/ppermute | solution.py:977
  24.9 1.5 %collective-permute-start.4 = (f32[320,128]{1,0:T(8,128)S(1)}, f32[320,128]{1,0:T(8,128)S(1)}, u32[]{:S(2)}, u32[]{:S(2)}) collective-permute-start(f32[320,128]{1,0:T(8,128)S(1)} %get-tuple-element.51.f_own), channel_id=1, source_target_pairs={{0,1},{1,0},{2,3},{3,2},{4,5},{5,4},{6,7},{7,6},{8,9},{9,8},{10,11... | collective-permute-start | bytes 491528 | tf_op jit(solution)/shard_map/ppermute | solution.py:977
  26.4 6.1 %collective-permute-start.5 = (f32[320,128]{1,0:T(8,128)S(1)}, f32[320,128]{1,0:T(8,128)S(1)}, u32[]{:S(2)}, u32[]{:S(2)}) collective-permute-start(f32[320,128]{1,0:T(8,128)S(1)} %pad_maximum_fusion.2), channel_id=1, source_target_pairs={{0,127},{1,2},{2,1},{3,4},{4,3},{5,6},{6,5},{7,8},{8,7},{9,10},{10... | collective-permute-start | bytes 491528 | tf_op jit(solution)/shard_map/ppermute | solution.py:977
  27.5 11.2 %collective-permute-start.7 = (f32[304,128]{1,0:T(8,128)S(1)}, f32[304,128]{1,0:T(8,128)S(1)}, u32[]{:S(2)}, u32[]{:S(2)}) collective-permute-start(f32[304,128]{1,0:T(8,128)S(1)} %get-tuple-element.60.own), channel_id=1, source_target_pairs={{0,2},{1,3},{2,0},{3,1},{4,6},{5,7},{6,4},{7,5},{8,10},{9,11},{10,... | collective-permute-start | bytes 466952 | tf_op jit(solution)/shard_map/ppermute | solution.py:977
  32.5 5.1 %collective-permute-start.6 = (f32[32,128]{1,0:T(8,128)S(1)}, f32[32,128]{1,0:T(8,128)S(1)}, u32[]{:S(2)}, u32[]{:S(2)}) collective-permute-start(f32[32,128]{1,0:T(8,128)S(1)} %slice.58), channel_id=1, source_target_pairs={{0,1},{1,0},{2,3},{3,2},{4,5},{5,4},{6,7},{7,6},{8,9},{9,8},{10,11... | collective-permute-start | bytes 49160 | tf_op jit(solution)/shard_map/ppermute | solution.py:977
  38.7 4.3 %collective-permute-start.9 = (f32[608,128]{1,0:T(8,128)S(1)}, f32[608,128]{1,0:T(8,128)S(1)}, u32[]{:S(2)}, u32[]{:S(2)}) collective-permute-start(f32[608,128]{1,0:T(8,128)S(1)} %pad_maximum_fusion.1), channel_id=1, source_target_pairs={{0,1},{1,0},{2,3},{3,2},{4,5},{5,4},{6,7},{7,6},{8,9},{9,8},{10,11... | collective-permute-start | bytes 933896 | tf_op jit(solution)/shard_map/ppermute | solution.py:977
  40.2 2.8 %collective-permute-start.8 = (f32[64,128]{1,0:T(8,128)S(1)}, f32[64,128]{1,0:T(8,128)S(1)}, u32[]{:S(2)}, u32[]{:S(2)}) collective-permute-start(f32[64,128]{1,0:T(8,128)S(1)} %get-tuple-element.62.own_sides), channel_id=1, source_target_pairs={{0,2},{1,3},{2,0},{3,1},{4,6},{5,7},{6,4},{7,5},{8,10},{9,11},{10,... | collective-permute-start | bytes 98312 | tf_op jit(solution)/shard_map/ppermute | solution.py:977
  43.0 2.2 %collective-permute-start.10 = (f32[128,128]{1,0:T(8,128)S(1)}, f32[128,128]{1,0:T(8,128)S(1)}, u32[]{:S(2)}, u32[]{:S(2)}) collective-permute-start(f32[128,128]{1,0:T(8,128)S(1)} %pad_maximum_fusion.4), channel_id=1, source_target_pairs={{0,1},{1,0},{2,3},{3,2},{4,5},{5,4},{6,7},{7,6},{8,9},{9,8},{10,11... | collective-permute-start | bytes 196616 | tf_op jit(solution)/shard_map/ppermute | solution.py:977

commit v7 on v6

--- a/solution.py
+++ b/solution.py
@@ -882,66 +882,73 @@
         c.wait()
 
 
-def coarse_last_kernel(
-    f_first,
-    cpassed,
-    own,
-    two,
-    x_in,
-    own_sides,
-    two_sides,
-    x_sides,
-    coarse_out,
-    gathered,
-    sides,
-    meta,
-    sem,
-):
+def merge_kernel(f_first, cpassed, own, two, x_in, merged, gathered, meta, sem):
     device, _ = place()
     (fetch,) = fetch_meta(((f_first, meta),), sem)
     put(gathered, 0, own[...])
     put(gathered, K_ROWS, x_in[0:K_ROWS, :])
     put(gathered, 2 * K_ROWS, two[...])
     put(gathered, 3 * K_ROWS, x_in[K_ROWS : 2 * K_ROWS, :])
-    put(sides, 0, own_sides[...])
-    put(sides, S_ROWS, x_sides[0:S_ROWS, :])
-    put(sides, 2 * S_ROWS, two_sides[...])
-    put(sides, 3 * S_ROWS, x_sides[S_ROWS : 2 * S_ROWS, :])
-    coarse_out[...] = cpassed[...]
+    merged[...] = cpassed[...]
+    _, lane = iotas(8)
+    x_half = (lane >> 3) & 1
+    fetch.wait()
+    for c in range(CB):
+        for qy in range(2):
+            children = [number(meta, c, M_CHILD + 2 * qy + qx) for qx in range(2)]
+            starts, shifts = [], []
+            for qx in range(2):
+                child = jnp.maximum(children[qx], 0)
+                slot = ((child >> 2) ^ device) & 3
+                starts.append(slot * K_ROWS + ((child & 3) >> 1) * (19 * 8))
+                shifts.append((8 * (qx - (child & 1))) & 127)
+            index = jnp.where(x_half == 0, children[0], children[1])
+            for i in range(19):
+                rows = pl.ds(i * CR + 2 * qy + c, 8, stride=4)
+                values = [
+                    roll(at(gathered, starts[qx] + 8 * i, 8), shifts[qx], 1) for qx in range(2)
+                ]
+                value = jnp.where(x_half == 0, values[0], values[1])
+                merged[rows, :] = jnp.where(index >= 0, value, cpassed[rows, :])
+
+
+def coarse_last_kernel(f_first, merged, own, two, x_in, coarse_out, sides, meta, sem):
+    device, _ = place()
+    (fetch,) = fetch_meta(((f_first, meta),), sem)
+    put(sides, 0, own[...])
+    put(sides, S_ROWS, x_in[0:S_ROWS, :])
+    put(sides, 2 * S_ROWS, two[...])
+    put(sides, 3 * S_ROWS, x_in[S_ROWS : 2 * S_ROWS, :])
+    coarse_out[...] = merged[...]
     _, lane = iotas(8)
     x = lane & 15
     x_half = (lane >> 3) & 1
     fetch.wait()
     for c in range(CB):
         for qy in range(2):
-            children = [number(meta, c, M_CHILD + 2 * qy + qx) for qx in range(2)]
-            found = []
+            changes = {i: [] for i in range(19)}
             for qx in range(2):
-                child = jnp.maximum(children[qx], 0)
+                index = number(meta, c, M_CHILD + 2 * qy + qx)
+                child = jnp.maximum(index, 0)
                 slot = ((child >> 2) ^ device) & 3
                 pair, h = (child & 3) >> 1, child & 1
-                start = slot * K_ROWS + pair * (19 * 8)
                 layers = [at(sides, slot * S_ROWS + pair * 32 + 8 * k, 8) for k in range(4)]
-                values = []
-                for i in range(19):
-                    value = roll(at(gathered, start + 8 * i, 8), (8 * (qx - h)) & 127, 1)
-                    for k, group in enumerate((XP, XM)):
-                        if i in group:
-                            to = 8 * qx + 7 * k
-                            shift = (to - 2 * group.index(i) - h) & 127
-                            value = jnp.where(x == to, roll(layers[k], shift, 1), value)
-                    for k, group in enumerate((YP, YM)):
-                        if i in group:
-                            shift = (112 * k + 8 * (qx - h) - 16 * group.index(i)) & 127
-                            edge = (lane >> 4) == 7 * k
-                            value = jnp.where(edge, roll(layers[2 + k], shift, 1), value)
-                    values.append(value)
-                found.append(values)
-            index = jnp.where(x_half == 0, children[0], children[1])
+                for k in range(2):
+                    to = 8 * qx + 7 * k
+                    here = (x == to) & (index >= 0)
+                    for n, i in enumerate((XP, XM)[k]):
+                        changes[i].append((here, roll(layers[k], (to - 2 * n - h) & 127, 1)))
+                    here = ((lane >> 4) == 7 * k) & (x_half == qx) & (index >= 0)
+                    for n, i in enumerate((YP, YM)[k]):
+                        shift = (112 * k + 8 * (qx - h) - 16 * n) & 127
+                        changes[i].append((here, roll(layers[2 + k], shift, 1)))
             for i in range(19):
-                rows = pl.ds(i * CR + 2 * qy + c, 8, stride=4)
-                value = jnp.where(x_half == 0, found[0][i], found[1][i])
-                coarse_out[rows, :] = jnp.where(index >= 0, value, cpassed[rows, :])
+                if changes[i]:
+                    rows = pl.ds(i * CR + 2 * qy + c, 8, stride=4)
+                    value = merged[rows, :]
+                    for here, change in changes[i]:
+                        value = jnp.where(here, change, value)
+                    coarse_out[rows, :] = value
 
 
 VMEM = pl.BlockSpec(memory_space=pltpu.VMEM)
@@ -1112,15 +1119,22 @@
         [HBM, VMEM],
     )(f_own, new2, cornered, f2_own, x2_in, n2_in, cmid)
     k_one = by_one(jnp.concatenate([means, k_two]))
-    sides_two, cpassed, k_one = lax.optimization_barrier((sides_two, cpassed, k_one))
+    (merged,) = call(
+        merge_kernel,
+        "merge",
+        [VMEM] * 5,
+        [rows_of(C_ALL)],
+        [scratch(4 * K_ROWS)] + meta_scratch(1),
+    )(f_own, cpassed, means, k_two, k_one)
+    sides_two, merged = lax.optimization_barrier((sides_two, merged))
     sides_one = by_one(jnp.concatenate([sides, sides_two]))
     (coarse_out,) = call(
         coarse_last_kernel,
         "coarse_last",
-        [VMEM] * 8,
+        [VMEM] * 5,
         [rows_of(C_ALL)],
-        [scratch(4 * K_ROWS), scratch(4 * S_ROWS)] + meta_scratch(1),
-    )(f_own, cpassed, means, k_two, k_one, sides, sides_two, sides_one)
+        [scratch(4 * S_ROWS)] + meta_scratch(1),
+    )(f_own, merged, sides, sides_two, sides_one)
     return as_cells(fine_out, FB), as_cells(coarse_out, CB)
 
 

time: 47.2 us -> 46.9 us (level)
  waiting for transfers between devices: 11.7 us -> 10.8 us
  Pallas kernels: 14.7 us -> 15.4 us
    ppermute x11, waiting for transfers between devices: 11.7 us -> 10.8 us  [exchange(): return lax.ppermute(rows, AXES, [(i, partner(i)) for i in range(devices)])]
    pallas_call x1 -> x2, Pallas kernels: 1.84 us -> 2.53 us  [the longest x1 1.68 us: on_device(): call(coarse_last_kernel, 'coarse_last', [VMEM] * 5, [rows_of(C_ALL)], [sc...]
  transfers between devices with their start and end apart: 11 -> 11, of which waited for: 6 -> 7; matrix products, arithmetic and copies ran while one was open for 0% -> 0% of each run, Pallas kernels for 22% -> 24%
where the time goes in v7:
time: 46.9 us; the launch traced here: 46.8 us
  starting transfers between devices  19.6 us (42%)
  Pallas kernels  15.4 us (33%)
  waiting for transfers between devices  10.8 us (23%)
  between operations  0.81 us (2%)
    ppermute x11, starting transfers between devices, exchange(): return lax.ppermute(rows, AXES, [(i, partner(i)) for i in range(devices)])  19.6 us
    ppermute x11, waiting for transfers between devices, exchange(): return lax.ppermute(rows, AXES, [(i, partner(i)) for i in range(devices)])  10.8 us
    pallas_call x1, Pallas kernels, on_device(): call(fine_first_kernel, 'fine_first', [VMEM, VMEM, HBM, HBM], [rows_of(C_...  2.61 us
    pallas_call x1, Pallas kernels, on_device(): call(first_sides_kernel, 'first_sides', [VMEM] * 8, [rows_of(F_ALL), rows...  2.14 us
    pallas_call x1, Pallas kernels, on_device(): call(coarse_last_kernel, 'coarse_last', [VMEM] * 5, [rows_of(C_ALL)], [sc...  1.68 us
    pallas_call x1, Pallas kernels, on_device(): call(first_local_kernel, 'first_local', [VMEM] * 6, [rows_of(2 * FR), row...  1.51 us
    pallas_call x1, Pallas kernels, on_device(): call(coarse_first_kernel, 'coarse_first', [HBM] * 5, [rows_of(C_ALL), row...  1.44 us
    pallas_call x1, Pallas kernels, on_device(): call(second_collision_kernel, 'second_collision', [VMEM] * 9, [rows_of(F_...  1.28 us
  transfers between devices with their start and end apart: 11, of which 7 were waited for; matrix products, arithmetic and copies ran while one was open for 0% of the time, Pallas kernels for 24%

profile of v7, /device:TPU:1, one launch (start us, length us, event | category | flops | bytes accessed | tf_op | source)
XLA Modules:
  0.0 46.8 jit_solution(12719219719953150715)
XLA Ops:
  0.6 1.4 %coarse_first.1 = (f32[1216,128]{1,0:T(8,128)S(1)}, f32[176,128]{1,0:T(8,128)S(1)}, f32[8,128]{1,0:T(8,128)S(1)}) custom-call(f32[1216,128]{1,0:T(8,128)} %bitcast.27, s32[4,4]{1,0:T(4,128)} %nbr_hbm.1, s32[2,4]{1,0:T(2,128)} %bitcast.30, s32[2,6]{1,0:T(2,128)} %cnbr_hbm.1, s32[2,4]{1,0:T(2,128)} %children_hbm.1), custom_call_target="tpu_custom_call" | custom-call | flops 1048576 | bytes 4194304 | tf_op jit(solution)/shard_map/coarse_first/pallas_call | solution.py:1006
  2.1 2.2 %collective-permute-start = (f32[176,128]{1,0:T(8,128)S(1)}, f32[176,128]{1,0:T(8,128)S(1)}, u32[]{:S(2)}, u32[]{:S(2)}) collective-permute-start(f32[176,128]{1,0:T(8,128)S(1)} %get-tuple-element.37.e_own), channel_id=1, source_target_pairs={{0,2},{1,3},{2,0},{3,1},{4,6},{5,7},{6,4},{7,5},{8,10},{9,11},{10,... | collective-permute-start | bytes 270344 | tf_op jit(solution)/shard_map/ppermute | solution.py:984
  4.3 2.6 %fine_first.1 = (f32[1216,128]{1,0:T(8,128)S(1)}, f32[2432,128]{1,0:T(8,128)S(1)}, s32[128,128]{1,0:T(8,128)S(1)}, f32[304,128]{1,0:T(8,128)S(1)}) custom-call(f32[8,128]{1,0:T(8,128)S(1)} %get-tuple-element.34.meta, f32[1216,128]{1,0:T(8,128)S(1)} %get-tuple-element.35.raw, f32[2432,128]{1,0:T(8,128)} %bitcast.26, s32[128,128]{1,0:T(8,128)} %bitcast.29), custom_call_target="tpu_custom_call" | custom-call | flops 1048576 | bytes 4194304 | tf_op jit(solution)/shard_map/fine_first/pallas_call | solution.py:1026
  6.9 0.0 collective-permute-done.e_two
  6.9 1.3 %collective-permute-start.1 = (f32[656,128]{1,0:T(8,128)S(1)}, f32[656,128]{1,0:T(8,128)S(1)}, u32[]{:S(2)}, u32[]{:S(2)}) collective-permute-start(f32[656,128]{1,0:T(8,128)S(1)} %pad_maximum_fusion), channel_id=1, source_target_pairs={{0,1},{1,0},{2,3},{3,2},{4,5},{5,4},{6,7},{7,6},{8,9},{9,8},{10,11... | collective-permute-start | bytes 1007624 | tf_op jit(solution)/shard_map/ppermute | solution.py:984
  8.2 1.3 %collective-permute-done.1.x_in = f32[656,128]{1,0:T(8,128)S(1)} collective-permute-done((f32[656,128]{1,0:T(8,128)S(1)}, f32[656,128]{1,0:T(8,128)S(1)}, u32[]{:S(2)}, u32[]{:S(2)}) %collective-permute-start.1) | collective-permute-done | bytes 335904 | tf_op jit(solution)/shard_map/ppermute | solution.py:984
  9.5 1.7 %collective-permute-start.2 = (f32[312,128]{1,0:T(8,128)S(1)}, f32[312,128]{1,0:T(8,128)S(1)}, u32[]{:S(2)}, u32[]{:S(2)}) collective-permute-start(f32[312,128]{1,0:T(8,128)S(1)} %pad_maximum_fusion.3), channel_id=1, source_target_pairs={{0,127},{1,2},{2,1},{3,4},{4,3},{5,6},{6,5},{7,8},{8,7},{9,10},{10... | collective-permute-start | bytes 479240 | tf_op jit(solution)/shard_map/ppermute | solution.py:984
  11.2 1.5 %first_local.1 = (f32[256,128]{1,0:T(8,128)S(1)}, f32[80,128]{1,0:T(8,128)S(1)}, f32[2432,128]{1,0:T(8,128)S(1)}, s32[64,128]{1,0:T(8,128)S(1)}) custom-call(f32[304,128]{1,0:T(8,128)S(1)} %get-tuple-element.36.f_own.f_first, f32[176,128]{1,0:T(8,128)S(1)} %get-tuple-element.37.e_own, f32[176,128]{1,0:T(8,128)S(1)} %collective-permute-done.e_two, ...), custom_call_target="tpu_custom_call" | custom-call | flops 1048576 | bytes 4194304 | tf_op jit(solution)/shard_map/first_local/pallas_call | solution.py:1049
  12.8 1.5 %collective-permute-done.2.n_in = f32[312,128]{1,0:T(8,128)S(1)} collective-permute-done((f32[312,128]{1,0:T(8,128)S(1)}, f32[312,128]{1,0:T(8,128)S(1)}, u32[]{:S(2)}, u32[]{:S(2)}) %collective-permute-start.2) | collective-permute-done | bytes 159776 | tf_op jit(solution)/shard_map/ppermute | solution.py:984
  14.3 7.1 %collective-permute-start.3 = (f32[32,128]{1,0:T(8,128)S(1)}, f32[32,128]{1,0:T(8,128)S(1)}, u32[]{:S(2)}, u32[]{:S(2)}) collective-permute-start(f32[32,128]{1,0:T(8,128)S(1)} %slice.56), channel_id=1, source_target_pairs={{0,1},{1,0},{2,3},{3,2},{4,5},{5,4},{6,7},{7,6},{8,9},{9,8},{10,11... | collective-permute-start | bytes 49160 | tf_op jit(solution)/shard_map/ppermute | solution.py:984
  21.4 2.1 %first_sides.1 = (f32[2432,128]{1,0:T(8,128)S(1)}, f32[128,128]{1,0:T(8,128)S(1)}, s32[128,128]{1,0:T(8,128)S(1)}, f32[1216,128]{1,0:T(8,128)S(1)}, f32[288,128]{1,0:T(8,128)S(1)}) custom-call(f32[2432,128]{1,0:T(8,128)S(1)} %get-tuple-element.40.local, f32[304,128]{1,0:T(8,128)S(1)} %get-tuple-element.36.f_own.f_first, ...), custom_call_target="tpu_custom_call" | custom-call | flops 1048576 | bytes 4194304 | tf_op jit(solution)/shard_map/first_sides/pallas_call | solution.py:1058
  23.6 0.0 collective-permute-done.3.x_late
  23.6 1.3 %second_collision.1 = (f32[2432,128]{1,0:T(8,128)S(1)}, f32[320,128]{1,0:T(8,128)S(1)}) custom-call(f32[2432,128]{1,0:T(8,128)S(1)} %get-tuple-element.44.new, s32[128,128]{1,0:T(8,128)S(1)} %get-tuple-element.39.mask, f32[304,128]{1,0:T(8,128)S(1)} %get-tuple-element.36.f_own.f_first, f32[656,128]{1,0:T(8,128)S(1)} %collective-permute-done.1.x_in, ...), custom_call_target="tpu_custom_call" | custom-call | flops 1048576 | bytes 4194304 | tf_op jit(solution)/shard_map/second_collision/pallas_call | solution.py:1072
  24.9 0.1 collective-permute-start.4
  25.0 1.4 %collective-permute-done.4.x_in = f32[320,128]{1,0:T(8,128)S(1)} collective-permute-done((f32[320,128]{1,0:T(8,128)S(1)}, f32[320,128]{1,0:T(8,128)S(1)}, u32[]{:S(2)}, u32[]{:S(2)}) %collective-permute-start.4) | collective-permute-done | bytes 163872 | tf_op jit(solution)/shard_map/ppermute | solution.py:984
  26.4 0.1 collective-permute-start.5
  26.5 1.0 %second_local.1 = (f32[2432,128]{1,0:T(8,128)S(1)}, f32[304,128]{1,0:T(8,128)S(1)}) custom-call(f32[2432,128]{1,0:T(8,128)S(1)} %get-tuple-element.51.post, s32[128,128]{1,0:T(8,128)S(1)} %get-tuple-element.39.mask, f32[80,128]{1,0:T(8,128)S(1)} %get-tuple-element.52.ez), custom_call_target="tpu_custom_call" | custom-call | flops 1048576 | bytes 4194304 | tf_op jit(solution)/shard_map/second_local/pallas_call | solution.py:1084
  27.5 0.1 collective-permute-start.7
  27.6 4.9 %collective-permute-done.5.n_in = f32[320,128]{1,0:T(8,128)S(1)} collective-permute-done((f32[320,128]{1,0:T(8,128)S(1)}, f32[320,128]{1,0:T(8,128)S(1)}, u32[]{:S(2)}, u32[]{:S(2)}) %collective-permute-start.5) | collective-permute-done | bytes 163872 | tf_op jit(solution)/shard_map/ppermute | solution.py:984
  32.5 4.3 %collective-permute-start.6 = (f32[32,128]{1,0:T(8,128)S(1)}, f32[32,128]{1,0:T(8,128)S(1)}, u32[]{:S(2)}, u32[]{:S(2)}) collective-permute-start(f32[32,128]{1,0:T(8,128)S(1)} %slice.58), channel_id=1, source_target_pairs={{0,1},{1,0},{2,3},{3,2},{4,5},{5,4},{6,7},{7,6},{8,9},{9,8},{10,11... | collective-permute-start | bytes 49160 | tf_op jit(solution)/shard_map/ppermute | solution.py:984
  36.8 0.9 %second_sides.1.new = f32[2432,128]{1,0:T(8,128)S(1)} custom-call(f32[2432,128]{1,0:T(8,128)S(1)} %get-tuple-element.54.local, f32[320,128]{1,0:T(8,128)S(1)} %get-tuple-element.50.f_own, f32[320,128]{1,0:T(8,128)S(1)} %collective-permute-done.4.x_in, f32[320,128]{1,0:T(8,128)S(1)} %collective-permute-done.5.n_in, f32[256,128]{1,0:T(8,128)S(1)} %get-tuple-element.42.e_halo, ...), custom_call_target="tpu_custom_call" | custom-call | flops 1048576 | bytes 4194304 | tf_op jit(solution)/shard_map/second_sides/pallas_call | solution.py:1094
  37.6 0.0 collective-permute-done.6.x_late
  37.6 1.0 %coarsen.1 = (f32[512,128]{1,0:T(8,128)S(1)}, f32[64,128]{1,0:T(8,128)S(1)}) custom-call(f32[2432,128]{1,0:T(8,128)S(1)} %second_sides.1.new, f32[320,128]{1,0:T(8,128)S(1)} %get-tuple-element.50.f_own, f32[320,128]{1,0:T(8,128)S(1)} %collective-permute-done.4.x_in, f32[320,128]{1,0:T(8,128)S(1)} %collective-permute-done.5.n_in, ...), custom_call_target="tpu_custom_call" | custom-call | flops 1048576 | bytes 4194304 | tf_op jit(solution)/shard_map/coarsen/pallas_call | solution.py:1101
  38.7 0.0 collective-permute-done.7.two
  38.7 1.5 %collective-permute-start.9 = (f32[608,128]{1,0:T(8,128)S(1)}, f32[608,128]{1,0:T(8,128)S(1)}, u32[]{:S(2)}, u32[]{:S(2)}) collective-permute-start(f32[608,128]{1,0:T(8,128)S(1)} %pad_maximum_fusion.1), channel_id=1, source_target_pairs={{0,1},{1,0},{2,3},{3,2},{4,5},{5,4},{6,7},{7,6},{8,9},{9,8},{10,11... | collective-permute-start | bytes 933896 | tf_op jit(solution)/shard_map/ppermute | solution.py:984
  40.2 1.1 %tail.1 = (f32[2432,128]{1,0:T(8,128)}, f32[1216,128]{1,0:T(8,128)S(1)}) custom-call(f32[304,128]{1,0:T(8,128)S(1)} %get-tuple-element.36.f_own.f_first, f32[2432,128]{1,0:T(8,128)S(1)} %second_sides.1.new, f32[512,128]{1,0:T(8,128)S(1)} %get-tuple-element.56.cornered, f32[320,128]{1,0:T(8,128)S(1)} %get-tuple-element.50.f_own, ...), custom_call_target="tpu_custom_call" | custom-call | flops 1048576 | bytes 4194304 | tf_op jit(solution)/shard_map/tail/pallas_call | solution.py:1111
  41.3 0.2 collective-permute-done.9.x_in
  41.4 0.8 %merge.1.merged = f32[1216,128]{1,0:T(8,128)S(1)} custom-call(f32[304,128]{1,0:T(8,128)S(1)} %get-tuple-element.36.f_own.f_first, f32[1216,128]{1,0:T(8,128)S(1)} %get-tuple-element.62.cpassed, f32[304,128]{1,0:T(8,128)S(1)} %get-tuple-element.59.own, f32[304,128]{1,0:T(8,128)S(1)} %collective-permute-done.7.two, f32[608,128]{1,0:T(8,128)S(1)} %collective-permute-done.9.x_in), custom_call_target="tpu_custom_call" | custom-call | flops 1048576 | bytes 4194304 | tf_op jit(solution)/shard_map/merge/pallas_call | solution.py:1122
  42.3 0.7 %collective-permute-done.8.two = f32[64,128]{1,0:T(8,128)S(1)} collective-permute-done((f32[64,128]{1,0:T(8,128)S(1)}, f32[64,128]{1,0:T(8,128)S(1)}, u32[]{:S(2)}, u32[]{:S(2)}) %collective-permute-start.8) | collective-permute-done | bytes 32800 | tf_op jit(solution)/shard_map/ppermute | solution.py:984
  43.0 1.2 %collective-permute-start.10 = (f32[128,128]{1,0:T(8,128)S(1)}, f32[128,128]{1,0:T(8,128)S(1)}, u32[]{:S(2)}, u32[]{:S(2)}) collective-permute-start(f32[128,128]{1,0:T(8,128)S(1)} %pad_maximum_fusion.4), channel_id=1, source_target_pairs={{0,1},{1,0},{2,3},{3,2},{4,5},{5,4},{6,7},{7,6},{8,9},{9,8},{10,11... | collective-permute-start | bytes 196616 | tf_op jit(solution)/shard_map/ppermute | solution.py:984
  44.2 0.9 %collective-permute-done.10.x_in = f32[128,128]{1,0:T(8,128)S(1)} collective-permute-done((f32[128,128]{1,0:T(8,128)S(1)}, f32[128,128]{1,0:T(8,128)S(1)}, u32[]{:S(2)}, u32[]{:S(2)}) %collective-permute-start.10) | collective-permute-done | bytes 65568 | tf_op jit(solution)/shard_map/ppermute | solution.py:984
  45.1 1.7 %coarse_last.1 = f32[1216,128]{1,0:T(8,128)} custom-call(f32[304,128]{1,0:T(8,128)S(1)} %get-tuple-element.36.f_own.f_first, f32[1216,128]{1,0:T(8,128)S(1)} %merge.1.merged, f32[64,128]{1,0:T(8,128)S(1)} %get-tuple-element.61.own, f32[64,128]{1,0:T(8,128)S(1)} %collective-permute-done.8.two, f32[128,128]{1,0:T(8,128)S(1)} %collective-permute-done.10.x_in), custom_call_target="tpu_custom_call" | custom-call | flops 1048576 | bytes 4194304 | tf_op jit(solution)/shard_map/coarse_last/pallas_call | solution.py:1131
  (14 shorter events, 0.1 us)
Async XLA Ops:
  2.1 4.8 %collective-permute-start = (f32[176,128]{1,0:T(8,128)S(1)}, f32[176,128]{1,0:T(8,128)S(1)}, u32[]{:S(2)}, u32[]{:S(2)}) collective-permute-start(f32[176,128]{1,0:T(8,128)S(1)} %get-tuple-element.37.e_own), channel_id=1, source_target_pairs={{0,2},{1,3},{2,0},{3,1},{4,6},{5,7},{6,4},{7,5},{8,10},{9,11},{10,... | collective-permute-start | bytes 270344 | tf_op jit(solution)/shard_map/ppermute | solution.py:984
  6.9 2.5 %collective-permute-start.1 = (f32[656,128]{1,0:T(8,128)S(1)}, f32[656,128]{1,0:T(8,128)S(1)}, u32[]{:S(2)}, u32[]{:S(2)}) collective-permute-start(f32[656,128]{1,0:T(8,128)S(1)} %pad_maximum_fusion), channel_id=1, source_target_pairs={{0,1},{1,0},{2,3},{3,2},{4,5},{5,4},{6,7},{7,6},{8,9},{9,8},{10,11... | collective-permute-start | bytes 1007624 | tf_op jit(solution)/shard_map/ppermute | solution.py:984
  9.5 4.8 %collective-permute-start.2 = (f32[312,128]{1,0:T(8,128)S(1)}, f32[312,128]{1,0:T(8,128)S(1)}, u32[]{:S(2)}, u32[]{:S(2)}) collective-permute-start(f32[312,128]{1,0:T(8,128)S(1)} %pad_maximum_fusion.3), channel_id=1, source_target_pairs={{0,127},{1,2},{2,1},{3,4},{4,3},{5,6},{6,5},{7,8},{8,7},{9,10},{10... | collective-permute-start | bytes 479240 | tf_op jit(solution)/shard_map/ppermute | solution.py:984
  14.3 9.3 %collective-permute-start.3 = (f32[32,128]{1,0:T(8,128)S(1)}, f32[32,128]{1,0:T(8,128)S(1)}, u32[]{:S(2)}, u32[]{:S(2)}) collective-permute-start(f32[32,128]{1,0:T(8,128)S(1)} %slice.56), channel_id=1, source_target_pairs={{0,1},{1,0},{2,3},{3,2},{4,5},{5,4},{6,7},{7,6},{8,9},{9,8},{10,11... | collective-permute-start | bytes 49160 | tf_op jit(solution)/shard_map/ppermute | solution.py:984
  24.9 1.5 %collective-permute-start.4 = (f32[320,128]{1,0:T(8,128)S(1)}, f32[320,128]{1,0:T(8,128)S(1)}, u32[]{:S(2)}, u32[]{:S(2)}) collective-permute-start(f32[320,128]{1,0:T(8,128)S(1)} %get-tuple-element.50.f_own), channel_id=1, source_target_pairs={{0,1},{1,0},{2,3},{3,2},{4,5},{5,4},{6,7},{7,6},{8,9},{9,8},{10,11... | collective-permute-start | bytes 491528 | tf_op jit(solution)/shard_map/ppermute | solution.py:984
  26.4 6.1 %collective-permute-start.5 = (f32[320,128]{1,0:T(8,128)S(1)}, f32[320,128]{1,0:T(8,128)S(1)}, u32[]{:S(2)}, u32[]{:S(2)}) collective-permute-start(f32[320,128]{1,0:T(8,128)S(1)} %pad_maximum_fusion.2), channel_id=1, source_target_pairs={{0,127},{1,2},{2,1},{3,4},{4,3},{5,6},{6,5},{7,8},{8,7},{9,10},{10... | collective-permute-start | bytes 491528 | tf_op jit(solution)/shard_map/ppermute | solution.py:984
  27.5 11.2 %collective-permute-start.7 = (f32[304,128]{1,0:T(8,128)S(1)}, f32[304,128]{1,0:T(8,128)S(1)}, u32[]{:S(2)}, u32[]{:S(2)}) collective-permute-start(f32[304,128]{1,0:T(8,128)S(1)} %get-tuple-element.59.own), channel_id=1, source_target_pairs={{0,2},{1,3},{2,0},{3,1},{4,6},{5,7},{6,4},{7,5},{8,10},{9,11},{10,... | collective-permute-start | bytes 466952 | tf_op jit(solution)/shard_map/ppermute | solution.py:984
  32.5 5.1 %collective-permute-start.6 = (f32[32,128]{1,0:T(8,128)S(1)}, f32[32,128]{1,0:T(8,128)S(1)}, u32[]{:S(2)}, u32[]{:S(2)}) collective-permute-start(f32[32,128]{1,0:T(8,128)S(1)} %slice.58), channel_id=1, source_target_pairs={{0,1},{1,0},{2,3},{3,2},{4,5},{5,4},{6,7},{7,6},{8,9},{9,8},{10,11... | collective-permute-start | bytes 49160 | tf_op jit(solution)/shard_map/ppermute | solution.py:984
  38.7 2.7 %collective-permute-start.9 = (f32[608,128]{1,0:T(8,128)S(1)}, f32[608,128]{1,0:T(8,128)S(1)}, u32[]{:S(2)}, u32[]{:S(2)}) collective-permute-start(f32[608,128]{1,0:T(8,128)S(1)} %pad_maximum_fusion.1), channel_id=1, source_target_pairs={{0,1},{1,0},{2,3},{3,2},{4,5},{5,4},{6,7},{7,6},{8,9},{9,8},{10,11... | collective-permute-start | bytes 933896 | tf_op jit(solution)/shard_map/ppermute | solution.py:984
  40.2 2.8 %collective-permute-start.8 = (f32[64,128]{1,0:T(8,128)S(1)}, f32[64,128]{1,0:T(8,128)S(1)}, u32[]{:S(2)}, u32[]{:S(2)}) collective-permute-start(f32[64,128]{1,0:T(8,128)S(1)} %get-tuple-element.61.own), channel_id=1, source_target_pairs={{0,2},{1,3},{2,0},{3,1},{4,6},{5,7},{6,4},{7,5},{8,10},{9,11},{10,... | collective-permute-start | bytes 98312 | tf_op jit(solution)/shard_map/ppermute | solution.py:984
  43.0 2.1 %collective-permute-start.10 = (f32[128,128]{1,0:T(8,128)S(1)}, f32[128,128]{1,0:T(8,128)S(1)}, u32[]{:S(2)}, u32[]{:S(2)}) collective-permute-start(f32[128,128]{1,0:T(8,128)S(1)} %pad_maximum_fusion.4), channel_id=1, source_target_pairs={{0,1},{1,0},{2,3},{3,2},{4,5},{5,4},{6,7},{7,6},{8,9},{9,8},{10,11... | collective-permute-start | bytes 196616 | tf_op jit(solution)/shard_map/ppermute | solution.py:984
